TPU v7x, 512 devices: a whole 4x4x16 slice. The times are simulated.
512 devices in a mesh: pts: 512 (over z, y, x, core).
Axes of the slice: x: 4, y: 4, z: 16, core: 2. Of those that a mesh axis runs over, the one named last changes fastest.
Arguments:
- right_side: float32 [128, 524288], P(None, 'pts')
- coordinates: float32 [3, 524288], P(None, 'pts'), may hold values from -1 to 1
- tree_order: int32 [512, 1024], P('pts'), may hold values from 0 to 1023, each once within a row
- leaf_sizes: int32 [512, 2], P('pts'), may hold values from 1 to 640, 1024 in all within a row
- level_basis: bfloat16 [10, 32, 524288], P(None, None, 'pts'), may hold values from -6 to 6
- coupling: float32 [512, 10, 64, 64], P('pts'), as said below
Outputs:
- solution: float32 [128, 524288], P(None, 'pts')
- residual: float32 [128, 524288], P(None, 'pts')
Inputs may be any that keep to these rules, and one draw needn't show every extreme that they name: `tree_order`: each row is a permutation of 0 to 1023. `leaf_sizes`: each device's two leaf sizes sum to 1024; each leaf holds at least 384 points. `coupling`: at level 0 the first 32 rows of a device's factor belong to its first leaf and the rest to its second; at a level l of 1 or more all devices whose indices agree from bit l up hold one factor, its first 32 rows belonging to the node whose bit l - 1 is 0, and devices whose bit l - 1 is 1 hold it with the two halves of rows exchanged.
All inputs are finite; a program needn't handle non-finite values.
Results may differ from a plain program's by a relative error of at most 0.007.
Values sent between devices are 32-bit elements; how exact they have to be, the bound alone decides.
No kernel may reach another device: no remote copies, remote signals or barrier semaphores. Data moves between devices by JAX's collectives and lax.ppermute only.
A program may use at most 64 MiB of HBM per device.

v0:
```python
import jax
import jax.numpy as jnp
from jax import lax
from jax.sharding import PartitionSpec as P

ITERS = 2


SQRT_THREE = 1.7320508075688772
NOISE_VAR = 1.0


def partner(block, axis, stride):
    count = lax.axis_size(axis)
    route = []
    for low in range(count):
        high = low | 1 << stride
        if high != low and high < count:
            route += [(low, high), (high, low)]
    return lax.ppermute(block, axis, route)


def kernel_columns(points, boundary, col_start, column_width):
    row_count = points.shape[1]
    columns = lax.dynamic_slice_in_dim(points, col_start, column_width, 1)
    dist_sq = jnp.zeros((row_count, column_width), jnp.float32)
    for component in range(3):
        offset = points[component][:, None] - columns[component][None, :]
        dist_sq = dist_sq + offset * offset
    scaled = SQRT_THREE * jnp.sqrt(dist_sq)
    values = (1.0 + scaled) * jnp.exp(-scaled)
    row_ids = lax.iota(jnp.int32, row_count)
    col_ids = col_start + lax.iota(jnp.int32, column_width)
    same_leaf = (row_ids < boundary)[:, None] == (col_ids < boundary)[None, :]
    values = jnp.where(same_leaf, values, 0.0) + jnp.where(
        row_ids[:, None] == col_ids[None, :], NOISE_VAR, 0.0
    )
    return values.astype(jnp.bfloat16)


def level_partner(values, bit_pos):
    return partner(values, "pts", bit_pos)


def global_sum(values):
    return lax.psum(values, "pts")


def combine_levels(projected, dev_levels):
    own_sums = []
    sib_sums = []
    for level_idx in range(dev_levels):
        partial_sum = projected[level_idx]
        for bit_pos in range(level_idx):
            partial_sum = partial_sum + level_partner(partial_sum, bit_pos)
        own_sums.append(partial_sum)
        sib_sums.append(level_partner(partial_sum, level_idx))
    return (jnp.stack(own_sums), jnp.stack(sib_sums))


def on_device(right_side, coordinates, tree_order, leaf_sizes, level_basis, coupling):
    highest = lax.Precision.HIGHEST
    rank_dim = level_basis.shape[1]
    points_dev = level_basis.shape[2]
    dev_levels = level_basis.shape[0] - 1
    ordered = jnp.take(coordinates, tree_order[0], axis=1)
    boundary = leaf_sizes[0, 0]
    first_leaf = lax.iota(jnp.int32, points_dev) < boundary
    own_half = coupling[0, :, :rank_dim, :]
    sib_half = coupling[0, :, rank_dim:, :]
    self_block = jnp.einsum("lrc,lsc->lrs", own_half, own_half, precision=highest)
    cross_block = jnp.einsum("lrc,lsc->lrs", own_half, sib_half, precision=highest)
    second_block = jnp.einsum("rc,sc->rs", sib_half[0], sib_half[0], precision=highest)
    column_width = min(512, points_dev)
    col_starts = list(range(0, points_dev, column_width))
    kernel_tile = jnp.concatenate(
        [kernel_columns(ordered, boundary, col_start, column_width) for col_start in col_starts],
        axis=1,
    )
    iterations = ITERS
    solution = jnp.zeros_like(right_side)
    residual = right_side
    direction = right_side
    local_norm = jnp.sum(residual * residual, axis=1)
    norm_now = global_sum(local_norm)
    for iteration in range(iterations):
        apply_rounded = direction.astype(jnp.bfloat16)
        leaf_term = jnp.dot(apply_rounded, kernel_tile, preferred_element_type=jnp.float32)
        projected = jnp.einsum(
            "lrp,kp->lrk", level_basis[1:], apply_rounded, preferred_element_type=jnp.float32
        )
        blank_probe = jnp.zeros_like(apply_rounded)
        proj_first = jnp.einsum(
            "rp,kp->rk",
            level_basis[0],
            jnp.where(first_leaf[None, :], apply_rounded, blank_probe),
            preferred_element_type=jnp.float32,
        )
        proj_second = jnp.einsum(
            "rp,kp->rk",
            level_basis[0],
            jnp.where(first_leaf[None, :], blank_probe, apply_rounded),
            preferred_element_type=jnp.float32,
        )
        own_sums, sib_sums = combine_levels(projected, dev_levels)
        coefficients = (
            jnp.einsum("lrs,lsk->lrk", self_block[1:], own_sums, precision=highest)
            + jnp.einsum("lrs,lsk->lrk", cross_block[1:], sib_sums, precision=highest)
        ).astype(jnp.bfloat16)
        coef_first = (
            jnp.dot(self_block[0], proj_first, precision=highest)
            + jnp.dot(cross_block[0], proj_second, precision=highest)
        ).astype(jnp.bfloat16)
        coef_second = (
            jnp.dot(second_block, proj_second, precision=highest)
            + jnp.dot(cross_block[0].T, proj_first, precision=highest)
        ).astype(jnp.bfloat16)
        expanded = jnp.einsum(
            "lrk,lrp->kp", coefficients, level_basis[1:], preferred_element_type=jnp.float32
        )
        local_first = jnp.einsum(
            "rk,rp->kp", coef_first, level_basis[0], preferred_element_type=jnp.float32
        )
        local_second = jnp.einsum(
            "rk,rp->kp", coef_second, level_basis[0], preferred_element_type=jnp.float32
        )
        local_term = jnp.where(first_leaf[None, :], local_first, local_second)
        kernel_image = leaf_term + expanded + local_term
        local_curv = jnp.sum(direction * kernel_image, axis=1)
        curvature = global_sum(local_curv)
        step_size = norm_now / curvature
        solution = solution + step_size[:, None] * direction
        residual = residual - step_size[:, None] * kernel_image
        if iteration + 1 < iterations:
            norm_next = global_sum(jnp.sum(residual * residual, axis=1))
            direction = residual + (norm_next / norm_now)[:, None] * direction
            norm_now = norm_next
    return (solution, residual)


def solution(mesh):
    in_specs = (
        P(None, "pts"),
        P(None, "pts"),
        P("pts", None),
        P("pts", None),
        P(None, None, "pts"),
        P("pts", None, None, None),
    )
    out_specs = (P(None, "pts"), P(None, "pts"))
    return jax.shard_map(
        on_device, mesh=mesh, in_specs=in_specs, out_specs=out_specs, check_vma=False
    )
```

profile of v0, /device:TPU:1, one launch (start us, length us, event | category | flops | bytes accessed | tf_op | source)
XLA Modules:
  0.0 637.4 jit_solution(17833473014307980975)
XLA Ops:
  2.4 8.8 %collective-permute-start = (f32[32,128]{1,0:T(8,128)S(1)}, f32[32,128]{1,0:T(8,128)S(1)}, u32[]{:S(2)}, u32[]{:S(2)}) collective-permute-start(f32[32,128]{1,0:T(8,128)S(1)} %get-tuple-element.83), channel_id=1, source_target_pairs={{0,1},{1,0},{2,3},{3,2},{4,5},{5,4},{6,7},{7,6},{8,9},{9,8},{10,11... | collective-permute-start | bytes 49160 | tf_op jit(solution)/shard_map/ppermute | solution.py:20
  13.2 2.8 gather_fusion
  18.3 4.2 add_convert_fusion.1
  24.7 2.4 collective-permute-start.21
  29.2 2.4 collective-permute-start.10
  33.6 2.4 collective-permute-start.3
  40.0 2.4 collective-permute-start.36
  42.5 3.6 collective-permute-start.29
  48.1 3.4 collective-permute-start.16
  53.4 3.4 collective-permute-start.2
  58.8 3.4 collective-permute-start.7
  64.1 4.9 collective-permute-start.5
  70.9 4.9 collective-permute-start.17
  77.8 4.9 collective-permute-start.8
  86.6 3.4 collective-permute-start.24
  92.0 3.4 collective-permute-start.13
  97.3 3.4 collective-permute-start.39
  102.9 4.6 collective-permute-start.25
  109.8 4.6 collective-permute-start.14
  116.6 3.5 collective-permute-start.33
  122.2 3.4 collective-permute-start.20
  127.5 4.9 collective-permute-start.34
  134.4 4.3 collective-permute-start.42
  138.7 8.8 %collective-permute-start.35 = (f32[32,128]{1,0:T(8,128)S(1)}, f32[32,128]{1,0:T(8,128)S(1)}, u32[]{:S(2)}, u32[]{:S(2)}) collective-permute-start(f32[32,128]{1,0:T(8,128)S(1)} %add.368), channel_id=1, source_target_pairs={{0,128},{128,0},{1,129},{129,1},{2,130},{130,2},{3,131},{131,3},{4... | collective-permute-start | bytes 49160 | tf_op jit(solution)/shard_map/ppermute | solution.py:20
  149.5 11.9 %collective-permute-start.44 = (f32[32,128]{1,0:T(8,128)S(1)}, f32[32,128]{1,0:T(8,128)S(1)}, u32[]{:S(2)}, u32[]{:S(2)}) collective-permute-start(f32[32,128]{1,0:T(8,128)S(1)} %get-tuple-element.34), channel_id=1, source_target_pairs={{0,256},{256,0},{1,257},{257,1},{2,258},{258,2},{3,259},{259,3},{4... | collective-permute-start | bytes 49160 | tf_op jit(solution)/shard_map/ppermute | solution.py:20
  165.4 112.6 %all-reduce = (f32[128]{0:T(128)S(1)}, f32[128]{0:T(128)S(1)}) all-reduce(f32[128]{0:T(128)S(1)} %multiply_reduce_fusion.3, f32[128]{0:T(128)S(1)} %get-tuple-element.87), channel_id=1, replica_groups=mesh['pts'=512] {'pts'}, use_global_device_ids=true, to_apply=%region_1.2 | all-reduce | flops 256 | bytes 2048 | tf_op jit(solution)/shard_map/psum | solution.py:46
  278.1 99.5 %psum.30 = f32[128]{0:T(128)S(1)} all-reduce(f32[128]{0:T(128)S(1)} %multiply_reduce_fusion.1), channel_id=1, replica_groups=mesh['pts'=512] {'pts'}, use_global_device_ids=true, to_apply=%region_5.6 | all-reduce | flops 128 | bytes 1024 | tf_op jit(solution)/shard_map/psum | solution.py:46
  378.8 2.6 collective-permute-start.45
  386.7 2.3 collective-permute-start.60
  397.9 2.7 collective-permute-start.82
  400.7 2.4 collective-permute-start.81
  403.1 2.6 collective-permute-start.74
  405.6 2.7 collective-permute-start.67
  408.4 2.6 collective-permute-start.61
  410.9 2.7 collective-permute-start.49
  413.7 2.6 collective-permute-start.47
  416.3 2.7 collective-permute-start.56
  419.0 2.6 collective-permute-start.52
  421.6 3.7 collective-permute-start.75
  425.3 3.1 collective-permute-start.50
  428.5 3.7 collective-permute-start.68
  432.2 3.1 collective-permute-start.62
  435.3 3.7 collective-permute-start.57
  439.0 3.1 collective-permute-start.53
  442.2 3.7 collective-permute-start.83
  445.9 2.4 collective-permute-start.76
  448.4 2.8 collective-permute-start.69
  451.2 2.4 collective-permute-start.63
  453.7 2.8 collective-permute-start.58
  456.6 2.4 collective-permute-start.54
  459.1 2.8 collective-permute-start.84
  461.9 2.5 collective-permute-start.77
  464.4 4.3 collective-permute-start.70
  468.8 2.5 collective-permute-start.64
  471.3 4.3 collective-permute-start.59
  475.6 2.5 collective-permute-start.85
  478.2 3.7 collective-permute-start.78
  483.8 3.4 collective-permute-start.65
  491.1 4.3 collective-permute-start.72
  497.4 5.5 collective-permute-start.80
  502.9 3.7 collective-permute-start.88
  506.7 8.2 %collective-permute-start.89 = (f32[32,128]{1,0:T(8,128)S(1)}, f32[32,128]{1,0:T(8,128)S(1)}, u32[]{:S(2)}, u32[]{:S(2)}) collective-permute-start(f32[32,128]{1,0:T(8,128)S(1)} %get-tuple-element.18), channel_id=1, source_target_pairs={{0,256},{256,0},{1,257},{257,1},{2,258},{258,2},{3,259},{259,3},{4... | collective-permute-start | bytes 49160 | tf_op jit(solution)/shard_map/ppermute | solution.py:20
  514.9 5.0 collective-permute-done.89
  522.8 112.4 %psum.31 = f32[128]{0:T(128)S(1)} all-reduce(f32[128]{0:T(128)S(1)} %get-tuple-element.89), channel_id=1, replica_groups=mesh['pts'=512] {'pts'}, use_global_device_ids=true, to_apply=%region_7.8 | all-reduce | flops 128 | bytes 1024 | tf_op jit(solution)/shard_map/psum | solution.py:46
  (271 shorter events, 82.2 us)
Async XLA Ops:
  2.4 20.3 %collective-permute-start = (f32[32,128]{1,0:T(8,128)S(1)}, f32[32,128]{1,0:T(8,128)S(1)}, u32[]{:S(2)}, u32[]{:S(2)}) collective-permute-start(f32[32,128]{1,0:T(8,128)S(1)} %get-tuple-element.83), channel_id=1, source_target_pairs={{0,1},{1,0},{2,3},{3,2},{4,5},{5,4},{6,7},{7,6},{8,9},{9,8},{10,11... | collective-permute-start | bytes 49160 | tf_op jit(solution)/shard_map/ppermute | solution.py:20
  38.1 15.3 %collective-permute-start.37 = (f32[32,128]{1,0:T(8,128)S(1)}, f32[32,128]{1,0:T(8,128)S(1)}, u32[]{:S(2)}, u32[]{:S(2)}) collective-permute-start(f32[32,128]{1,0:T(8,128)S(1)} %get-tuple-element.48), channel_id=1, source_target_pairs={{0,2},{2,0},{1,3},{3,1},{4,6},{6,4},{5,7},{7,5},{8,10},{10,8},{9,1... | collective-permute-start | bytes 49160 | tf_op jit(solution)/shard_map/ppermute | solution.py:20
  40.0 11.4 %collective-permute-start.36 = (f32[32,128]{1,0:T(8,128)S(1)}, f32[32,128]{1,0:T(8,128)S(1)}, u32[]{:S(2)}, u32[]{:S(2)}) collective-permute-start(f32[32,128]{1,0:T(8,128)S(1)} %get-tuple-element.82), channel_id=1, source_target_pairs={{0,1},{1,0},{2,3},{3,2},{4,5},{5,4},{6,7},{7,6},{8,9},{9,8},{10,11... | collective-permute-start | bytes 49160 | tf_op jit(solution)/shard_map/ppermute | solution.py:20
  42.5 14.3 %collective-permute-start.29 = (f32[32,128]{1,0:T(8,128)S(1)}, f32[32,128]{1,0:T(8,128)S(1)}, u32[]{:S(2)}, u32[]{:S(2)}) collective-permute-start(f32[32,128]{1,0:T(8,128)S(1)} %get-tuple-element.68), channel_id=1, source_target_pairs={{0,2},{2,0},{1,3},{3,1},{4,6},{6,4},{5,7},{7,5},{8,10},{10,8},{9,1... | collective-permute-start | bytes 49160 | tf_op jit(solution)/shard_map/ppermute | solution.py:20
  46.1 16.0 %collective-permute-start.22 = (f32[32,128]{1,0:T(8,128)S(1)}, f32[32,128]{1,0:T(8,128)S(1)}, u32[]{:S(2)}, u32[]{:S(2)}) collective-permute-start(f32[32,128]{1,0:T(8,128)S(1)} %get-tuple-element.69), channel_id=1, source_target_pairs={{0,2},{2,0},{1,3},{3,1},{4,6},{6,4},{5,7},{7,5},{8,10},{10,8},{9,1... | collective-permute-start | bytes 49160 | tf_op jit(solution)/shard_map/ppermute | solution.py:20
  48.1 20.9 %collective-permute-start.16 = (f32[32,128]{1,0:T(8,128)S(1)}, f32[32,128]{1,0:T(8,128)S(1)}, u32[]{:S(2)}, u32[]{:S(2)}) collective-permute-start(f32[32,128]{1,0:T(8,128)S(1)} %get-tuple-element.70), channel_id=1, source_target_pairs={{0,2},{2,0},{1,3},{3,1},{4,6},{6,4},{5,7},{7,5},{8,10},{10,8},{9,1... | collective-permute-start | bytes 49160 | tf_op jit(solution)/shard_map/ppermute | solution.py:20
  56.8 14.1 %collective-permute-start.11 = (f32[32,128]{1,0:T(8,128)S(1)}, f32[32,128]{1,0:T(8,128)S(1)}, u32[]{:S(2)}, u32[]{:S(2)}) collective-permute-start(f32[32,128]{1,0:T(8,128)S(1)} %get-tuple-element.71), channel_id=1, source_target_pairs={{0,2},{2,0},{1,3},{3,1},{4,6},{6,4},{5,7},{7,5},{8,10},{10,8},{9,1... | collective-permute-start | bytes 49160 | tf_op jit(solution)/shard_map/ppermute | solution.py:20
  58.8 17.1 %collective-permute-start.7 = (f32[32,128]{1,0:T(8,128)S(1)}, f32[32,128]{1,0:T(8,128)S(1)}, u32[]{:S(2)}, u32[]{:S(2)}) collective-permute-start(f32[32,128]{1,0:T(8,128)S(1)} %get-tuple-element.72), channel_id=1, source_target_pairs={{0,2},{2,0},{1,3},{3,1},{4,6},{6,4},{5,7},{7,5},{8,10},{10,8},{9,1... | collective-permute-start | bytes 49160 | tf_op jit(solution)/shard_map/ppermute | solution.py:20
  62.1 15.6 %collective-permute-start.30 = (f32[32,128]{1,0:T(8,128)S(1)}, f32[32,128]{1,0:T(8,128)S(1)}, u32[]{:S(2)}, u32[]{:S(2)}) collective-permute-start(f32[32,128]{1,0:T(8,128)S(1)} %add.363), channel_id=1, source_target_pairs={{0,4},{4,0},{1,5},{5,1},{2,6},{6,2},{3,7},{7,3},{8,12},{12,8},{9,1... | collective-permute-start | bytes 49160 | tf_op jit(solution)/shard_map/ppermute | solution.py:20
  64.1 18.6 %collective-permute-start.5 = (f32[32,128]{1,0:T(8,128)S(1)}, f32[32,128]{1,0:T(8,128)S(1)}, u32[]{:S(2)}, u32[]{:S(2)}) collective-permute-start(f32[32,128]{1,0:T(8,128)S(1)} %add.338), channel_id=1, source_target_pairs={{0,4},{4,0},{1,5},{5,1},{2,6},{6,2},{3,7},{7,3},{8,12},{12,8},{9,1... | collective-permute-start | bytes 49160 | tf_op jit(solution)/shard_map/ppermute | solution.py:20
  69.0 15.6 %collective-permute-start.23 = (f32[32,128]{1,0:T(8,128)S(1)}, f32[32,128]{1,0:T(8,128)S(1)}, u32[]{:S(2)}, u32[]{:S(2)}) collective-permute-start(f32[32,128]{1,0:T(8,128)S(1)} %add.356), channel_id=1, source_target_pairs={{0,4},{4,0},{1,5},{5,1},{2,6},{6,2},{3,7},{7,3},{8,12},{12,8},{9,1... | collective-permute-start | bytes 49160 | tf_op jit(solution)/shard_map/ppermute | solution.py:20
  70.9 15.6 %collective-permute-start.17 = (f32[32,128]{1,0:T(8,128)S(1)}, f32[32,128]{1,0:T(8,128)S(1)}, u32[]{:S(2)}, u32[]{:S(2)}) collective-permute-start(f32[32,128]{1,0:T(8,128)S(1)} %add.350), channel_id=1, source_target_pairs={{0,4},{4,0},{1,5},{5,1},{2,6},{6,2},{3,7},{7,3},{8,12},{12,8},{9,1... | collective-permute-start | bytes 49160 | tf_op jit(solution)/shard_map/ppermute | solution.py:20
  75.8 14.1 %collective-permute-start.12 = (f32[32,128]{1,0:T(8,128)S(1)}, f32[32,128]{1,0:T(8,128)S(1)}, u32[]{:S(2)}, u32[]{:S(2)}) collective-permute-start(f32[32,128]{1,0:T(8,128)S(1)} %add.345), channel_id=1, source_target_pairs={{0,4},{4,0},{1,5},{5,1},{2,6},{6,2},{3,7},{7,3},{8,12},{12,8},{9,1... | collective-permute-start | bytes 49160 | tf_op jit(solution)/shard_map/ppermute | solution.py:20
  77.8 14.1 %collective-permute-start.8 = (f32[32,128]{1,0:T(8,128)S(1)}, f32[32,128]{1,0:T(8,128)S(1)}, u32[]{:S(2)}, u32[]{:S(2)}) collective-permute-start(f32[32,128]{1,0:T(8,128)S(1)} %add.341), channel_id=1, source_target_pairs={{0,4},{4,0},{1,5},{5,1},{2,6},{6,2},{3,7},{7,3},{8,12},{12,8},{9,1... | collective-permute-start | bytes 49160 | tf_op jit(solution)/shard_map/ppermute | solution.py:20
  82.7 12.7 %collective-permute-start.38 = (f32[32,128]{1,0:T(8,128)S(1)}, f32[32,128]{1,0:T(8,128)S(1)}, u32[]{:S(2)}, u32[]{:S(2)}) collective-permute-start(f32[32,128]{1,0:T(8,128)S(1)} %get-tuple-element.46), channel_id=1, source_target_pairs={{0,4},{4,0},{1,5},{5,1},{2,6},{6,2},{3,7},{7,3},{8,12},{12,8},{9,1... | collective-permute-start | bytes 49160 | tf_op jit(solution)/shard_map/ppermute | solution.py:20
  84.7 12.6 %collective-permute-start.31 = (f32[32,128]{1,0:T(8,128)S(1)}, f32[32,128]{1,0:T(8,128)S(1)}, u32[]{:S(2)}, u32[]{:S(2)}) collective-permute-start(f32[32,128]{1,0:T(8,128)S(1)} %add.364), channel_id=1, source_target_pairs={{0,8},{8,0},{1,9},{9,1},{2,10},{10,2},{3,11},{11,3},{4,12},{12,4},... | collective-permute-start | bytes 49160 | tf_op jit(solution)/shard_map/ppermute | solution.py:20
  86.6 14.1 %collective-permute-start.24 = (f32[32,128]{1,0:T(8,128)S(1)}, f32[32,128]{1,0:T(8,128)S(1)}, u32[]{:S(2)}, u32[]{:S(2)}) collective-permute-start(f32[32,128]{1,0:T(8,128)S(1)} %add.357), channel_id=1, source_target_pairs={{0,8},{8,0},{1,9},{9,1},{2,10},{10,2},{3,11},{11,3},{4,12},{12,4},... | collective-permute-start | bytes 49160 | tf_op jit(solution)/shard_map/ppermute | solution.py:20
  90.0 12.9 %collective-permute-start.18 = (f32[32,128]{1,0:T(8,128)S(1)}, f32[32,128]{1,0:T(8,128)S(1)}, u32[]{:S(2)}, u32[]{:S(2)}) collective-permute-start(f32[32,128]{1,0:T(8,128)S(1)} %add.351), channel_id=1, source_target_pairs={{0,8},{8,0},{1,9},{9,1},{2,10},{10,2},{3,11},{11,3},{4,12},{12,4},... | collective-permute-start | bytes 49160 | tf_op jit(solution)/shard_map/ppermute | solution.py:20
  92.0 15.6 %collective-permute-start.13 = (f32[32,128]{1,0:T(8,128)S(1)}, f32[32,128]{1,0:T(8,128)S(1)}, u32[]{:S(2)}, u32[]{:S(2)}) collective-permute-start(f32[32,128]{1,0:T(8,128)S(1)} %add.346), channel_id=1, source_target_pairs={{0,8},{8,0},{1,9},{9,1},{2,10},{10,2},{3,11},{11,3},{4,12},{12,4},... | collective-permute-start | bytes 49160 | tf_op jit(solution)/shard_map/ppermute | solution.py:20
  95.3 14.4 %collective-permute-start.9 = (f32[32,128]{1,0:T(8,128)S(1)}, f32[32,128]{1,0:T(8,128)S(1)}, u32[]{:S(2)}, u32[]{:S(2)}) collective-permute-start(f32[32,128]{1,0:T(8,128)S(1)} %add.342), channel_id=1, source_target_pairs={{0,8},{8,0},{1,9},{9,1},{2,10},{10,2},{3,11},{11,3},{4,12},{12,4},... | collective-permute-start | bytes 49160 | tf_op jit(solution)/shard_map/ppermute | solution.py:20
  97.3 17.1 %collective-permute-start.39 = (f32[32,128]{1,0:T(8,128)S(1)}, f32[32,128]{1,0:T(8,128)S(1)}, u32[]{:S(2)}, u32[]{:S(2)}) collective-permute-start(f32[32,128]{1,0:T(8,128)S(1)} %get-tuple-element.44), channel_id=1, source_target_pairs={{0,8},{8,0},{1,9},{9,1},{2,10},{10,2},{3,11},{11,3},{4,12},{12,4},... | collective-permute-start | bytes 49160 | tf_op jit(solution)/shard_map/ppermute | solution.py:20
  100.7 15.9 %collective-permute-start.32 = (f32[32,128]{1,0:T(8,128)S(1)}, f32[32,128]{1,0:T(8,128)S(1)}, u32[]{:S(2)}, u32[]{:S(2)}) collective-permute-start(f32[32,128]{1,0:T(8,128)S(1)} %add.365), channel_id=1, source_target_pairs={{0,16},{16,0},{1,17},{17,1},{2,18},{18,2},{3,19},{19,3},{4,20},{20... | collective-permute-start | bytes 49160 | tf_op jit(solution)/shard_map/ppermute | solution.py:20
  102.9 17.3 %collective-permute-start.25 = (f32[32,128]{1,0:T(8,128)S(1)}, f32[32,128]{1,0:T(8,128)S(1)}, u32[]{:S(2)}, u32[]{:S(2)}) collective-permute-start(f32[32,128]{1,0:T(8,128)S(1)} %add.358), channel_id=1, source_target_pairs={{0,16},{16,0},{1,17},{17,1},{2,18},{18,2},{3,19},{19,3},{4,20},{20... | collective-permute-start | bytes 49160 | tf_op jit(solution)/shard_map/ppermute | solution.py:20
  107.5 14.6 %collective-permute-start.19 = (f32[32,128]{1,0:T(8,128)S(1)}, f32[32,128]{1,0:T(8,128)S(1)}, u32[]{:S(2)}, u32[]{:S(2)}) collective-permute-start(f32[32,128]{1,0:T(8,128)S(1)} %add.352), channel_id=1, source_target_pairs={{0,16},{16,0},{1,17},{17,1},{2,18},{18,2},{3,19},{19,3},{4,20},{20... | collective-permute-start | bytes 49160 | tf_op jit(solution)/shard_map/ppermute | solution.py:20
  109.8 15.8 %collective-permute-start.14 = (f32[32,128]{1,0:T(8,128)S(1)}, f32[32,128]{1,0:T(8,128)S(1)}, u32[]{:S(2)}, u32[]{:S(2)}) collective-permute-start(f32[32,128]{1,0:T(8,128)S(1)} %add.347), channel_id=1, source_target_pairs={{0,16},{16,0},{1,17},{17,1},{2,18},{18,2},{3,19},{19,3},{4,20},{20... | collective-permute-start | bytes 49160 | tf_op jit(solution)/shard_map/ppermute | solution.py:20
  114.4 13.1 %collective-permute-start.40 = (f32[32,128]{1,0:T(8,128)S(1)}, f32[32,128]{1,0:T(8,128)S(1)}, u32[]{:S(2)}, u32[]{:S(2)}) collective-permute-start(f32[32,128]{1,0:T(8,128)S(1)} %get-tuple-element.42), channel_id=1, source_target_pairs={{0,16},{16,0},{1,17},{17,1},{2,18},{18,2},{3,19},{19,3},{4,20},{20... | collective-permute-start | bytes 49160 | tf_op jit(solution)/shard_map/ppermute | solution.py:20
  120.2 12.2 %collective-permute-start.26 = (f32[32,128]{1,0:T(8,128)S(1)}, f32[32,128]{1,0:T(8,128)S(1)}, u32[]{:S(2)}, u32[]{:S(2)}) collective-permute-start(f32[32,128]{1,0:T(8,128)S(1)} %add.359), channel_id=1, source_target_pairs={{0,32},{32,0},{1,33},{33,1},{2,34},{34,2},{3,35},{35,3},{4,36},{36... | collective-permute-start | bytes 49160 | tf_op jit(solution)/shard_map/ppermute | solution.py:20
  122.2 12.2 %collective-permute-start.20 = (f32[32,128]{1,0:T(8,128)S(1)}, f32[32,128]{1,0:T(8,128)S(1)}, u32[]{:S(2)}, u32[]{:S(2)}) collective-permute-start(f32[32,128]{1,0:T(8,128)S(1)} %add.353), channel_id=1, source_target_pairs={{0,32},{32,0},{1,33},{33,1},{2,34},{34,2},{3,35},{35,3},{4,36},{36... | collective-permute-start | bytes 49160 | tf_op jit(solution)/shard_map/ppermute | solution.py:20
  125.5 13.1 %collective-permute-start.41 = (f32[32,128]{1,0:T(8,128)S(1)}, f32[32,128]{1,0:T(8,128)S(1)}, u32[]{:S(2)}, u32[]{:S(2)}) collective-permute-start(f32[32,128]{1,0:T(8,128)S(1)} %get-tuple-element.40), channel_id=1, source_target_pairs={{0,32},{32,0},{1,33},{33,1},{2,34},{34,2},{3,35},{35,3},{4,36},{36... | collective-permute-start | bytes 49160 | tf_op jit(solution)/shard_map/ppermute | solution.py:20
  132.5 15.1 %collective-permute-start.27 = (f32[32,128]{1,0:T(8,128)S(1)}, f32[32,128]{1,0:T(8,128)S(1)}, u32[]{:S(2)}, u32[]{:S(2)}) collective-permute-start(f32[32,128]{1,0:T(8,128)S(1)} %add.360), channel_id=1, source_target_pairs={{0,64},{64,0},{1,65},{65,1},{2,66},{66,2},{3,67},{67,3},{4,68},{68... | collective-permute-start | bytes 49160 | tf_op jit(solution)/shard_map/ppermute | solution.py:20
  134.4 15.1 %collective-permute-start.42 = (f32[32,128]{1,0:T(8,128)S(1)}, f32[32,128]{1,0:T(8,128)S(1)}, u32[]{:S(2)}, u32[]{:S(2)}) collective-permute-start(f32[32,128]{1,0:T(8,128)S(1)} %get-tuple-element.38), channel_id=1, source_target_pairs={{0,64},{64,0},{1,65},{65,1},{2,66},{66,2},{3,67},{67,3},{4,68},{68... | collective-permute-start | bytes 49160 | tf_op jit(solution)/shard_map/ppermute | solution.py:20
  147.6 13.9 %collective-permute-start.43 = (f32[32,128]{1,0:T(8,128)S(1)}, f32[32,128]{1,0:T(8,128)S(1)}, u32[]{:S(2)}, u32[]{:S(2)}) collective-permute-start(f32[32,128]{1,0:T(8,128)S(1)} %get-tuple-element.36), channel_id=1, source_target_pairs={{0,128},{128,0},{1,129},{129,1},{2,130},{130,2},{3,131},{131,3},{4... | collective-permute-start | bytes 49160 | tf_op jit(solution)/shard_map/ppermute | solution.py:20
  149.5 13.2 %collective-permute-start.44 = (f32[32,128]{1,0:T(8,128)S(1)}, f32[32,128]{1,0:T(8,128)S(1)}, u32[]{:S(2)}, u32[]{:S(2)}) collective-permute-start(f32[32,128]{1,0:T(8,128)S(1)} %get-tuple-element.34), channel_id=1, source_target_pairs={{0,256},{256,0},{1,257},{257,1},{2,258},{258,2},{3,259},{259,3},{4... | collective-permute-start | bytes 49160 | tf_op jit(solution)/shard_map/ppermute | solution.py:20
  389.0 11.7 %collective-permute-start.55 = (f32[32,128]{1,0:T(8,128)S(1)}, f32[32,128]{1,0:T(8,128)S(1)}, u32[]{:S(2)}, u32[]{:S(2)}) collective-permute-start(f32[32,128]{1,0:T(8,128)S(1)} %get-tuple-element.61), channel_id=1, source_target_pairs={{0,1},{1,0},{2,3},{3,2},{4,5},{5,4},{6,7},{7,6},{8,9},{9,8},{10,11... | collective-permute-start | bytes 49160 | tf_op jit(solution)/shard_map/ppermute | solution.py:20
  391.0 12.0 %collective-permute-start.51 = (f32[32,128]{1,0:T(8,128)S(1)}, f32[32,128]{1,0:T(8,128)S(1)}, u32[]{:S(2)}, u32[]{:S(2)}) collective-permute-start(f32[32,128]{1,0:T(8,128)S(1)} %get-tuple-element.62), channel_id=1, source_target_pairs={{0,1},{1,0},{2,3},{3,2},{4,5},{5,4},{6,7},{7,6},{8,9},{9,8},{10,11... | collective-permute-start | bytes 49160 | tf_op jit(solution)/shard_map/ppermute | solution.py:20
  397.9 15.8 %collective-permute-start.82 = (f32[32,128]{1,0:T(8,128)S(1)}, f32[32,128]{1,0:T(8,128)S(1)}, u32[]{:S(2)}, u32[]{:S(2)}) collective-permute-start(f32[32,128]{1,0:T(8,128)S(1)} %get-tuple-element.32), channel_id=1, source_target_pairs={{0,2},{2,0},{1,3},{3,1},{4,6},{6,4},{5,7},{7,5},{8,10},{10,8},{9,1... | collective-permute-start | bytes 49160 | tf_op jit(solution)/shard_map/ppermute | solution.py:20
  403.1 13.2 %collective-permute-start.74 = (f32[32,128]{1,0:T(8,128)S(1)}, f32[32,128]{1,0:T(8,128)S(1)}, u32[]{:S(2)}, u32[]{:S(2)}) collective-permute-start(f32[32,128]{1,0:T(8,128)S(1)} %get-tuple-element.51), channel_id=1, source_target_pairs={{0,2},{2,0},{1,3},{3,1},{4,6},{6,4},{5,7},{7,5},{8,10},{10,8},{9,1... | collective-permute-start | bytes 49160 | tf_op jit(solution)/shard_map/ppermute | solution.py:20
  405.6 16.0 %collective-permute-start.67 = (f32[32,128]{1,0:T(8,128)S(1)}, f32[32,128]{1,0:T(8,128)S(1)}, u32[]{:S(2)}, u32[]{:S(2)}) collective-permute-start(f32[32,128]{1,0:T(8,128)S(1)} %get-tuple-element.52), channel_id=1, source_target_pairs={{0,2},{2,0},{1,3},{3,1},{4,6},{6,4},{5,7},{7,5},{8,10},{10,8},{9,1... | collective-permute-start | bytes 49160 | tf_op jit(solution)/shard_map/ppermute | solution.py:20
  408.4 20.1 %collective-permute-start.61 = (f32[32,128]{1,0:T(8,128)S(1)}, f32[32,128]{1,0:T(8,128)S(1)}, u32[]{:S(2)}, u32[]{:S(2)}) collective-permute-start(f32[32,128]{1,0:T(8,128)S(1)} %get-tuple-element.53), channel_id=1, source_target_pairs={{0,2},{2,0},{1,3},{3,1},{4,6},{6,4},{5,7},{7,5},{8,10},{10,8},{9,1... | collective-permute-start | bytes 49160 | tf_op jit(solution)/shard_map/ppermute | solution.py:20
  413.7 11.6 %collective-permute-start.47 = (f32[32,128]{1,0:T(8,128)S(1)}, f32[32,128]{1,0:T(8,128)S(1)}, u32[]{:S(2)}, u32[]{:S(2)}) collective-permute-start(f32[32,128]{1,0:T(8,128)S(1)} %get-tuple-element.57), channel_id=1, source_target_pairs={{0,2},{2,0},{1,3},{3,1},{4,6},{6,4},{5,7},{7,5},{8,10},{10,8},{9,1... | collective-permute-start | bytes 49160 | tf_op jit(solution)/shard_map/ppermute | solution.py:20
  416.3 15.9 %collective-permute-start.56 = (f32[32,128]{1,0:T(8,128)S(1)}, f32[32,128]{1,0:T(8,128)S(1)}, u32[]{:S(2)}, u32[]{:S(2)}) collective-permute-start(f32[32,128]{1,0:T(8,128)S(1)} %get-tuple-element.54), channel_id=1, source_target_pairs={{0,2},{2,0},{1,3},{3,1},{4,6},{6,4},{5,7},{7,5},{8,10},{10,8},{9,1... | collective-permute-start | bytes 49160 | tf_op jit(solution)/shard_map/ppermute | solution.py:20
  419.0 16.3 %collective-permute-start.52 = (f32[32,128]{1,0:T(8,128)S(1)}, f32[32,128]{1,0:T(8,128)S(1)}, u32[]{:S(2)}, u32[]{:S(2)}) collective-permute-start(f32[32,128]{1,0:T(8,128)S(1)} %get-tuple-element.55), channel_id=1, source_target_pairs={{0,2},{2,0},{1,3},{3,1},{4,6},{6,4},{5,7},{7,5},{8,10},{10,8},{9,1... | collective-permute-start | bytes 49160 | tf_op jit(solution)/shard_map/ppermute | solution.py:20
  421.6 17.4 %collective-permute-start.75 = (f32[32,128]{1,0:T(8,128)S(1)}, f32[32,128]{1,0:T(8,128)S(1)}, u32[]{:S(2)}, u32[]{:S(2)}) collective-permute-start(f32[32,128]{1,0:T(8,128)S(1)} %add.405), channel_id=1, source_target_pairs={{0,4},{4,0},{1,5},{5,1},{2,6},{6,2},{3,7},{7,3},{8,12},{12,8},{9,1... | collective-permute-start | bytes 49160 | tf_op jit(solution)/shard_map/ppermute | solution.py:20
  425.3 16.8 %collective-permute-start.50 = (f32[32,128]{1,0:T(8,128)S(1)}, f32[32,128]{1,0:T(8,128)S(1)}, u32[]{:S(2)}, u32[]{:S(2)}) collective-permute-start(f32[32,128]{1,0:T(8,128)S(1)} %add.380), channel_id=1, source_target_pairs={{0,4},{4,0},{1,5},{5,1},{2,6},{6,2},{3,7},{7,3},{8,12},{12,8},{9,1... | collective-permute-start | bytes 49160 | tf_op jit(solution)/shard_map/ppermute | solution.py:20
  428.5 17.4 %collective-permute-start.68 = (f32[32,128]{1,0:T(8,128)S(1)}, f32[32,128]{1,0:T(8,128)S(1)}, u32[]{:S(2)}, u32[]{:S(2)}) collective-permute-start(f32[32,128]{1,0:T(8,128)S(1)} %add.398), channel_id=1, source_target_pairs={{0,4},{4,0},{1,5},{5,1},{2,6},{6,2},{3,7},{7,3},{8,12},{12,8},{9,1... | collective-permute-start | bytes 49160 | tf_op jit(solution)/shard_map/ppermute | solution.py:20
  432.2 16.2 %collective-permute-start.62 = (f32[32,128]{1,0:T(8,128)S(1)}, f32[32,128]{1,0:T(8,128)S(1)}, u32[]{:S(2)}, u32[]{:S(2)}) collective-permute-start(f32[32,128]{1,0:T(8,128)S(1)} %add.392), channel_id=1, source_target_pairs={{0,4},{4,0},{1,5},{5,1},{2,6},{6,2},{3,7},{7,3},{8,12},{12,8},{9,1... | collective-permute-start | bytes 49160 | tf_op jit(solution)/shard_map/ppermute | solution.py:20
  435.3 15.9 %collective-permute-start.57 = (f32[32,128]{1,0:T(8,128)S(1)}, f32[32,128]{1,0:T(8,128)S(1)}, u32[]{:S(2)}, u32[]{:S(2)}) collective-permute-start(f32[32,128]{1,0:T(8,128)S(1)} %add.387), channel_id=1, source_target_pairs={{0,4},{4,0},{1,5},{5,1},{2,6},{6,2},{3,7},{7,3},{8,12},{12,8},{9,1... | collective-permute-start | bytes 49160 | tf_op jit(solution)/shard_map/ppermute | solution.py:20
  439.0 14.7 %collective-permute-start.53 = (f32[32,128]{1,0:T(8,128)S(1)}, f32[32,128]{1,0:T(8,128)S(1)}, u32[]{:S(2)}, u32[]{:S(2)}) collective-permute-start(f32[32,128]{1,0:T(8,128)S(1)} %add.383), channel_id=1, source_target_pairs={{0,4},{4,0},{1,5},{5,1},{2,6},{6,2},{3,7},{7,3},{8,12},{12,8},{9,1... | collective-permute-start | bytes 49160 | tf_op jit(solution)/shard_map/ppermute | solution.py:20
  442.2 14.4 %collective-permute-start.83 = (f32[32,128]{1,0:T(8,128)S(1)}, f32[32,128]{1,0:T(8,128)S(1)}, u32[]{:S(2)}, u32[]{:S(2)}) collective-permute-start(f32[32,128]{1,0:T(8,128)S(1)} %get-tuple-element.30), channel_id=1, source_target_pairs={{0,4},{4,0},{1,5},{5,1},{2,6},{6,2},{3,7},{7,3},{8,12},{12,8},{9,1... | collective-permute-start | bytes 49160 | tf_op jit(solution)/shard_map/ppermute | solution.py:20
  445.9 13.2 %collective-permute-start.76 = (f32[32,128]{1,0:T(8,128)S(1)}, f32[32,128]{1,0:T(8,128)S(1)}, u32[]{:S(2)}, u32[]{:S(2)}) collective-permute-start(f32[32,128]{1,0:T(8,128)S(1)} %add.406), channel_id=1, source_target_pairs={{0,8},{8,0},{1,9},{9,1},{2,10},{10,2},{3,11},{11,3},{4,12},{12,4},... | collective-permute-start | bytes 49160 | tf_op jit(solution)/shard_map/ppermute | solution.py:20
  448.4 13.6 %collective-permute-start.69 = (f32[32,128]{1,0:T(8,128)S(1)}, f32[32,128]{1,0:T(8,128)S(1)}, u32[]{:S(2)}, u32[]{:S(2)}) collective-permute-start(f32[32,128]{1,0:T(8,128)S(1)} %add.399), channel_id=1, source_target_pairs={{0,8},{8,0},{1,9},{9,1},{2,10},{10,2},{3,11},{11,3},{4,12},{12,4},... | collective-permute-start | bytes 49160 | tf_op jit(solution)/shard_map/ppermute | solution.py:20
  451.2 13.2 %collective-permute-start.63 = (f32[32,128]{1,0:T(8,128)S(1)}, f32[32,128]{1,0:T(8,128)S(1)}, u32[]{:S(2)}, u32[]{:S(2)}) collective-permute-start(f32[32,128]{1,0:T(8,128)S(1)} %add.393), channel_id=1, source_target_pairs={{0,8},{8,0},{1,9},{9,1},{2,10},{10,2},{3,11},{11,3},{4,12},{12,4},... | collective-permute-start | bytes 49160 | tf_op jit(solution)/shard_map/ppermute | solution.py:20
  453.7 15.1 %collective-permute-start.58 = (f32[32,128]{1,0:T(8,128)S(1)}, f32[32,128]{1,0:T(8,128)S(1)}, u32[]{:S(2)}, u32[]{:S(2)}) collective-permute-start(f32[32,128]{1,0:T(8,128)S(1)} %add.388), channel_id=1, source_target_pairs={{0,8},{8,0},{1,9},{9,1},{2,10},{10,2},{3,11},{11,3},{4,12},{12,4},... | collective-permute-start | bytes 49160 | tf_op jit(solution)/shard_map/ppermute | solution.py:20
  456.6 14.7 %collective-permute-start.54 = (f32[32,128]{1,0:T(8,128)S(1)}, f32[32,128]{1,0:T(8,128)S(1)}, u32[]{:S(2)}, u32[]{:S(2)}) collective-permute-start(f32[32,128]{1,0:T(8,128)S(1)} %add.384), channel_id=1, source_target_pairs={{0,8},{8,0},{1,9},{9,1},{2,10},{10,2},{3,11},{11,3},{4,12},{12,4},... | collective-permute-start | bytes 49160 | tf_op jit(solution)/shard_map/ppermute | solution.py:20
  459.1 16.6 %collective-permute-start.84 = (f32[32,128]{1,0:T(8,128)S(1)}, f32[32,128]{1,0:T(8,128)S(1)}, u32[]{:S(2)}, u32[]{:S(2)}) collective-permute-start(f32[32,128]{1,0:T(8,128)S(1)} %get-tuple-element.28), channel_id=1, source_target_pairs={{0,8},{8,0},{1,9},{9,1},{2,10},{10,2},{3,11},{11,3},{4,12},{12,4},... | collective-permute-start | bytes 49160 | tf_op jit(solution)/shard_map/ppermute | solution.py:20
  461.9 16.2 %collective-permute-start.77 = (f32[32,128]{1,0:T(8,128)S(1)}, f32[32,128]{1,0:T(8,128)S(1)}, u32[]{:S(2)}, u32[]{:S(2)}) collective-permute-start(f32[32,128]{1,0:T(8,128)S(1)} %add.407), channel_id=1, source_target_pairs={{0,16},{16,0},{1,17},{17,1},{2,18},{18,2},{3,19},{19,3},{4,20},{20... | collective-permute-start | bytes 49160 | tf_op jit(solution)/shard_map/ppermute | solution.py:20
  464.4 17.4 %collective-permute-start.70 = (f32[32,128]{1,0:T(8,128)S(1)}, f32[32,128]{1,0:T(8,128)S(1)}, u32[]{:S(2)}, u32[]{:S(2)}) collective-permute-start(f32[32,128]{1,0:T(8,128)S(1)} %add.400), channel_id=1, source_target_pairs={{0,16},{16,0},{1,17},{17,1},{2,18},{18,2},{3,19},{19,3},{4,20},{20... | collective-permute-start | bytes 49160 | tf_op jit(solution)/shard_map/ppermute | solution.py:20
  468.8 15.0 %collective-permute-start.64 = (f32[32,128]{1,0:T(8,128)S(1)}, f32[32,128]{1,0:T(8,128)S(1)}, u32[]{:S(2)}, u32[]{:S(2)}) collective-permute-start(f32[32,128]{1,0:T(8,128)S(1)} %add.394), channel_id=1, source_target_pairs={{0,16},{16,0},{1,17},{17,1},{2,18},{18,2},{3,19},{19,3},{4,20},{20... | collective-permute-start | bytes 49160 | tf_op jit(solution)/shard_map/ppermute | solution.py:20
  471.3 15.9 %collective-permute-start.59 = (f32[32,128]{1,0:T(8,128)S(1)}, f32[32,128]{1,0:T(8,128)S(1)}, u32[]{:S(2)}, u32[]{:S(2)}) collective-permute-start(f32[32,128]{1,0:T(8,128)S(1)} %add.389), channel_id=1, source_target_pairs={{0,16},{16,0},{1,17},{17,1},{2,18},{18,2},{3,19},{19,3},{4,20},{20... | collective-permute-start | bytes 49160 | tf_op jit(solution)/shard_map/ppermute | solution.py:20
  475.6 13.5 %collective-permute-start.85 = (f32[32,128]{1,0:T(8,128)S(1)}, f32[32,128]{1,0:T(8,128)S(1)}, u32[]{:S(2)}, u32[]{:S(2)}) collective-permute-start(f32[32,128]{1,0:T(8,128)S(1)} %get-tuple-element.26), channel_id=1, source_target_pairs={{0,16},{16,0},{1,17},{17,1},{2,18},{18,2},{3,19},{19,3},{4,20},{20... | collective-permute-start | bytes 49160 | tf_op jit(solution)/shard_map/ppermute | solution.py:20
  483.8 11.6 %collective-permute-start.65 = (f32[32,128]{1,0:T(8,128)S(1)}, f32[32,128]{1,0:T(8,128)S(1)}, u32[]{:S(2)}, u32[]{:S(2)}) collective-permute-start(f32[32,128]{1,0:T(8,128)S(1)} %add.395), channel_id=1, source_target_pairs={{0,32},{32,0},{1,33},{33,1},{2,34},{34,2},{3,35},{35,3},{4,36},{36... | collective-permute-start | bytes 49160 | tf_op jit(solution)/shard_map/ppermute | solution.py:20
  491.1 11.7 %collective-permute-start.72 = (f32[32,128]{1,0:T(8,128)S(1)}, f32[32,128]{1,0:T(8,128)S(1)}, u32[]{:S(2)}, u32[]{:S(2)}) collective-permute-start(f32[32,128]{1,0:T(8,128)S(1)} %add.402), channel_id=1, source_target_pairs={{0,64},{64,0},{1,65},{65,1},{2,66},{66,2},{3,67},{67,3},{4,68},{68... | collective-permute-start | bytes 49160 | tf_op jit(solution)/shard_map/ppermute | solution.py:20
  502.9 12.0 %collective-permute-start.88 = (f32[32,128]{1,0:T(8,128)S(1)}, f32[32,128]{1,0:T(8,128)S(1)}, u32[]{:S(2)}, u32[]{:S(2)}) collective-permute-start(f32[32,128]{1,0:T(8,128)S(1)} %get-tuple-element.20), channel_id=1, source_target_pairs={{0,128},{128,0},{1,129},{129,1},{2,130},{130,2},{3,131},{131,3},{4... | collective-permute-start | bytes 49160 | tf_op jit(solution)/shard_map/ppermute | solution.py:20
  506.7 13.2 %collective-permute-start.89 = (f32[32,128]{1,0:T(8,128)S(1)}, f32[32,128]{1,0:T(8,128)S(1)}, u32[]{:S(2)}, u32[]{:S(2)}) collective-permute-start(f32[32,128]{1,0:T(8,128)S(1)} %get-tuple-element.18), channel_id=1, source_target_pairs={{0,256},{256,0},{1,257},{257,1},{2,258},{258,2},{3,259},{259,3},{4... | collective-permute-start | bytes 49160 | tf_op jit(solution)/shard_map/ppermute | solution.py:20
  (36 other events, 597.6 us)
where the time goes:
time: 640 us; the launch traced here: 637 us
  blocking collectives  324 us (51%)
  starting transfers between devices  279 us (44%)
  matrix products  9.52 us (1%)
  local copies, waits for them, and re-layouts  8.59 us (1%)
  waiting for transfers between devices  6.88 us (1%)
    psum x3, blocking collectives, global_sum(): return lax.psum(values, 'pts')  324 us
    ppermute x90, starting transfers between devices, partner(): return lax.ppermute(block, axis, route)  279 us
  transfers between devices with their start and end apart: 90, of which 3 were waited for; matrix products, arithmetic and copies ran while one was open for 2% of the time, Pallas kernels for 0%

commit v1 on v0

v1 whole, which is shorter than its diff:
```python
import functools

import jax
import jax.numpy as jnp
from jax import lax
from jax.experimental import pallas as pl
from jax.experimental.pallas import tpu as pltpu
from jax.sharding import PartitionSpec as P

f32 = jnp.float32
bf16 = jnp.bfloat16

SQRT_THREE = 1.7320508075688772
NOISE_VAR = 1.0

RANK = 32
PROBES = 128
POINTS = 1024
PLANE = 32
DEPTH = 16
ROWS = 24
Z_ROWS = 16
LEAST = 384
MOST = 640

NT = (((1,), (1,)), ((), ()))
TN = (((0,), (0,)), ((), ()))
NN = (((1,), (0,)), ((), ()))


def first_row(level):
    if level < 5:
        return 2 * (level - 1)
    return 16 if level == 5 else 8 + 2 * (level - 6)


def dot(a, b, dims):
    return lax.dot_general(a, b, dims, preferred_element_type=f32)


def halves(x):
    high = x.astype(bf16)
    return high, (x - high.astype(f32)).astype(bf16)


def dot_split(a, b, dims):
    a_high, a_low = halves(a)
    b_high, b_low = halves(b)
    a_dim, b_dim = dims[0][0][0], dims[0][1][0]
    return dot(
        jnp.concatenate([a_high, a_high, a_low], axis=a_dim),
        jnp.concatenate([b_high, b_low, b_high], axis=b_dim),
        dims,
    )


def rows_of(products):
    part = products[:, :PROBES]
    for start in range(PROBES, POINTS, PROBES):
        part = part + products[:, start : start + PROBES]
    return jnp.sum(part.T, axis=0, keepdims=True)


def down_rows(row):
    square = jnp.broadcast_to(row, (PROBES, PROBES)).T
    return jnp.concatenate([square] * (POINTS // PROBES), axis=1)


def row_ids(rows):
    return lax.broadcasted_iota(jnp.int32, (rows, PROBES), 0)


def send_levels(rounded, basis_ref, coupling_ref, send_ref):
    wide = basis_ref[1:10].reshape(9 * RANK, POINTS)
    projected = dot(wide, rounded, NT)
    for level in range(1, 10):
        own = coupling_ref[0, level, :RANK, :]
        partial = dot_split(own, projected[RANK * (level - 1) : RANK * level], TN)
        for half in range(2):
            send_ref[pl.ds(first_row(level) + half, PLANE, stride=ROWS), :] = partial[
                PLANE * half : PLANE * (half + 1)
            ]
    blank = jnp.zeros((PLANE, PROBES), f32)
    for row in range(18, ROWS):
        send_ref[pl.ds(row, PLANE, stride=ROWS), :] = blank


def start_kernel(right_ref, basis_ref, coupling_ref, send_ref):
    send_levels(right_ref[...].astype(bf16), basis_ref, coupling_ref, send_ref)


def leaf_level(v, rounded, boundary, tile, basis_ref, coupling_ref):
    leaf = dot(rounded, tile, NN)
    wide = basis_ref[0].astype(f32)
    in_first = lax.broadcasted_iota(jnp.int32, (RANK, POINTS), 1) < boundary
    both = jnp.concatenate(
        [jnp.where(in_first, wide, 0.0), jnp.where(in_first, 0.0, wide)], axis=0
    ).astype(bf16)
    factor = coupling_ref[0, 0]
    mixed = dot_split(factor, dot(both, rounded, NT), TN)
    coefficients = dot_split(factor, mixed, NN).astype(bf16)
    image = leaf + dot(coefficients, both, TN)
    curvature = rows_of(v * leaf) + jnp.sum(mixed * mixed, axis=0, keepdims=True)
    return image, curvature


def tile_kernel(
    coordinates_ref, order_ref, sizes_ref, right_ref, basis_ref, coupling_ref,
    tile_ref, image_ref, scalars_ref, pick_ref, column_ref,
):
    boundary = sizes_ref[0, 0]
    order = order_ref[...]
    step = 128

    @pl.loop(0, POINTS // step)
    def _(block):
        start = pl.multiple_of(block * step, step)
        ids = start + lax.broadcasted_iota(jnp.int32, (step, POINTS), 0)
        pick_ref[pl.ds(start, step), :] = jnp.where(ids == order, 1.0, 0.0).astype(bf16)

    whole = coordinates_ref[...]
    high = whole.astype(bf16).astype(f32)
    middle = (whole - high).astype(bf16).astype(f32)
    low = whole - high - middle
    terms = jnp.concatenate([high, middle, low], axis=0).astype(bf16)
    picked = dot(terms, pick_ref[...], NN)
    x = (picked[0:3] + picked[3:6]) + picked[6:9]
    column_ref[...] = jnp.concatenate([x, jnp.zeros((5, POINTS), f32)], axis=0).T

    def fill(row_start, row_stop, col_start, col_stop):
        group = 16
        width = col_stop - col_start
        across = [x[c : c + 1, col_start:col_stop] for c in range(3)]
        col_ids = col_start + lax.broadcasted_iota(jnp.int32, (group, width), 1)
        col_first = col_ids < boundary

        @pl.loop(0, (row_stop - row_start) // group)
        def _(block):
            start = pl.multiple_of(row_start + block * group, group)
            down = column_ref[pl.ds(start, group), :]
            dist_sq = jnp.zeros((group, width), f32)
            for c in range(3):
                offset = down[:, c : c + 1] - across[c]
                dist_sq = dist_sq + offset * offset
            scaled = SQRT_THREE * jnp.sqrt(dist_sq)
            values = (1.0 + scaled) * jnp.exp(-scaled)
            ids = start + lax.broadcasted_iota(jnp.int32, (group, width), 0)
            limit = jnp.where(ids < boundary, 0, boundary)
            low_end = jnp.where(ids < boundary, boundary, POINTS)
            same = (col_ids >= limit) & (col_ids < low_end)
            values = jnp.where(same, values, 0.0) + jnp.where(ids == col_ids, NOISE_VAR, 0.0)
            tile_ref[pl.ds(start, group), col_start:col_stop] = values.astype(bf16)

    tile_ref[:LEAST, MOST:] = jnp.zeros((LEAST, POINTS - MOST), bf16)
    tile_ref[MOST:, :LEAST] = jnp.zeros((POINTS - MOST, LEAST), bf16)
    fill(0, LEAST, 0, MOST)
    fill(LEAST, MOST, 0, POINTS)
    fill(MOST, POINTS, LEAST, POINTS)

    v = right_ref[...]
    image, curvature = leaf_level(
        v, v.astype(bf16), boundary, tile_ref[...], basis_ref, coupling_ref
    )
    image_ref[...] = image
    scalars_ref[...] = jnp.concatenate(
        [jnp.zeros((2, PROBES), f32), curvature, rows_of(v * v), jnp.zeros((4, PROBES), f32)],
        axis=0,
    )


def leaf_kernel(
    sizes_ref, residual_ref, first_image_ref, tile_ref, basis_ref, coupling_ref,
    image_ref, scalars_ref,
):
    v = residual_ref[...]
    image, curvature = leaf_level(
        v, v.astype(bf16), sizes_ref[0, 0], tile_ref[...], basis_ref, coupling_ref
    )
    image_ref[...] = image
    scalars_ref[...] = jnp.concatenate(
        [
            jnp.zeros((2, PROBES), f32),
            curvature,
            rows_of(v * v),
            rows_of(v * first_image_ref[...]),
            jnp.zeros((3, PROBES), f32),
        ],
        axis=0,
    )


def pair_sums(got_ref):
    sums = [[got_ref[ROWS * d : ROWS * d + 8, :] for d in range(PLANE)]]
    for _ in range(4):
        last = sums[-1]
        sums.append([last[2 * i] + last[2 * i + 1] for i in range(len(last) // 2)])
    return sums


def total(got_ref, count, rows, start):
    parts = [got_ref[rows * d + start : rows * d + start + 8, :] for d in range(count)]
    while len(parts) > 1:
        parts = [parts[2 * i] + parts[2 * i + 1] for i in range(len(parts) // 2)]
    return parts[0]


def squares(nodes):
    result = nodes[0] * nodes[0]
    for node in nodes[1:]:
        result = result + node * node
    return result


def plane_kernel(got_ref, scalars_ref, send_ref):
    ids = row_ids(8)
    sums = pair_sums(got_ref)
    square = jnp.zeros((8, PROBES), f32)
    for level in range(1, 5):
        square = jnp.where(ids // 2 == level - 1, squares(sums[level]), square)
    fifth = total(got_ref, PLANE, ROWS, 16)
    square = square + jnp.where(ids < 2, fifth * fifth, 0.0)
    curvature = jnp.sum(square, axis=0, keepdims=True)
    scalars = scalars_ref[...] + jnp.where(ids == 2, curvature, 0.0)
    upper = total(got_ref, PLANE, ROWS, 8)
    for z in range(DEPTH):
        send_ref[Z_ROWS * z : Z_ROWS * z + 8, :] = upper
        send_ref[Z_ROWS * z + 8 : Z_ROWS * (z + 1), :] = scalars


def depth_kernel(got_ref, z_got_ref, send_ref):
    own = lax.axis_index("pts") // PLANE
    ids = row_ids(8)
    reach = jnp.left_shift(2, ids // 2)
    pair = jnp.zeros((8, PROBES), f32)
    nodes = []
    for z in range(DEPTH):
        block = z_got_ref[Z_ROWS * z : Z_ROWS * z + 8, :]
        nodes.append(block)
        apart = jnp.bitwise_xor(own, z)
        pair = pair + jnp.where(apart < reach, block, 0.0)
    square = jnp.zeros((8, PROBES), f32)
    for level in range(4):
        nodes = [nodes[2 * i] + nodes[2 * i + 1] for i in range(len(nodes) // 2)]
        square = jnp.where(ids // 2 == level, squares(nodes), square)
    curvature = jnp.sum(square, axis=0, keepdims=True)
    scalars = total(z_got_ref, DEPTH, Z_ROWS, 8) + jnp.where(ids == 2, curvature, 0.0)
    fifth = total(got_ref, PLANE, ROWS, 16)
    last = jnp.where(ids < 2, fifth, scalars)
    sums = pair_sums(got_ref)
    for d in range(PLANE):
        first = sums[4][d >> 4]
        for level in (3, 2, 1):
            first = jnp.where(ids // 2 == level - 1, sums[level][d >> level], first)
        send_ref[ROWS * d : ROWS * d + 8, :] = first
        send_ref[ROWS * d + 8 : ROWS * d + 16, :] = pair
        send_ref[ROWS * d + 16 : ROWS * d + 24, :] = last


def expand(got_ref, basis_ref, coupling_ref):
    coefficients = []
    for level in range(1, 10):
        mixed = jnp.concatenate(
            [
                got_ref[pl.ds(first_row(level) + half, PLANE, stride=ROWS), :]
                for half in range(2)
            ],
            axis=0,
        )
        coefficients.append(dot_split(coupling_ref[0, level, :RANK, :], mixed, NN))
    narrow = jnp.concatenate(coefficients, axis=0).astype(bf16)
    return dot(narrow, basis_ref[1:10].reshape(9 * RANK, POINTS), TN)


def turn_kernel(
    got_ref, right_ref, image_ref, basis_ref, coupling_ref,
    residual_ref, whole_image_ref, send_ref, keep_ref,
):
    scalars = total(got_ref, PLANE, ROWS, 16)
    curvature, norm = scalars[2:3], scalars[3:4]
    step = norm / curvature
    whole = image_ref[...] + expand(got_ref, basis_ref, coupling_ref)
    residual = right_ref[...] - down_rows(step) * whole
    whole_image_ref[...] = whole
    residual_ref[...] = residual
    keep_ref[...] = jnp.concatenate(
        [step, curvature, norm, jnp.zeros((5, PROBES), f32)], axis=0
    )
    send_levels(residual.astype(bf16), basis_ref, coupling_ref, send_ref)


def end_kernel(
    got_ref, right_ref, residual_ref, first_image_ref, image_ref, basis_ref, coupling_ref,
    keep_ref, solution_ref, last_ref,
):
    scalars = total(got_ref, PLANE, ROWS, 16)
    own, norm, cross = scalars[2:3], scalars[3:4], scalars[4:5]
    step, curvature, norm_before = keep_ref[0:1, :], keep_ref[1:2, :], keep_ref[2:3, :]
    ratio = norm / norm_before
    step_now = norm / (own + 2.0 * ratio * cross + ratio * ratio * curvature)
    ratio_down, step_down = down_rows(ratio), down_rows(step_now)
    right, residual = right_ref[...], residual_ref[...]
    direction = residual + ratio_down * right
    solution_ref[...] = down_rows(step) * right + step_down * direction
    image = image_ref[...] + expand(got_ref, basis_ref, coupling_ref)
    last_ref[...] = residual - step_down * (image + ratio_down * first_image_ref[...])


VMEM = pl.BlockSpec(memory_space=pltpu.VMEM)
SMEM = pl.BlockSpec(memory_space=pltpu.SMEM)


def call(body, outs, ins, megabytes, cost, scratch=(), name=None):
    specs = [SMEM if a.dtype == jnp.int32 and a.shape == (1, 2) else VMEM for a in ins]
    return pl.pallas_call(
        body,
        out_shape=[jax.ShapeDtypeStruct(shape, kind) for shape, kind in outs],
        in_specs=specs,
        out_specs=[VMEM] * len(outs),
        scratch_shapes=list(scratch),
        compiler_params=pltpu.CompilerParams(vmem_limit_bytes=megabytes << 20),
        cost_estimate=pl.CostEstimate(flops=cost, bytes_accessed=2 << 20, transcendentals=0),
        name=name,
    )(*ins)


def plane_groups(count):
    return [list(range(PLANE * z, PLANE * (z + 1))) for z in range(count // PLANE)]


def depth_groups(count):
    return [list(range(place, count, PLANE)) for place in range(PLANE)]


def exchange(rows, groups):
    members = len(groups[0])
    blocks = rows.reshape(members, rows.shape[0] // members, PROBES)
    got = lax.all_to_all(blocks, "pts", 0, 0, axis_index_groups=groups)
    return got.reshape(rows.shape)


def on_device(right_side, coordinates, tree_order, leaf_sizes, level_basis, coupling):
    count = lax.axis_size("pts")
    planes, depths = plane_groups(count), depth_groups(count)
    field = ((PROBES, POINTS), f32)
    message = ((PLANE * ROWS, PROBES), f32)
    z_message = ((DEPTH * Z_ROWS, PROBES), f32)
    row_block = ((8, PROBES), f32)

    def tree(send, scalars_of):
        got = exchange(send, planes)
        local = scalars_of()
        (z_send,) = call(plane_kernel, [z_message], [got, local[-1]], 8, 1 << 20, name="plane")
        z_got = exchange(z_send, depths)
        (back,) = call(depth_kernel, [message], [got, z_got], 8, 1 << 20, name="depth")
        return local, exchange(back, planes)

    (send,) = call(
        start_kernel, [message], [right_side, level_basis, coupling], 16, 1 << 26, name="start"
    )
    (tile, image, _), got = tree(
        send,
        lambda: call(
            tile_kernel,
            [((POINTS, POINTS), bf16), field, row_block],
            [coordinates, tree_order, leaf_sizes, right_side, level_basis, coupling],
            24,
            4 << 30,
            scratch=[pltpu.VMEM((POINTS, POINTS), bf16), pltpu.VMEM((POINTS, 8), f32)],
            name="tile",
        ),
    )
    residual, first_image, send, keep = call(
        turn_kernel,
        [field, field, message, row_block],
        [got, right_side, image, level_basis, coupling],
        16,
        1 << 28,
        name="turn",
    )
    (image, _), got = tree(
        send,
        lambda: call(
            leaf_kernel,
            [field, row_block],
            [leaf_sizes, residual, first_image, tile, level_basis, coupling],
            24,
            1 << 30,
            name="leaf",
        ),
    )
    return tuple(
        call(
            end_kernel,
            [field, field],
            [got, right_side, residual, first_image, image, level_basis, coupling, keep],
            16,
            1 << 28,
            name="end",
        )
    )


def solution(mesh):
    in_specs = (
        P(None, "pts"),
        P(None, "pts"),
        P("pts", None),
        P("pts", None),
        P(None, None, "pts"),
        P("pts", None, None, None),
    )
    out_specs = (P(None, "pts"), P(None, "pts"))
    return jax.shard_map(
        on_device, mesh=mesh, in_specs=in_specs, out_specs=out_specs, check_vma=False
    )
```

time: 640 us -> 124 us (0.19)
  starting transfers between devices: 279 us -> 14.3 us
  blocking collectives: 324 us -> 77.8 us
  Pallas kernels: 0 us -> 16.4 us
  matrix products: 9.52 us -> 0 us
    psum x3 -> x0, blocking collectives: 324 us -> none  [global_sum(): return lax.psum(values, 'pts')]
    ppermute x90 -> x0, starting transfers between devices: 279 us -> none  [partner(): return lax.ppermute(block, axis, route)]
    all_to_all x0 -> x4, blocking collectives: none -> 77.8 us  [exchange(): got = lax.all_to_all(blocks, 'pts', 0, 0, axis_index_groups=groups)]
    pallas_call x0 -> x9, Pallas kernels: none -> 16.4 us  [call(): pl.pallas_call(body, out_shape=[jax.ShapeDtypeStruct(shape, kind) for sha...]
    all_to_all x0 -> x2, starting transfers between devices: none -> 14.3 us  [exchange(): got = lax.all_to_all(blocks, 'pts', 0, 0, axis_index_groups=groups)]
    dot_general x29 -> x0, matrix products: 9.52 us -> none  [the longest x2 1.74 us: on_device(): jnp.dot(apply_rounded, kernel_tile, preferred_element_type=jnp.float32)]
    all_to_all x0 -> x2, waiting for transfers between devices: none -> 6.99 us  [exchange(): got = lax.all_to_all(blocks, 'pts', 0, 0, axis_index_groups=groups)]
    ppermute x90 -> x0, waiting for transfers between devices: 6.88 us -> none  [partner(): return lax.ppermute(block, axis, route)]
  transfers between devices with their start and end apart: 90 -> 2, of which waited for: 3 -> 1; matrix products, arithmetic and copies ran while one was open for 2% -> 0% of each run, Pallas kernels for 0% -> 10%
where the time goes in v1:
time: 124 us; the launch traced here: 123 us
  blocking collectives  77.8 us (63%)
  Pallas kernels  16.4 us (13%)
  starting transfers between devices  14.3 us (12%)
  waiting for transfers between devices  6.99 us (6%)
  local copies, waits for them, and re-layouts  6.77 us (5%)
    all_to_all x4, blocking collectives, exchange(): got = lax.all_to_all(blocks, 'pts', 0, 0, axis_index_groups=groups)  77.8 us
    pallas_call x9, Pallas kernels, call(): pl.pallas_call(body, out_shape=[jax.ShapeDtypeStruct(shape, kind) for sha...  16.4 us
    all_to_all x2, starting transfers between devices, exchange(): got = lax.all_to_all(blocks, 'pts', 0, 0, axis_index_groups=groups)  14.3 us
    all_to_all x2, waiting for transfers between devices, exchange(): got = lax.all_to_all(blocks, 'pts', 0, 0, axis_index_groups=groups)  6.99 us
    unnamed x24, local copies, waits for them, and re-layouts  6.77 us
  transfers between devices with their start and end apart: 2, of which 1 were waited for; matrix products, arithmetic and copies ran while one was open for 0% of the time, Pallas kernels for 10%

profile of v1, /device:TPU:1, one launch (start us, length us, event | category | flops | bytes accessed | tf_op | source)
XLA Modules:
  0.0 123.1 jit_solution(11738089539331363214)
XLA Ops:
  0.6 0.0 copy-start
  0.6 1.1 copy-done
  1.7 0.0 copy-start.2
  1.7 1.0 copy-done.2
  2.7 0.0 copy-start.4
  2.7 1.0 copy-done.4
  3.7 0.0 copy-start.1
  3.7 0.0 copy-start.3
  3.7 0.0 copy-start.5
  3.7 0.0 copy-start.9
  3.7 0.0 copy-start.10
  3.8 0.0 copy-start.11
  3.8 1.3 %start.1 = f32[768,128]{1,0:T(8,128)} custom-call(f32[128,1024]{1,0:T(8,128)S(1)} %copy-done.4, bf16[10,32,1024]{2,1,0:T(8,128)(2,1)S(1)} %copy-done, f32[1,10,64,64]{3,2,1,0:T(8,128)S(1)} %copy-done.2), custom_call_target="tpu_custom_call" | custom-call | flops 67108864 | bytes 2097152 | tf_op jit(solution)/shard_map/start/pallas_call | solution.py:314
  5.0 10.4 %all-to-all-start = ((f32[32,24,128]{2,1,0:T(8,128)}), f32[32,24,128]{2,1,0:T(8,128)S(1)}, u32[]{:S(2)}, u32[]{:S(2)}) async-start(f32[32,24,128]{2,1,0:T(8,128)} %bitcast), calls=%async_computation | async-start | bytes 786432 | tf_op jit(solution)/shard_map/all_to_all | solution.py:337
  15.5 0.0 copy-done.1
  15.5 0.0 copy-done.3
  15.5 0.0 copy-done.5
  15.5 0.0 copy-done.9
  15.5 0.0 copy-done.10
  15.5 0.0 copy-done.11
  15.5 10.5 %tile.1 = (bf16[1024,1024]{1,0:T(8,128)(2,1)S(1)}, f32[128,1024]{1,0:T(8,128)S(1)}, f32[8,128]{1,0:T(8,128)S(1)}) custom-call(f32[3,1024]{1,0:T(4,128)S(1)} %copy-done.10, s32[1,1024]{1,0:T(1,128)S(1)} %copy-done.11, s32[1,2]{1,0:T(1,128)S(1)} %copy-done.9, f32[128,1024]{1,0:T(8,128)S(1)} %copy-done.5, bf16[10,32,1024]{2,1,0:T(8,128)(2,1)S(1)} %copy-done.1, ...), custom_call_target="tpu_custom_call" | custom-call | flops 4294967296 | bytes 2097152 | tf_op jit(solution)/shard_map/tile/pallas_call | solution.py:314
  26.1 0.0 copy-start.6
  26.1 1.3 %copy-done.6 = bf16[1024,1024]{1,0:T(8,128)(2,1)} copy-done((bf16[1024,1024]{1,0:T(8,128)(2,1)}, bf16[1024,1024]{1,0:T(8,128)(2,1)S(1)}, u32[]{:S(2)}) %copy-start.6) | copy-done | bytes 2097176
  27.4 0.0 all-to-all-done
  27.4 25.1 %all_to_all.30 = f32[16,16,128]{2,1,0:T(8,128)S(1)} all-to-all(f32[16,16,128]{2,1,0:T(8,128)S(1)} %bitcast.22), channel_id=1, replica_groups={{0,32,64,96,128,160,192,224,256,288,320,352,384,416,448,480},{1,33,65,9..., dimensions={0} | all-to-all | bytes 262144 | tf_op jit(solution)/shard_map/all_to_all | solution.py:337
  52.5 0.1 depth.2
  52.6 20.2 %all_to_all.31 = f32[32,24,128]{2,1,0:T(8,128)S(1)} all-to-all(f32[32,24,128]{2,1,0:T(8,128)S(1)} %bitcast.17), channel_id=1, replica_groups={{0,1,2,3,4,5,6,7,8,9,10,11,12,13,14,15,16,17,18,19,20,21,22,23,24,25,26..., dimensions={0} | all-to-all | bytes 786432 | tf_op jit(solution)/shard_map/all_to_all | solution.py:337
  72.8 1.1 turn.1
  73.9 0.0 copy-start.8
  73.9 0.7 copy-done.8
  74.6 3.9 %all-to-all-start.3 = ((f32[32,24,128]{2,1,0:T(8,128)}), f32[32,24,128]{2,1,0:T(8,128)S(1)}, u32[]{:S(2)}, u32[]{:S(2)}) async-start(f32[32,24,128]{2,1,0:T(8,128)} %bitcast.24), calls=%async_computation.3 | async-start | bytes 786432 | tf_op jit(solution)/shard_map/all_to_all | solution.py:337
  78.5 0.0 copy-start.7
  78.5 1.6 %copy-done.7 = bf16[1024,1024]{1,0:T(8,128)(2,1)S(1)} copy-done((bf16[1024,1024]{1,0:T(8,128)(2,1)S(1)}, bf16[1024,1024]{1,0:T(8,128)(2,1)}, u32[]{:S(2)}) %copy-start.7) | copy-done | bytes 2097176
  80.1 1.7 %leaf.1 = (f32[128,1024]{1,0:T(8,128)S(1)}, f32[8,128]{1,0:T(8,128)S(1)}) custom-call(s32[1,2]{1,0:T(1,128)S(1)} %copy-done.9, f32[128,1024]{1,0:T(8,128)S(1)} %get-tuple-element.14.residual_ref, f32[128,1024]{1,0:T(8,128)S(1)} %get-tuple-element.15.first_image_ref, bf16[1024,1024]{1,0:T(8,128)(2,1)S(1)} %copy-done.7, bf16[10,32,1024]{2,1,0:T(8,128)(2,1)S(1)} %copy-done.1, ...), custom_call_target="tpu_custom_call" | custom-call | flops 1073741824 | bytes 2097152 | tf_op jit(solution)/shard_map/leaf/pallas_call | solution.py:314
  81.8 7.0 %all-to-all-done.3 = f32[32,24,128]{2,1,0:T(8,128)S(1)} async-done(((f32[32,24,128]{2,1,0:T(8,128)}), f32[32,24,128]{2,1,0:T(8,128)S(1)}, u32[]{:S(2)}, u32[]{:S(2)}) %all-to-all-start.3) | async-done | bytes 393248 | tf_op jit(solution)/shard_map/all_to_all | solution.py:337
  88.9 15.8 %all_to_all.32 = f32[16,16,128]{2,1,0:T(8,128)S(1)} all-to-all(f32[16,16,128]{2,1,0:T(8,128)S(1)} %bitcast.23), channel_id=1, replica_groups={{0,32,64,96,128,160,192,224,256,288,320,352,384,416,448,480},{1,33,65,9..., dimensions={0} | all-to-all | bytes 262144 | tf_op jit(solution)/shard_map/all_to_all | solution.py:337
  104.6 0.1 depth.3
  104.7 16.7 %all_to_all.33 = f32[32,24,128]{2,1,0:T(8,128)S(1)} all-to-all(f32[32,24,128]{2,1,0:T(8,128)S(1)} %bitcast.18), channel_id=1, replica_groups={{0,1,2,3,4,5,6,7,8,9,10,11,12,13,14,15,16,17,18,19,20,21,22,23,24,25,26..., dimensions={0} | all-to-all | bytes 786432 | tf_op jit(solution)/shard_map/all_to_all | solution.py:337
  121.4 1.6 %end.1 = (f32[128,1024]{1,0:T(8,128)}, f32[128,1024]{1,0:T(8,128)}) custom-call(f32[768,128]{1,0:T(8,128)S(1)} %bitcast.19, f32[128,1024]{1,0:T(8,128)S(1)} %copy-done.5, f32[128,1024]{1,0:T(8,128)S(1)} %get-tuple-element.14.residual_ref, f32[128,1024]{1,0:T(8,128)S(1)} %get-tuple-element.15.first_image_ref, f32[128,1024]{1,0:T(8,128)S(1)} %get-tuple-element.18.image_ref, ...), custom_call_target="tpu_custom_call" | custom-call | flops 268435456 | bytes 2097152 | tf_op jit(solution)/shard_map/end/pallas_call | solution.py:314
  (2 shorter events, 0.1 us)
Async XLA Ops:
  0.6 1.1 copy-start
  1.7 1.0 copy-start.2
  2.7 1.0 copy-start.4
  3.7 11.7 %copy-start.1 = (bf16[10,32,1024]{2,1,0:T(8,128)(2,1)S(1)}, bf16[10,32,1024]{2,1,0:T(8,128)(2,1)}, u32[]{:S(2)}) copy-start(bf16[10,32,1024]{2,1,0:T(8,128)(2,1)} %basis_ref.9) | copy-start | bytes 1966084
  3.7 11.7 %copy-start.3 = (f32[1,10,64,64]{3,2,1,0:T(8,128)S(1)}, f32[1,10,64,64]{3,2,1,0:T(8,128)}, u32[]{:S(2)}) copy-start(f32[1,10,64,64]{3,2,1,0:T(8,128)} %coupling_ref.9) | copy-start | bytes 491524
  3.7 11.7 %copy-start.5 = (f32[128,1024]{1,0:T(8,128)S(1)}, f32[128,1024]{1,0:T(8,128)}, u32[]{:S(2)}) copy-start(f32[128,1024]{1,0:T(8,128)} %right_ref.7) | copy-start | bytes 1572868
  3.7 11.8 %copy-start.9 = (s32[1,2]{1,0:T(1,128)S(1)}, s32[1,2]{1,0:T(1,128)}, u32[]{:S(2)}) copy-start(s32[1,2]{1,0:T(1,128)} %sizes_ref.3) | copy-start | bytes 28
  3.7 11.8 %copy-start.10 = (f32[3,1024]{1,0:T(4,128)S(1)}, f32[3,1024]{1,0:T(4,128)}, u32[]{:S(2)}) copy-start(f32[3,1024]{1,0:T(4,128)} %coordinates_ref.1) | copy-start | bytes 36868
  3.8 11.8 %copy-start.11 = (s32[1,1024]{1,0:T(1,128)S(1)}, s32[1,1024]{1,0:T(1,128)}, u32[]{:S(2)}) copy-start(s32[1,1024]{1,0:T(1,128)} %order_ref.1) | copy-start | bytes 12292
  5.0 22.4 %all-to-all-start = ((f32[32,24,128]{2,1,0:T(8,128)}), f32[32,24,128]{2,1,0:T(8,128)S(1)}, u32[]{:S(2)}, u32[]{:S(2)}) async-start(f32[32,24,128]{2,1,0:T(8,128)} %bitcast), calls=%async_computation | async-start | bytes 786432 | tf_op jit(solution)/shard_map/all_to_all | solution.py:337
  26.1 1.3 %copy-start.6 = (bf16[1024,1024]{1,0:T(8,128)(2,1)}, bf16[1024,1024]{1,0:T(8,128)(2,1)S(1)}, u32[]{:S(2)}) copy-start(bf16[1024,1024]{1,0:T(8,128)(2,1)S(1)} %get-tuple-element.16.tile_ref) | copy-start | bytes 6291460
  73.9 0.7 copy-start.8
  74.6 14.2 %all-to-all-start.3 = ((f32[32,24,128]{2,1,0:T(8,128)}), f32[32,24,128]{2,1,0:T(8,128)S(1)}, u32[]{:S(2)}, u32[]{:S(2)}) async-start(f32[32,24,128]{2,1,0:T(8,128)} %bitcast.24), calls=%async_computation.3 | async-start | bytes 786432 | tf_op jit(solution)/shard_map/all_to_all | solution.py:337
  78.5 1.6 %copy-start.7 = (bf16[1024,1024]{1,0:T(8,128)(2,1)S(1)}, bf16[1024,1024]{1,0:T(8,128)(2,1)}, u32[]{:S(2)}) copy-start(bf16[1024,1024]{1,0:T(8,128)(2,1)} %copy-done.6) | copy-start | bytes 6291460

commit v2 on v1

--- a/solution.py
+++ b/solution.py
@@ -18,8 +18,9 @@
 POINTS = 1024
 PLANE = 32
 DEPTH = 16
-ROWS = 24
-Z_ROWS = 16
+ROWS = 18
+BACK = 21
+Z_ROWS = 11
 LEAST = 384
 MOST = 640
 
@@ -80,13 +81,25 @@
             send_ref[pl.ds(first_row(level) + half, PLANE, stride=ROWS), :] = partial[
                 PLANE * half : PLANE * (half + 1)
             ]
-    blank = jnp.zeros((PLANE, PROBES), f32)
-    for row in range(18, ROWS):
-        send_ref[pl.ds(row, PLANE, stride=ROWS), :] = blank
-
-
-def start_kernel(right_ref, basis_ref, coupling_ref, send_ref):
+
+
+def start_kernel(
+    right_hbm, basis_hbm, coupling_hbm, send_hbm,
+    right_ref, basis_ref, coupling_ref, send_ref, sems,
+):
+    copies = [
+        pltpu.make_async_copy(right_hbm, right_ref, sems.at[0]),
+        pltpu.make_async_copy(basis_hbm, basis_ref, sems.at[1]),
+        pltpu.make_async_copy(coupling_hbm, coupling_ref, sems.at[2]),
+    ]
+    for copy in copies:
+        copy.start()
+    for copy in copies:
+        copy.wait()
     send_levels(right_ref[...].astype(bf16), basis_ref, coupling_ref, send_ref)
+    out = pltpu.make_async_copy(send_ref, send_hbm, sems.at[3])
+    out.start()
+    out.wait()
 
 
 def leaf_level(v, rounded, boundary, tile, basis_ref, coupling_ref):
@@ -106,49 +119,55 @@
 
 def tile_kernel(
     coordinates_ref, order_ref, sizes_ref, right_ref, basis_ref, coupling_ref,
-    tile_ref, image_ref, scalars_ref, pick_ref, column_ref,
+    tile_ref, image_ref, scalars_ref, down_ref,
 ):
     boundary = sizes_ref[0, 0]
     order = order_ref[...]
-    step = 128
-
-    @pl.loop(0, POINTS // step)
-    def _(block):
-        start = pl.multiple_of(block * step, step)
-        ids = start + lax.broadcasted_iota(jnp.int32, (step, POINTS), 0)
-        pick_ref[pl.ds(start, step), :] = jnp.where(ids == order, 1.0, 0.0).astype(bf16)
-
-    whole = coordinates_ref[...]
-    high = whole.astype(bf16).astype(f32)
-    middle = (whole - high).astype(bf16).astype(f32)
-    low = whole - high - middle
-    terms = jnp.concatenate([high, middle, low], axis=0).astype(bf16)
-    picked = dot(terms, pick_ref[...], NN)
-    x = (picked[0:3] + picked[3:6]) + picked[6:9]
-    column_ref[...] = jnp.concatenate([x, jnp.zeros((5, POINTS), f32)], axis=0).T
+    place, segment = jnp.bitwise_and(order, 127), jnp.right_shift(order, 7)
+    sources = [
+        jnp.concatenate(
+            [coordinates_ref[:, start : start + 128], jnp.zeros((5, 128), f32)], axis=0
+        )
+        for start in range(0, POINTS, 128)
+    ]
+    pieces = []
+    for start in range(0, POINTS, 128):
+        lane = jnp.broadcast_to(place[:, start : start + 128], (8, 128))
+        chosen = jnp.broadcast_to(segment[:, start : start + 128], (8, 128))
+        piece = jnp.zeros((8, 128), f32)
+        for number, source in enumerate(sources):
+            piece = jnp.where(chosen == number, jnp.take_along_axis(source, lane, axis=1), piece)
+        pieces.append(piece)
+    x = jnp.concatenate(pieces, axis=1)
+    column = x.T
+    for c in range(3):
+        down_ref[c] = jnp.broadcast_to(column[:, c : c + 1], (POINTS, 128))
+    edge = boundary.astype(f32) - 0.5
 
     def fill(row_start, row_stop, col_start, col_stop):
-        group = 16
+        group = 128
         width = col_stop - col_start
         across = [x[c : c + 1, col_start:col_stop] for c in range(3)]
-        col_ids = col_start + lax.broadcasted_iota(jnp.int32, (group, width), 1)
-        col_first = col_ids < boundary
+        col_ids = col_start + lax.broadcasted_iota(jnp.int32, (1, width), 1)
+        col_side = col_ids.astype(f32) - edge
+
+        def widen(block):
+            return jnp.concatenate([block] * (width // 128), axis=1)
 
         @pl.loop(0, (row_stop - row_start) // group)
         def _(block):
             start = pl.multiple_of(row_start + block * group, group)
-            down = column_ref[pl.ds(start, group), :]
-            dist_sq = jnp.zeros((group, width), f32)
+            dist_sq = None
             for c in range(3):
-                offset = down[:, c : c + 1] - across[c]
-                dist_sq = dist_sq + offset * offset
-            scaled = SQRT_THREE * jnp.sqrt(dist_sq)
+                offset = widen(down_ref[c, pl.ds(start, group), :]) - across[c]
+                dist_sq = offset * offset if c == 0 else dist_sq + offset * offset
+            root = dist_sq * lax.rsqrt(jnp.maximum(dist_sq, 1e-37))
+            scaled = SQRT_THREE * root
             values = (1.0 + scaled) * jnp.exp(-scaled)
-            ids = start + lax.broadcasted_iota(jnp.int32, (group, width), 0)
-            limit = jnp.where(ids < boundary, 0, boundary)
-            low_end = jnp.where(ids < boundary, boundary, POINTS)
-            same = (col_ids >= limit) & (col_ids < low_end)
-            values = jnp.where(same, values, 0.0) + jnp.where(ids == col_ids, NOISE_VAR, 0.0)
+            ids = start + lax.broadcasted_iota(jnp.int32, (group, 128), 0)
+            same = widen(ids.astype(f32) - edge) * col_side > 0.0
+            values = jnp.where(same, values, 0.0)
+            values = values + jnp.where(widen(ids) == col_ids, NOISE_VAR, 0.0)
             tile_ref[pl.ds(start, group), col_start:col_stop] = values.astype(bf16)
 
     tile_ref[:LEAST, MOST:] = jnp.zeros((LEAST, POINTS - MOST), bf16)
@@ -163,8 +182,7 @@
     )
     image_ref[...] = image
     scalars_ref[...] = jnp.concatenate(
-        [jnp.zeros((2, PROBES), f32), curvature, rows_of(v * v), jnp.zeros((4, PROBES), f32)],
-        axis=0,
+        [curvature, rows_of(v * v), jnp.zeros((6, PROBES), f32)], axis=0
     )
 
 
@@ -179,11 +197,10 @@
     image_ref[...] = image
     scalars_ref[...] = jnp.concatenate(
         [
-            jnp.zeros((2, PROBES), f32),
             curvature,
             rows_of(v * v),
             rows_of(v * first_image_ref[...]),
-            jnp.zeros((3, PROBES), f32),
+            jnp.zeros((5, PROBES), f32),
         ],
         axis=0,
     )
@@ -197,8 +214,8 @@
     return sums
 
 
-def total(got_ref, count, rows, start):
-    parts = [got_ref[rows * d + start : rows * d + start + 8, :] for d in range(count)]
+def total(got_ref, count, stride, start, rows):
+    parts = [got_ref[stride * d + start : stride * d + start + rows, :] for d in range(count)]
     while len(parts) > 1:
         parts = [parts[2 * i] + parts[2 * i + 1] for i in range(len(parts) // 2)]
     return parts[0]
@@ -217,14 +234,14 @@
     square = jnp.zeros((8, PROBES), f32)
     for level in range(1, 5):
         square = jnp.where(ids // 2 == level - 1, squares(sums[level]), square)
-    fifth = total(got_ref, PLANE, ROWS, 16)
-    square = square + jnp.where(ids < 2, fifth * fifth, 0.0)
-    curvature = jnp.sum(square, axis=0, keepdims=True)
-    scalars = scalars_ref[...] + jnp.where(ids == 2, curvature, 0.0)
-    upper = total(got_ref, PLANE, ROWS, 8)
+    fifth = total(got_ref, PLANE, ROWS, 16, 2)
+    curvature = jnp.sum(square, axis=0, keepdims=True) + jnp.sum(
+        fifth * fifth, axis=0, keepdims=True
+    )
+    scalars = scalars_ref[0:3, :] + jnp.where(row_ids(3) == 0, curvature, 0.0)
+    block = jnp.concatenate([total(got_ref, PLANE, ROWS, 8, 8), scalars], axis=0)
     for z in range(DEPTH):
-        send_ref[Z_ROWS * z : Z_ROWS * z + 8, :] = upper
-        send_ref[Z_ROWS * z + 8 : Z_ROWS * (z + 1), :] = scalars
+        send_ref[Z_ROWS * z : Z_ROWS * (z + 1), :] = block
 
 
 def depth_kernel(got_ref, z_got_ref, send_ref):
@@ -243,17 +260,16 @@
         nodes = [nodes[2 * i] + nodes[2 * i + 1] for i in range(len(nodes) // 2)]
         square = jnp.where(ids // 2 == level, squares(nodes), square)
     curvature = jnp.sum(square, axis=0, keepdims=True)
-    scalars = total(z_got_ref, DEPTH, Z_ROWS, 8) + jnp.where(ids == 2, curvature, 0.0)
-    fifth = total(got_ref, PLANE, ROWS, 16)
-    last = jnp.where(ids < 2, fifth, scalars)
+    scalars = total(z_got_ref, DEPTH, Z_ROWS, 8, 3)
+    scalars = scalars + jnp.where(row_ids(3) == 0, curvature, 0.0)
+    tail = jnp.concatenate([pair, total(got_ref, PLANE, ROWS, 16, 2), scalars], axis=0)
     sums = pair_sums(got_ref)
     for d in range(PLANE):
         first = sums[4][d >> 4]
         for level in (3, 2, 1):
             first = jnp.where(ids // 2 == level - 1, sums[level][d >> level], first)
-        send_ref[ROWS * d : ROWS * d + 8, :] = first
-        send_ref[ROWS * d + 8 : ROWS * d + 16, :] = pair
-        send_ref[ROWS * d + 16 : ROWS * d + 24, :] = last
+        send_ref[BACK * d : BACK * d + 8, :] = first
+        send_ref[BACK * d + 8 : BACK * (d + 1), :] = tail
 
 
 def expand(got_ref, basis_ref, coupling_ref):
@@ -261,7 +277,7 @@
     for level in range(1, 10):
         mixed = jnp.concatenate(
             [
-                got_ref[pl.ds(first_row(level) + half, PLANE, stride=ROWS), :]
+                got_ref[pl.ds(first_row(level) + half, PLANE, stride=BACK), :]
                 for half in range(2)
             ],
             axis=0,
@@ -273,10 +289,10 @@
 
 def turn_kernel(
     got_ref, right_ref, image_ref, basis_ref, coupling_ref,
-    residual_ref, whole_image_ref, send_ref, keep_ref,
+    residual_ref, whole_image_ref, send_hbm, keep_ref, send_ref, sem,
 ):
-    scalars = total(got_ref, PLANE, ROWS, 16)
-    curvature, norm = scalars[2:3], scalars[3:4]
+    scalars = total(got_ref, PLANE, BACK, 18, 3)
+    curvature, norm = scalars[0:1], scalars[1:2]
     step = norm / curvature
     whole = image_ref[...] + expand(got_ref, basis_ref, coupling_ref)
     residual = right_ref[...] - down_rows(step) * whole
@@ -286,14 +302,17 @@
         [step, curvature, norm, jnp.zeros((5, PROBES), f32)], axis=0
     )
     send_levels(residual.astype(bf16), basis_ref, coupling_ref, send_ref)
+    out = pltpu.make_async_copy(send_ref, send_hbm, sem.at[0])
+    out.start()
+    out.wait()
 
 
 def end_kernel(
     got_ref, right_ref, residual_ref, first_image_ref, image_ref, basis_ref, coupling_ref,
     keep_ref, solution_ref, last_ref,
 ):
-    scalars = total(got_ref, PLANE, ROWS, 16)
-    own, norm, cross = scalars[2:3], scalars[3:4], scalars[4:5]
+    scalars = total(got_ref, PLANE, BACK, 18, 3)
+    own, norm, cross = scalars[0:1], scalars[1:2], scalars[2:3]
     step, curvature, norm_before = keep_ref[0:1, :], keep_ref[1:2, :], keep_ref[2:3, :]
     ratio = norm / norm_before
     step_now = norm / (own + 2.0 * ratio * cross + ratio * ratio * curvature)
@@ -307,15 +326,18 @@
 
 VMEM = pl.BlockSpec(memory_space=pltpu.VMEM)
 SMEM = pl.BlockSpec(memory_space=pltpu.SMEM)
-
-
-def call(body, outs, ins, megabytes, cost, scratch=(), name=None):
+HBM = pl.BlockSpec(memory_space=pltpu.HBM)
+
+
+def call(body, outs, ins, megabytes, cost, scratch=(), name=None, far_ins=(), far_outs=()):
     specs = [SMEM if a.dtype == jnp.int32 and a.shape == (1, 2) else VMEM for a in ins]
+    for place in far_ins:
+        specs[place] = HBM
     return pl.pallas_call(
         body,
         out_shape=[jax.ShapeDtypeStruct(shape, kind) for shape, kind in outs],
         in_specs=specs,
-        out_specs=[VMEM] * len(outs),
+        out_specs=[HBM if place in far_outs else VMEM for place in range(len(outs))],
         scratch_shapes=list(scratch),
         compiler_params=pltpu.CompilerParams(vmem_limit_bytes=megabytes << 20),
         cost_estimate=pl.CostEstimate(flops=cost, bytes_accessed=2 << 20, transcendentals=0),
@@ -333,7 +355,7 @@
 
 def exchange(rows, groups):
     members = len(groups[0])
-    blocks = rows.reshape(members, rows.shape[0] // members, PROBES)
+    blocks = rows.reshape(members, 1, rows.shape[0] // members * PROBES)
     got = lax.all_to_all(blocks, "pts", 0, 0, axis_index_groups=groups)
     return got.reshape(rows.shape)
 
@@ -343,19 +365,35 @@
     planes, depths = plane_groups(count), depth_groups(count)
     field = ((PROBES, POINTS), f32)
     message = ((PLANE * ROWS, PROBES), f32)
+    back_message = ((PLANE * BACK, PROBES), f32)
     z_message = ((DEPTH * Z_ROWS, PROBES), f32)
     row_block = ((8, PROBES), f32)
+    message_scratch = pltpu.VMEM(*message)
 
     def tree(send, scalars_of):
         got = exchange(send, planes)
         local = scalars_of()
-        (z_send,) = call(plane_kernel, [z_message], [got, local[-1]], 8, 1 << 20, name="plane")
+        (z_send,) = call(plane_kernel, [z_message], [got, local[-1]], 2, 1 << 20, name="plane")
         z_got = exchange(z_send, depths)
-        (back,) = call(depth_kernel, [message], [got, z_got], 8, 1 << 20, name="depth")
+        (back,) = call(depth_kernel, [back_message], [got, z_got], 2, 1 << 20, name="depth")
         return local, exchange(back, planes)
 
     (send,) = call(
-        start_kernel, [message], [right_side, level_basis, coupling], 16, 1 << 26, name="start"
+        start_kernel,
+        [message],
+        [right_side, level_basis, coupling],
+        60,
+        1 << 26,
+        scratch=[
+            pltpu.VMEM(right_side.shape, f32),
+            pltpu.VMEM(level_basis.shape, bf16),
+            pltpu.VMEM(coupling.shape, f32),
+            message_scratch,
+            pltpu.SemaphoreType.DMA((4,)),
+        ],
+        name="start",
+        far_ins=(0, 1, 2),
+        far_outs=(0,),
     )
     (tile, image, _), got = tree(
         send,
@@ -363,9 +401,9 @@
             tile_kernel,
             [((POINTS, POINTS), bf16), field, row_block],
             [coordinates, tree_order, leaf_sizes, right_side, level_basis, coupling],
-            24,
+            12,
             4 << 30,
-            scratch=[pltpu.VMEM((POINTS, POINTS), bf16), pltpu.VMEM((POINTS, 8), f32)],
+            scratch=[pltpu.VMEM((3, POINTS, 128), f32)],
             name="tile",
         ),
     )
@@ -373,9 +411,11 @@
         turn_kernel,
         [field, field, message, row_block],
         [got, right_side, image, level_basis, coupling],
-        16,
+        8,
         1 << 28,
+        scratch=[message_scratch, pltpu.SemaphoreType.DMA((1,))],
         name="turn",
+        far_outs=(2,),
     )
     (image, _), got = tree(
         send,
@@ -383,7 +423,7 @@
             leaf_kernel,
             [field, row_block],
             [leaf_sizes, residual, first_image, tile, level_basis, coupling],
-            24,
+            8,
             1 << 30,
             name="leaf",
         ),
@@ -393,7 +433,7 @@
             end_kernel,
             [field, field],
             [got, right_side, residual, first_image, image, level_basis, coupling, keep],
-            16,
+            8,
             1 << 28,
             name="end",
         )

time: 124 us -> 111 us (0.90)
  blocking collectives: 77.8 us -> 70.9 us
  Pallas kernels: 16.4 us -> 12.6 us
  local copies, waits for them, and re-layouts: 6.77 us -> 3.65 us
  waiting for transfers between devices: 6.99 us -> 8.81 us
    all_to_all x4, blocking collectives: 77.8 us -> 70.9 us  [exchange(): got = lax.all_to_all(blocks, 'pts', 0, 0, axis_index_groups=groups)]
    pallas_call x9, Pallas kernels: 16.4 us -> 12.6 us  [call(): pl.pallas_call(body, out_shape=[jax.ShapeDtypeStruct(shape, kind) for sha...]
    unnamed x24 -> x18, local copies, waits for them, and re-layouts: 6.77 us -> 3.65 us
    all_to_all x2, waiting for transfers between devices: 6.99 us -> 8.81 us  [exchange(): got = lax.all_to_all(blocks, 'pts', 0, 0, axis_index_groups=groups)]
  transfers between devices with their start and end apart: 2 -> 2, of which waited for: 1 -> 2; matrix products, arithmetic and copies ran while one was open for 0% -> 0% of each run, Pallas kernels for 10% -> 6%
where the time goes in v2:
time: 111 us
  blocking collectives  70.9 us (64%)
  starting transfers between devices  14.3 us (13%)
  Pallas kernels  12.6 us (11%)
  waiting for transfers between devices  8.81 us (8%)
  local copies, waits for them, and re-layouts  3.65 us (3%)
    all_to_all x4, blocking collectives, exchange(): got = lax.all_to_all(blocks, 'pts', 0, 0, axis_index_groups=groups)  70.9 us
    all_to_all x2, starting transfers between devices, exchange(): got = lax.all_to_all(blocks, 'pts', 0, 0, axis_index_groups=groups)  14.3 us
    pallas_call x9, Pallas kernels, call(): pl.pallas_call(body, out_shape=[jax.ShapeDtypeStruct(shape, kind) for sha...  12.6 us
    all_to_all x2, waiting for transfers between devices, exchange(): got = lax.all_to_all(blocks, 'pts', 0, 0, axis_index_groups=groups)  8.81 us
    unnamed x18, local copies, waits for them, and re-layouts  3.65 us
  transfers between devices with their start and end apart: 2, of which 2 were waited for; matrix products, arithmetic and copies ran while one was open for 0% of the time, Pallas kernels for 6%

profile of v2, /device:TPU:1, one launch (start us, length us, event | category | flops | bytes accessed | tf_op | source)
XLA Modules:
  0.0 111.0 jit_solution(1136706098477239220)
XLA Ops:
  0.6 0.0 copy-start.1
  0.6 0.0 copy-start
  0.7 0.0 copy-start.2
  0.7 0.0 copy-start.6
  0.7 0.0 copy-start.8
  0.7 0.0 copy-start.7
  0.7 2.7 %start.1 = f32[576,128]{1,0:T(8,128)} custom-call(f32[128,1024]{1,0:T(8,128)} %right_ref.5, bf16[10,32,1024]{2,1,0:T(8,128)(2,1)} %basis_ref.7, f32[1,10,64,64]{3,2,1,0:T(8,128)} %coupling_ref.7), custom_call_target="tpu_custom_call" | custom-call | flops 67108864 | bytes 2097152 | tf_op jit(solution)/shard_map/start/pallas_call | solution.py:336
  3.4 10.4 %all-to-all-start = ((f32[32,1,2304]{2,1,0:T(1,128)}), f32[32,1,2304]{2,1,0:T(1,128)S(1)}, u32[]{:S(2)}, u32[]{:S(2)}) async-start(f32[32,1,2304]{2,1,0:T(1,128)} %bitcast.25), calls=%async_computation | async-start | bytes 589824 | tf_op jit(solution)/shard_map/all_to_all | solution.py:359
  13.8 0.0 copy-done.1
  13.8 0.0 copy-done
  13.9 0.0 copy-done.2
  13.9 0.0 copy-done.6
  13.9 0.0 copy-done.8
  13.9 0.0 copy-done.7
  13.9 5.1 %tile.1 = (bf16[1024,1024]{1,0:T(8,128)(2,1)S(1)}, f32[128,1024]{1,0:T(8,128)S(1)}, f32[8,128]{1,0:T(8,128)S(1)}) custom-call(f32[3,1024]{1,0:T(4,128)S(1)} %copy-done.7, s32[1,1024]{1,0:T(1,128)S(1)} %copy-done.8, s32[1,2]{1,0:T(1,128)S(1)} %copy-done.6, f32[128,1024]{1,0:T(8,128)S(1)} %copy-done.2, bf16[10,32,1024]{2,1,0:T(8,128)(2,1)S(1)} %copy-done, ...), custom_call_target="tpu_custom_call" | custom-call | flops 4294967296 | bytes 2097152 | tf_op jit(solution)/shard_map/tile/pallas_call | solution.py:336
  19.0 0.0 copy-start.3
  19.1 1.3 %copy-done.3 = bf16[1024,1024]{1,0:T(8,128)(2,1)} copy-done((bf16[1024,1024]{1,0:T(8,128)(2,1)}, bf16[1024,1024]{1,0:T(8,128)(2,1)S(1)}, u32[]{:S(2)}) %copy-start.3) | copy-done | bytes 2097176
  20.4 2.8 %all-to-all-done = f32[32,1,2304]{2,1,0:T(1,128)S(1)} async-done(((f32[32,1,2304]{2,1,0:T(1,128)}), f32[32,1,2304]{2,1,0:T(1,128)S(1)}, u32[]{:S(2)}, u32[]{:S(2)}) %all-to-all-start) | async-done | bytes 294944 | tf_op jit(solution)/shard_map/all_to_all | solution.py:359
  23.2 24.6 %all_to_all.30 = f32[16,1,1408]{2,1,0:T(1,128)S(1)} all-to-all(f32[16,1,1408]{2,1,0:T(1,128)S(1)} %bitcast.22), channel_id=1, replica_groups={{0,32,64,96,128,160,192,224,256,288,320,352,384,416,448,480},{1,33,65,9..., dimensions={0} | all-to-all | bytes 180224 | tf_op jit(solution)/shard_map/all_to_all | solution.py:359
  47.8 0.1 depth.2
  47.8 16.4 %all_to_all.31 = f32[32,1,2688]{2,1,0:T(1,128)S(1)} all-to-all(f32[32,1,2688]{2,1,0:T(1,128)S(1)} %bitcast.17), channel_id=1, replica_groups={{0,1,2,3,4,5,6,7,8,9,10,11,12,13,14,15,16,17,18,19,20,21,22,23,24,25,26..., dimensions={0} | all-to-all | bytes 688128 | tf_op jit(solution)/shard_map/all_to_all | solution.py:359
  64.2 1.2 %turn.1 = (f32[128,1024]{1,0:T(8,128)S(1)}, f32[128,1024]{1,0:T(8,128)S(1)}, f32[576,128]{1,0:T(8,128)S(1)}, f32[8,128]{1,0:T(8,128)S(1)}) custom-call(f32[672,128]{1,0:T(8,128)S(1)} %bitcast.16, f32[128,1024]{1,0:T(8,128)S(1)} %copy-done.2, f32[128,1024]{1,0:T(8,128)S(1)} %get-tuple-element.12.image_ref, bf16[10,32,1024]{2,1,0:T(8,128)(2,1)S(1)} %copy-done, ...), custom_call_target="tpu_custom_call" | custom-call | flops 268435456 | bytes 2097152 | tf_op jit(solution)/shard_map/turn/pallas_call | solution.py:336
  65.4 0.0 copy-start.5
  65.4 0.7 copy-done.5
  66.1 3.8 %all-to-all-start.3 = ((f32[32,1,2304]{2,1,0:T(1,128)}), f32[32,1,2304]{2,1,0:T(1,128)S(1)}, u32[]{:S(2)}, u32[]{:S(2)}) async-start(f32[32,1,2304]{2,1,0:T(1,128)} %bitcast.24), calls=%async_computation.3 | async-start | bytes 589824 | tf_op jit(solution)/shard_map/all_to_all | solution.py:359
  70.0 0.0 copy-start.4
  70.0 1.6 %copy-done.4 = bf16[1024,1024]{1,0:T(8,128)(2,1)S(1)} copy-done((bf16[1024,1024]{1,0:T(8,128)(2,1)S(1)}, bf16[1024,1024]{1,0:T(8,128)(2,1)}, u32[]{:S(2)}) %copy-start.4) | copy-done | bytes 2097176
  71.6 1.7 %leaf.1 = (f32[128,1024]{1,0:T(8,128)S(1)}, f32[8,128]{1,0:T(8,128)S(1)}) custom-call(s32[1,2]{1,0:T(1,128)S(1)} %copy-done.6, f32[128,1024]{1,0:T(8,128)S(1)} %get-tuple-element.14.residual_ref, f32[128,1024]{1,0:T(8,128)S(1)} %get-tuple-element.15.first_image_ref, bf16[1024,1024]{1,0:T(8,128)(2,1)S(1)} %copy-done.4, bf16[10,32,1024]{2,1,0:T(8,128)(2,1)S(1)} %copy-done, ...), custom_call_target="tpu_custom_call" | custom-call | flops 1073741824 | bytes 2097152 | tf_op jit(solution)/shard_map/leaf/pallas_call | solution.py:336
  73.3 6.0 %all-to-all-done.3 = f32[32,1,2304]{2,1,0:T(1,128)S(1)} async-done(((f32[32,1,2304]{2,1,0:T(1,128)}), f32[32,1,2304]{2,1,0:T(1,128)S(1)}, u32[]{:S(2)}, u32[]{:S(2)}) %all-to-all-start.3) | async-done | bytes 294944 | tf_op jit(solution)/shard_map/all_to_all | solution.py:359
  79.4 14.7 %all_to_all.32 = f32[16,1,1408]{2,1,0:T(1,128)S(1)} all-to-all(f32[16,1,1408]{2,1,0:T(1,128)S(1)} %bitcast.23), channel_id=1, replica_groups={{0,32,64,96,128,160,192,224,256,288,320,352,384,416,448,480},{1,33,65,9..., dimensions={0} | all-to-all | bytes 180224 | tf_op jit(solution)/shard_map/all_to_all | solution.py:359
  94.1 0.1 depth.3
  94.1 15.2 %all_to_all.33 = f32[32,1,2688]{2,1,0:T(1,128)S(1)} all-to-all(f32[32,1,2688]{2,1,0:T(1,128)S(1)} %bitcast.18), channel_id=1, replica_groups={{0,1,2,3,4,5,6,7,8,9,10,11,12,13,14,15,16,17,18,19,20,21,22,23,24,25,26..., dimensions={0} | all-to-all | bytes 688128 | tf_op jit(solution)/shard_map/all_to_all | solution.py:359
  109.3 1.7 %end.1 = (f32[128,1024]{1,0:T(8,128)}, f32[128,1024]{1,0:T(8,128)}) custom-call(f32[672,128]{1,0:T(8,128)S(1)} %bitcast.19, f32[128,1024]{1,0:T(8,128)S(1)} %copy-done.2, f32[128,1024]{1,0:T(8,128)S(1)} %get-tuple-element.14.residual_ref, f32[128,1024]{1,0:T(8,128)S(1)} %get-tuple-element.15.first_image_ref, f32[128,1024]{1,0:T(8,128)S(1)} %get-tuple-element.18.image_ref, ...), custom_call_target="tpu_custom_call" | custom-call | flops 268435456 | bytes 2097152 | tf_op jit(solution)/shard_map/end/pallas_call | solution.py:336
  (2 shorter events, 0.1 us)
Async XLA Ops:
  0.6 13.2 %copy-start.1 = (f32[1,10,64,64]{3,2,1,0:T(8,128)S(1)}, f32[1,10,64,64]{3,2,1,0:T(8,128)}, u32[]{:S(2)}) copy-start(f32[1,10,64,64]{3,2,1,0:T(8,128)} %coupling_ref.7) | copy-start | bytes 491524
  0.6 13.2 %copy-start = (bf16[10,32,1024]{2,1,0:T(8,128)(2,1)S(1)}, bf16[10,32,1024]{2,1,0:T(8,128)(2,1)}, u32[]{:S(2)}) copy-start(bf16[10,32,1024]{2,1,0:T(8,128)(2,1)} %basis_ref.7) | copy-start | bytes 1966084
  0.7 13.2 %copy-start.2 = (f32[128,1024]{1,0:T(8,128)S(1)}, f32[128,1024]{1,0:T(8,128)}, u32[]{:S(2)}) copy-start(f32[128,1024]{1,0:T(8,128)} %right_ref.5) | copy-start | bytes 1572868
  0.7 13.2 %copy-start.6 = (s32[1,2]{1,0:T(1,128)S(1)}, s32[1,2]{1,0:T(1,128)}, u32[]{:S(2)}) copy-start(s32[1,2]{1,0:T(1,128)} %sizes_ref.3) | copy-start | bytes 28
  0.7 13.2 %copy-start.8 = (s32[1,1024]{1,0:T(1,128)S(1)}, s32[1,1024]{1,0:T(1,128)}, u32[]{:S(2)}) copy-start(s32[1,1024]{1,0:T(1,128)} %order_ref.1) | copy-start | bytes 12292
  0.7 13.2 %copy-start.7 = (f32[3,1024]{1,0:T(4,128)S(1)}, f32[3,1024]{1,0:T(4,128)}, u32[]{:S(2)}) copy-start(f32[3,1024]{1,0:T(4,128)} %coordinates_ref.1) | copy-start | bytes 36868
  3.4 19.8 %all-to-all-start = ((f32[32,1,2304]{2,1,0:T(1,128)}), f32[32,1,2304]{2,1,0:T(1,128)S(1)}, u32[]{:S(2)}, u32[]{:S(2)}) async-start(f32[32,1,2304]{2,1,0:T(1,128)} %bitcast.25), calls=%async_computation | async-start | bytes 589824 | tf_op jit(solution)/shard_map/all_to_all | solution.py:359
  19.0 1.3 %copy-start.3 = (bf16[1024,1024]{1,0:T(8,128)(2,1)}, bf16[1024,1024]{1,0:T(8,128)(2,1)S(1)}, u32[]{:S(2)}) copy-start(bf16[1024,1024]{1,0:T(8,128)(2,1)S(1)} %get-tuple-element.16.tile_ref) | copy-start | bytes 6291460
  65.4 0.7 copy-start.5
  66.1 13.2 %all-to-all-start.3 = ((f32[32,1,2304]{2,1,0:T(1,128)}), f32[32,1,2304]{2,1,0:T(1,128)S(1)}, u32[]{:S(2)}, u32[]{:S(2)}) async-start(f32[32,1,2304]{2,1,0:T(1,128)} %bitcast.24), calls=%async_computation.3 | async-start | bytes 589824 | tf_op jit(solution)/shard_map/all_to_all | solution.py:359
  70.0 1.6 %copy-start.4 = (bf16[1024,1024]{1,0:T(8,128)(2,1)S(1)}, bf16[1024,1024]{1,0:T(8,128)(2,1)}, u32[]{:S(2)}) copy-start(bf16[1024,1024]{1,0:T(8,128)(2,1)} %copy-done.3) | copy-start | bytes 6291460

commit v3 on v2

--- a/solution.py
+++ b/solution.py
@@ -23,6 +23,7 @@
 Z_ROWS = 11
 LEAST = 384
 MOST = 640
+HALVES = 2
 
 NT = (((1,), (1,)), ((), ()))
 TN = (((0,), (0,)), ((), ()))
@@ -71,9 +72,7 @@
     return lax.broadcasted_iota(jnp.int32, (rows, PROBES), 0)
 
 
-def send_levels(rounded, basis_ref, coupling_ref, send_ref):
-    wide = basis_ref[1:10].reshape(9 * RANK, POINTS)
-    projected = dot(wide, rounded, NT)
+def send_levels(projected, coupling_ref, send_ref):
     for level in range(1, 10):
         own = coupling_ref[0, level, :RANK, :]
         partial = dot_split(own, projected[RANK * (level - 1) : RANK * level], TN)
@@ -87,23 +86,42 @@
     right_hbm, basis_hbm, coupling_hbm, send_hbm,
     right_ref, basis_ref, coupling_ref, send_ref, sems,
 ):
-    copies = [
-        pltpu.make_async_copy(right_hbm, right_ref, sems.at[0]),
-        pltpu.make_async_copy(basis_hbm, basis_ref, sems.at[1]),
-        pltpu.make_async_copy(coupling_hbm, coupling_ref, sems.at[2]),
-    ]
-    for copy in copies:
-        copy.start()
-    for copy in copies:
-        copy.wait()
-    send_levels(right_ref[...].astype(bf16), basis_ref, coupling_ref, send_ref)
-    out = pltpu.make_async_copy(send_ref, send_hbm, sems.at[3])
+    width = POINTS // HALVES
+    fetches = []
+    for half in range(HALVES):
+        span = pl.ds(width * half, width)
+        right_copy = pltpu.make_async_copy(
+            right_hbm.at[:, span], right_ref.at[:, span], sems.at[2 * half]
+        )
+        basis_copy = pltpu.make_async_copy(
+            basis_hbm.at[pl.ds(1, 9), :, span],
+            basis_ref.at[:, :, span],
+            sems.at[2 * half + 1],
+        )
+        right_copy.start()
+        basis_copy.start()
+        fetches.append((right_copy, basis_copy))
+    factors = pltpu.make_async_copy(coupling_hbm, coupling_ref, sems.at[2 * HALVES])
+    factors.start()
+    projected = None
+    for half, (right_copy, basis_copy) in enumerate(fetches):
+        span = slice(width * half, width * (half + 1))
+        right_copy.wait()
+        basis_copy.wait()
+        part = dot(
+            basis_ref[:, :, span].reshape(9 * RANK, width),
+            right_ref[:, span].astype(bf16),
+            NT,
+        )
+        projected = part if half == 0 else projected + part
+    factors.wait()
+    send_levels(projected, coupling_ref, send_ref)
+    out = pltpu.make_async_copy(send_ref, send_hbm, sems.at[2 * HALVES + 1])
     out.start()
     out.wait()
 
 
-def leaf_level(v, rounded, boundary, tile, basis_ref, coupling_ref):
-    leaf = dot(rounded, tile, NN)
+def leaf_level(v, rounded, leaf, boundary, basis_ref, coupling_ref):
     wide = basis_ref[0].astype(f32)
     in_first = lax.broadcasted_iota(jnp.int32, (RANK, POINTS), 1) < boundary
     both = jnp.concatenate(
@@ -119,7 +137,7 @@
 
 def tile_kernel(
     coordinates_ref, order_ref, sizes_ref, right_ref, basis_ref, coupling_ref,
-    tile_ref, image_ref, scalars_ref, down_ref,
+    tile_hbm, image_ref, scalars_ref, tile_ref, down_ref, sems,
 ):
     boundary = sizes_ref[0, 0]
     order = order_ref[...]
@@ -172,27 +190,49 @@
 
     tile_ref[:LEAST, MOST:] = jnp.zeros((LEAST, POINTS - MOST), bf16)
     tile_ref[MOST:, :LEAST] = jnp.zeros((POINTS - MOST, LEAST), bf16)
-    fill(0, LEAST, 0, MOST)
-    fill(LEAST, MOST, 0, POINTS)
-    fill(MOST, POINTS, LEAST, POINTS)
+    copies = []
+    for number, (start, stop, low, high) in enumerate(
+        ((0, LEAST, 0, MOST), (LEAST, MOST, 0, POINTS), (MOST, POINTS, LEAST, POINTS))
+    ):
+        fill(start, stop, low, high)
+        rows = pl.ds(start, stop - start)
+        copies.append(
+            pltpu.make_async_copy(tile_ref.at[rows], tile_hbm.at[rows], sems.at[number])
+        )
+        copies[-1].start()
 
     v = right_ref[...]
-    image, curvature = leaf_level(
-        v, v.astype(bf16), boundary, tile_ref[...], basis_ref, coupling_ref
-    )
+    rounded = v.astype(bf16)
+    leaf = dot(rounded, tile_ref[...], NN)
+    image, curvature = leaf_level(v, rounded, leaf, boundary, basis_ref, coupling_ref)
     image_ref[...] = image
     scalars_ref[...] = jnp.concatenate(
         [curvature, rows_of(v * v), jnp.zeros((6, PROBES), f32)], axis=0
     )
+    for copy in copies:
+        copy.wait()
 
 
 def leaf_kernel(
-    sizes_ref, residual_ref, first_image_ref, tile_ref, basis_ref, coupling_ref,
-    image_ref, scalars_ref,
+    sizes_ref, residual_ref, first_image_ref, tile_hbm, basis_ref, coupling_ref,
+    image_ref, scalars_ref, tile_ref, sems,
 ):
+    width = POINTS // HALVES
+    copies = []
+    for half in range(HALVES):
+        rows = pl.ds(width * half, width)
+        copies.append(pltpu.make_async_copy(tile_hbm.at[rows], tile_ref.at[rows], sems.at[half]))
+        copies[-1].start()
     v = residual_ref[...]
+    rounded = v.astype(bf16)
+    leaf = None
+    for half in range(HALVES):
+        span = slice(width * half, width * (half + 1))
+        copies[half].wait()
+        part = dot(rounded[:, span], tile_ref[span, :], NN)
+        leaf = part if half == 0 else leaf + part
     image, curvature = leaf_level(
-        v, v.astype(bf16), sizes_ref[0, 0], tile_ref[...], basis_ref, coupling_ref
+        v, rounded, leaf, sizes_ref[0, 0], basis_ref, coupling_ref
     )
     image_ref[...] = image
     scalars_ref[...] = jnp.concatenate(
@@ -272,7 +312,7 @@
         send_ref[BACK * d + 8 : BACK * (d + 1), :] = tail
 
 
-def expand(got_ref, basis_ref, coupling_ref):
+def level_coefficients(got_ref, coupling_ref):
     coefficients = []
     for level in range(1, 10):
         mixed = jnp.concatenate(
@@ -283,8 +323,12 @@
             axis=0,
         )
         coefficients.append(dot_split(coupling_ref[0, level, :RANK, :], mixed, NN))
-    narrow = jnp.concatenate(coefficients, axis=0).astype(bf16)
-    return dot(narrow, basis_ref[1:10].reshape(9 * RANK, POINTS), TN)
+    return jnp.concatenate(coefficients, axis=0).astype(bf16)
+
+
+def expand(coefficients, basis_ref, span):
+    width = span.stop - span.start
+    return dot(coefficients, basis_ref[1:10, :, span].reshape(9 * RANK, width), TN)
 
 
 def turn_kernel(
@@ -294,14 +338,16 @@
     scalars = total(got_ref, PLANE, BACK, 18, 3)
     curvature, norm = scalars[0:1], scalars[1:2]
     step = norm / curvature
-    whole = image_ref[...] + expand(got_ref, basis_ref, coupling_ref)
+    coefficients = level_coefficients(got_ref, coupling_ref)
+    whole = image_ref[...] + expand(coefficients, basis_ref, slice(0, POINTS))
     residual = right_ref[...] - down_rows(step) * whole
     whole_image_ref[...] = whole
     residual_ref[...] = residual
     keep_ref[...] = jnp.concatenate(
         [step, curvature, norm, jnp.zeros((5, PROBES), f32)], axis=0
     )
-    send_levels(residual.astype(bf16), basis_ref, coupling_ref, send_ref)
+    wide = basis_ref[1:10].reshape(9 * RANK, POINTS)
+    send_levels(dot(wide, residual.astype(bf16), NT), coupling_ref, send_ref)
     out = pltpu.make_async_copy(send_ref, send_hbm, sem.at[0])
     out.start()
     out.wait()
@@ -309,7 +355,7 @@
 
 def end_kernel(
     got_ref, right_ref, residual_ref, first_image_ref, image_ref, basis_ref, coupling_ref,
-    keep_ref, solution_ref, last_ref,
+    keep_ref, solution_hbm, last_hbm, solution_ref, last_ref, sems,
 ):
     scalars = total(got_ref, PLANE, BACK, 18, 3)
     own, norm, cross = scalars[0:1], scalars[1:2], scalars[2:3]
@@ -320,8 +366,24 @@
     right, residual = right_ref[...], residual_ref[...]
     direction = residual + ratio_down * right
     solution_ref[...] = down_rows(step) * right + step_down * direction
-    image = image_ref[...] + expand(got_ref, basis_ref, coupling_ref)
-    last_ref[...] = residual - step_down * (image + ratio_down * first_image_ref[...])
+    copies = [pltpu.make_async_copy(solution_ref, solution_hbm, sems.at[HALVES])]
+    copies[0].start()
+    coefficients = level_coefficients(got_ref, coupling_ref)
+    width = POINTS // HALVES
+    for half in range(HALVES):
+        span = slice(width * half, width * (half + 1))
+        image = image_ref[:, span] + expand(coefficients, basis_ref, span)
+        image = image + ratio_down[:, span] * first_image_ref[:, span]
+        last_ref[:, span] = residual[:, span] - step_down[:, span] * image
+        columns = pl.ds(width * half, width)
+        copies.append(
+            pltpu.make_async_copy(
+                last_ref.at[:, columns], last_hbm.at[:, columns], sems.at[half]
+            )
+        )
+        copies[-1].start()
+    for copy in copies:
+        copy.wait()
 
 
 VMEM = pl.BlockSpec(memory_space=pltpu.VMEM)
@@ -335,7 +397,10 @@
         specs[place] = HBM
     return pl.pallas_call(
         body,
-        out_shape=[jax.ShapeDtypeStruct(shape, kind) for shape, kind in outs],
+        out_shape=[
+            (pltpu.HBM if place in far_outs else jax.ShapeDtypeStruct)(shape, kind)
+            for place, (shape, kind) in enumerate(outs)
+        ],
         in_specs=specs,
         out_specs=[HBM if place in far_outs else VMEM for place in range(len(outs))],
         scratch_shapes=list(scratch),
@@ -386,10 +451,10 @@
         1 << 26,
         scratch=[
             pltpu.VMEM(right_side.shape, f32),
-            pltpu.VMEM(level_basis.shape, bf16),
+            pltpu.VMEM((9, RANK, POINTS), bf16),
             pltpu.VMEM(coupling.shape, f32),
             message_scratch,
-            pltpu.SemaphoreType.DMA((4,)),
+            pltpu.SemaphoreType.DMA((2 * HALVES + 2,)),
         ],
         name="start",
         far_ins=(0, 1, 2),
@@ -403,8 +468,13 @@
             [coordinates, tree_order, leaf_sizes, right_side, level_basis, coupling],
             12,
             4 << 30,
-            scratch=[pltpu.VMEM((3, POINTS, 128), f32)],
+            scratch=[
+                pltpu.VMEM((POINTS, POINTS), bf16),
+                pltpu.VMEM((3, POINTS, 128), f32),
+                pltpu.SemaphoreType.DMA((3,)),
+            ],
             name="tile",
+            far_outs=(0,),
         ),
     )
     residual, first_image, send, keep = call(
@@ -425,7 +495,12 @@
             [leaf_sizes, residual, first_image, tile, level_basis, coupling],
             8,
             1 << 30,
+            scratch=[
+                pltpu.VMEM((POINTS, POINTS), bf16),
+                pltpu.SemaphoreType.DMA((HALVES,)),
+            ],
             name="leaf",
+            far_ins=(3,),
         ),
     )
     return tuple(
@@ -435,7 +510,13 @@
             [got, right_side, residual, first_image, image, level_basis, coupling, keep],
             8,
             1 << 28,
+            scratch=[
+                pltpu.VMEM(*field),
+                pltpu.VMEM(*field),
+                pltpu.SemaphoreType.DMA((HALVES + 1,)),
+            ],
             name="end",
+            far_outs=(0, 1),
         )
     )
 

time: 111 us -> 111 us (level)
  local copies, waits for them, and re-layouts: 3.65 us -> 1.61 us
    unnamed x18 -> x14, local copies, waits for them, and re-layouts: 3.65 us -> 1.61 us
where the time goes in v3:
time: 111 us; the launch traced here: 110 us
  blocking collectives  70 us (63%)
  starting transfers between devices  14.3 us (13%)
  Pallas kernels  13.5 us (12%)
  waiting for transfers between devices  9.84 us (9%)
  local copies, waits for them, and re-layouts  1.61 us (1%)
    all_to_all x4, blocking collectives, exchange(): got = lax.all_to_all(blocks, 'pts', 0, 0, axis_index_groups=groups)  70 us
    all_to_all x2, starting transfers between devices, exchange(): got = lax.all_to_all(blocks, 'pts', 0, 0, axis_index_groups=groups)  14.3 us
    pallas_call x9, Pallas kernels, call(): pl.pallas_call(body, out_shape=[(pltpu.HBM if place in far_outs else jax....  13.5 us
    all_to_all x2, waiting for transfers between devices, exchange(): got = lax.all_to_all(blocks, 'pts', 0, 0, axis_index_groups=groups)  9.84 us
  transfers between devices with their start and end apart: 2, of which 2 were waited for; matrix products, arithmetic and copies ran while one was open for 0% of the time, Pallas kernels for 6%

profile of v3, /device:TPU:1, one launch (start us, length us, event | category | flops | bytes accessed | tf_op | source)
XLA Modules:
  0.0 110.1 jit_solution(9674659913849253880)
XLA Ops:
  0.6 0.0 copy-start.1
  0.6 0.0 copy-start
  0.7 0.0 copy-start.2
  0.7 0.0 copy-start.4
  0.7 0.0 copy-start.6
  0.7 0.0 copy-start.5
  0.7 2.7 %start.1 = f32[576,128]{1,0:T(8,128)} custom-call(f32[128,1024]{1,0:T(8,128)} %right_ref.5, bf16[10,32,1024]{2,1,0:T(8,128)(2,1)} %basis_ref.7, f32[1,10,64,64]{3,2,1,0:T(8,128)} %coupling_ref.7), custom_call_target="tpu_custom_call" | custom-call | flops 67108864 | bytes 2097152 | tf_op jit(solution)/shard_map/start/pallas_call | solution.py:398
  3.4 10.4 %all-to-all-start = ((f32[32,1,2304]{2,1,0:T(1,128)}), f32[32,1,2304]{2,1,0:T(1,128)S(1)}, u32[]{:S(2)}, u32[]{:S(2)}) async-start(f32[32,1,2304]{2,1,0:T(1,128)} %bitcast.24), calls=%async_computation | async-start | bytes 589824 | tf_op jit(solution)/shard_map/all_to_all | solution.py:424
  13.8 0.0 copy-done.1
  13.9 0.0 copy-done
  13.9 0.0 copy-done.2
  13.9 0.0 copy-done.4
  13.9 0.0 copy-done.6
  13.9 0.0 copy-done.5
  13.9 5.2 %tile.1 = (bf16[1024,1024]{1,0:T(8,128)(2,1)}, f32[128,1024]{1,0:T(8,128)S(1)}, f32[8,128]{1,0:T(8,128)S(1)}) custom-call(f32[3,1024]{1,0:T(4,128)S(1)} %copy-done.5, s32[1,1024]{1,0:T(1,128)S(1)} %copy-done.6, s32[1,2]{1,0:T(1,128)S(1)} %copy-done.4, f32[128,1024]{1,0:T(8,128)S(1)} %copy-done.2, bf16[10,32,1024]{2,1,0:T(8,128)(2,1)S(1)} %copy-done, ...), custom_call_target="tpu_custom_call" | custom-call | flops 4294967296 | bytes 2097152 | tf_op jit(solution)/shard_map/tile/pallas_call | solution.py:398
  19.1 4.1 %all-to-all-done = f32[32,1,2304]{2,1,0:T(1,128)S(1)} async-done(((f32[32,1,2304]{2,1,0:T(1,128)}), f32[32,1,2304]{2,1,0:T(1,128)S(1)}, u32[]{:S(2)}, u32[]{:S(2)}) %all-to-all-start) | async-done | bytes 294944 | tf_op jit(solution)/shard_map/all_to_all | solution.py:424
  23.2 24.6 %all_to_all.30 = f32[16,1,1408]{2,1,0:T(1,128)S(1)} all-to-all(f32[16,1,1408]{2,1,0:T(1,128)S(1)} %bitcast.22), channel_id=1, replica_groups={{0,32,64,96,128,160,192,224,256,288,320,352,384,416,448,480},{1,33,65,9..., dimensions={0} | all-to-all | bytes 180224 | tf_op jit(solution)/shard_map/all_to_all | solution.py:424
  47.8 0.1 depth.2
  47.9 15.2 %all_to_all.31 = f32[32,1,2688]{2,1,0:T(1,128)S(1)} all-to-all(f32[32,1,2688]{2,1,0:T(1,128)S(1)} %bitcast.17), channel_id=1, replica_groups={{0,1,2,3,4,5,6,7,8,9,10,11,12,13,14,15,16,17,18,19,20,21,22,23,24,25,26..., dimensions={0} | all-to-all | bytes 688128 | tf_op jit(solution)/shard_map/all_to_all | solution.py:424
  63.0 1.8 %turn.1 = (f32[128,1024]{1,0:T(8,128)S(1)}, f32[128,1024]{1,0:T(8,128)S(1)}, f32[576,128]{1,0:T(8,128)}, f32[8,128]{1,0:T(8,128)S(1)}) custom-call(f32[672,128]{1,0:T(8,128)S(1)} %bitcast.16, f32[128,1024]{1,0:T(8,128)S(1)} %copy-done.2, f32[128,1024]{1,0:T(8,128)S(1)} %get-tuple-element.12.image_ref, bf16[10,32,1024]{2,1,0:T(8,128)(2,1)S(1)} %copy-done, ...), custom_call_target="tpu_custom_call" | custom-call | flops 268435456 | bytes 2097152 | tf_op jit(solution)/shard_map/turn/pallas_call | solution.py:398
  64.9 3.9 %all-to-all-start.3 = ((f32[32,1,2304]{2,1,0:T(1,128)}), f32[32,1,2304]{2,1,0:T(1,128)S(1)}, u32[]{:S(2)}, u32[]{:S(2)}) async-start(f32[32,1,2304]{2,1,0:T(1,128)} %bitcast.25), calls=%async_computation.3 | async-start | bytes 589824 | tf_op jit(solution)/shard_map/all_to_all | solution.py:424
  68.8 0.0 copy-start.3
  68.8 1.6 %copy-done.3 = bf16[1024,1024]{1,0:T(8,128)(2,1)S(1)} copy-done((bf16[1024,1024]{1,0:T(8,128)(2,1)S(1)}, bf16[1024,1024]{1,0:T(8,128)(2,1)}, u32[]{:S(2)}) %copy-start.3) | copy-done | bytes 2097176
  70.3 2.0 %leaf.1 = (f32[128,1024]{1,0:T(8,128)S(1)}, f32[8,128]{1,0:T(8,128)S(1)}) custom-call(s32[1,2]{1,0:T(1,128)S(1)} %copy-done.4, f32[128,1024]{1,0:T(8,128)S(1)} %get-tuple-element.14.residual_ref, f32[128,1024]{1,0:T(8,128)S(1)} %get-tuple-element.15.first_image_ref, bf16[1024,1024]{1,0:T(8,128)(2,1)S(1)} %copy-done.3, bf16[10,32,1024]{2,1,0:T(8,128)(2,1)S(1)} %copy-done, ...), custom_call_target="tpu_custom_call" | custom-call | flops 1073741824 | bytes 2097152 | tf_op jit(solution)/shard_map/leaf/pallas_call | solution.py:398
  72.3 5.8 %all-to-all-done.3 = f32[32,1,2304]{2,1,0:T(1,128)S(1)} async-done(((f32[32,1,2304]{2,1,0:T(1,128)}), f32[32,1,2304]{2,1,0:T(1,128)S(1)}, u32[]{:S(2)}, u32[]{:S(2)}) %all-to-all-start.3) | async-done | bytes 294944 | tf_op jit(solution)/shard_map/all_to_all | solution.py:424
  78.1 15.1 %all_to_all.32 = f32[16,1,1408]{2,1,0:T(1,128)S(1)} all-to-all(f32[16,1,1408]{2,1,0:T(1,128)S(1)} %bitcast.23), channel_id=1, replica_groups={{0,32,64,96,128,160,192,224,256,288,320,352,384,416,448,480},{1,33,65,9..., dimensions={0} | all-to-all | bytes 180224 | tf_op jit(solution)/shard_map/all_to_all | solution.py:424
  93.2 0.1 depth.3
  93.2 15.2 %all_to_all.33 = f32[32,1,2688]{2,1,0:T(1,128)S(1)} all-to-all(f32[32,1,2688]{2,1,0:T(1,128)S(1)} %bitcast.18), channel_id=1, replica_groups={{0,1,2,3,4,5,6,7,8,9,10,11,12,13,14,15,16,17,18,19,20,21,22,23,24,25,26..., dimensions={0} | all-to-all | bytes 688128 | tf_op jit(solution)/shard_map/all_to_all | solution.py:424
  108.4 1.6 %end.1 = (f32[128,1024]{1,0:T(8,128)}, f32[128,1024]{1,0:T(8,128)}) custom-call(f32[672,128]{1,0:T(8,128)S(1)} %bitcast.19, f32[128,1024]{1,0:T(8,128)S(1)} %copy-done.2, f32[128,1024]{1,0:T(8,128)S(1)} %get-tuple-element.14.residual_ref, f32[128,1024]{1,0:T(8,128)S(1)} %get-tuple-element.15.first_image_ref, f32[128,1024]{1,0:T(8,128)S(1)} %get-tuple-element.18.image_ref, ...), custom_call_target="tpu_custom_call" | custom-call | flops 268435456 | bytes 2097152 | tf_op jit(solution)/shard_map/end/pallas_call | solution.py:398
  (2 shorter events, 0.1 us)
Async XLA Ops:
  0.6 13.2 %copy-start.1 = (f32[1,10,64,64]{3,2,1,0:T(8,128)S(1)}, f32[1,10,64,64]{3,2,1,0:T(8,128)}, u32[]{:S(2)}) copy-start(f32[1,10,64,64]{3,2,1,0:T(8,128)} %coupling_ref.7) | copy-start | bytes 491524
  0.6 13.2 %copy-start = (bf16[10,32,1024]{2,1,0:T(8,128)(2,1)S(1)}, bf16[10,32,1024]{2,1,0:T(8,128)(2,1)}, u32[]{:S(2)}) copy-start(bf16[10,32,1024]{2,1,0:T(8,128)(2,1)} %basis_ref.7) | copy-start | bytes 1966084
  0.7 13.2 %copy-start.2 = (f32[128,1024]{1,0:T(8,128)S(1)}, f32[128,1024]{1,0:T(8,128)}, u32[]{:S(2)}) copy-start(f32[128,1024]{1,0:T(8,128)} %right_ref.5) | copy-start | bytes 1572868
  0.7 13.2 %copy-start.4 = (s32[1,2]{1,0:T(1,128)S(1)}, s32[1,2]{1,0:T(1,128)}, u32[]{:S(2)}) copy-start(s32[1,2]{1,0:T(1,128)} %sizes_ref.3) | copy-start | bytes 28
  0.7 13.2 %copy-start.6 = (s32[1,1024]{1,0:T(1,128)S(1)}, s32[1,1024]{1,0:T(1,128)}, u32[]{:S(2)}) copy-start(s32[1,1024]{1,0:T(1,128)} %order_ref.1) | copy-start | bytes 12292
  0.7 13.2 %copy-start.5 = (f32[3,1024]{1,0:T(4,128)S(1)}, f32[3,1024]{1,0:T(4,128)}, u32[]{:S(2)}) copy-start(f32[3,1024]{1,0:T(4,128)} %coordinates_ref.1) | copy-start | bytes 36868
  3.4 19.8 %all-to-all-start = ((f32[32,1,2304]{2,1,0:T(1,128)}), f32[32,1,2304]{2,1,0:T(1,128)S(1)}, u32[]{:S(2)}, u32[]{:S(2)}) async-start(f32[32,1,2304]{2,1,0:T(1,128)} %bitcast.24), calls=%async_computation | async-start | bytes 589824 | tf_op jit(solution)/shard_map/all_to_all | solution.py:424
  64.9 13.2 %all-to-all-start.3 = ((f32[32,1,2304]{2,1,0:T(1,128)}), f32[32,1,2304]{2,1,0:T(1,128)S(1)}, u32[]{:S(2)}, u32[]{:S(2)}) async-start(f32[32,1,2304]{2,1,0:T(1,128)} %bitcast.25), calls=%async_computation.3 | async-start | bytes 589824 | tf_op jit(solution)/shard_map/all_to_all | solution.py:424
  68.8 1.6 %copy-start.3 = (bf16[1024,1024]{1,0:T(8,128)(2,1)S(1)}, bf16[1024,1024]{1,0:T(8,128)(2,1)}, u32[]{:S(2)}) copy-start(bf16[1024,1024]{1,0:T(8,128)(2,1)} %get-tuple-element.16.tile_hbm) | copy-start | bytes 6291460

commit v4 on v3

--- a/solution.py
+++ b/solution.py
@@ -19,8 +19,7 @@
 PLANE = 32
 DEPTH = 16
 ROWS = 18
-BACK = 21
-Z_ROWS = 11
+Z_ROWS = 8
 LEAST = 384
 MOST = 640
 HALVES = 2
@@ -206,44 +205,10 @@
     leaf = dot(rounded, tile_ref[...], NN)
     image, curvature = leaf_level(v, rounded, leaf, boundary, basis_ref, coupling_ref)
     image_ref[...] = image
-    scalars_ref[...] = jnp.concatenate(
-        [curvature, rows_of(v * v), jnp.zeros((6, PROBES), f32)], axis=0
-    )
+    scalars_ref[0:1, :] = curvature
+    scalars_ref[1:2, :] = rows_of(v * v)
     for copy in copies:
         copy.wait()
-
-
-def leaf_kernel(
-    sizes_ref, residual_ref, first_image_ref, tile_hbm, basis_ref, coupling_ref,
-    image_ref, scalars_ref, tile_ref, sems,
-):
-    width = POINTS // HALVES
-    copies = []
-    for half in range(HALVES):
-        rows = pl.ds(width * half, width)
-        copies.append(pltpu.make_async_copy(tile_hbm.at[rows], tile_ref.at[rows], sems.at[half]))
-        copies[-1].start()
-    v = residual_ref[...]
-    rounded = v.astype(bf16)
-    leaf = None
-    for half in range(HALVES):
-        span = slice(width * half, width * (half + 1))
-        copies[half].wait()
-        part = dot(rounded[:, span], tile_ref[span, :], NN)
-        leaf = part if half == 0 else leaf + part
-    image, curvature = leaf_level(
-        v, rounded, leaf, sizes_ref[0, 0], basis_ref, coupling_ref
-    )
-    image_ref[...] = image
-    scalars_ref[...] = jnp.concatenate(
-        [
-            curvature,
-            rows_of(v * v),
-            rows_of(v * first_image_ref[...]),
-            jnp.zeros((5, PROBES), f32),
-        ],
-        axis=0,
-    )
 
 
 def pair_sums(got_ref):
@@ -268,7 +233,7 @@
     return result
 
 
-def plane_kernel(got_ref, scalars_ref, send_ref):
+def plane_kernel(count, got_ref, scalars_ref, send_ref):
     ids = row_ids(8)
     sums = pair_sums(got_ref)
     square = jnp.zeros((8, PROBES), f32)
@@ -278,20 +243,22 @@
     curvature = jnp.sum(square, axis=0, keepdims=True) + jnp.sum(
         fifth * fifth, axis=0, keepdims=True
     )
-    scalars = scalars_ref[0:3, :] + jnp.where(row_ids(3) == 0, curvature, 0.0)
+    scalars = scalars_ref[...] + jnp.where(row_ids(count) == 0, curvature, 0.0)
     block = jnp.concatenate([total(got_ref, PLANE, ROWS, 8, 8), scalars], axis=0)
+    stride = Z_ROWS + count
     for z in range(DEPTH):
-        send_ref[Z_ROWS * z : Z_ROWS * (z + 1), :] = block
-
-
-def depth_kernel(got_ref, z_got_ref, send_ref):
+        send_ref[stride * z : stride * (z + 1), :] = block
+
+
+def depth_kernel(count, got_ref, z_got_ref, send_ref):
+    z_stride, stride = Z_ROWS + count, ROWS + count
     own = lax.axis_index("pts") // PLANE
     ids = row_ids(8)
     reach = jnp.left_shift(2, ids // 2)
     pair = jnp.zeros((8, PROBES), f32)
     nodes = []
     for z in range(DEPTH):
-        block = z_got_ref[Z_ROWS * z : Z_ROWS * z + 8, :]
+        block = z_got_ref[z_stride * z : z_stride * z + 8, :]
         nodes.append(block)
         apart = jnp.bitwise_xor(own, z)
         pair = pair + jnp.where(apart < reach, block, 0.0)
@@ -300,24 +267,24 @@
         nodes = [nodes[2 * i] + nodes[2 * i + 1] for i in range(len(nodes) // 2)]
         square = jnp.where(ids // 2 == level, squares(nodes), square)
     curvature = jnp.sum(square, axis=0, keepdims=True)
-    scalars = total(z_got_ref, DEPTH, Z_ROWS, 8, 3)
-    scalars = scalars + jnp.where(row_ids(3) == 0, curvature, 0.0)
+    scalars = total(z_got_ref, DEPTH, z_stride, 8, count)
+    scalars = scalars + jnp.where(row_ids(count) == 0, curvature, 0.0)
     tail = jnp.concatenate([pair, total(got_ref, PLANE, ROWS, 16, 2), scalars], axis=0)
     sums = pair_sums(got_ref)
     for d in range(PLANE):
         first = sums[4][d >> 4]
         for level in (3, 2, 1):
             first = jnp.where(ids // 2 == level - 1, sums[level][d >> level], first)
-        send_ref[BACK * d : BACK * d + 8, :] = first
-        send_ref[BACK * d + 8 : BACK * (d + 1), :] = tail
-
-
-def level_coefficients(got_ref, coupling_ref):
+        send_ref[stride * d : stride * d + 8, :] = first
+        send_ref[stride * d + 8 : stride * (d + 1), :] = tail
+
+
+def level_coefficients(got_ref, coupling_ref, stride):
     coefficients = []
     for level in range(1, 10):
         mixed = jnp.concatenate(
             [
-                got_ref[pl.ds(first_row(level) + half, PLANE, stride=BACK), :]
+                got_ref[pl.ds(first_row(level) + half, PLANE, stride=stride), :]
                 for half in range(2)
             ],
             axis=0,
@@ -332,32 +299,36 @@
 
 
 def turn_kernel(
-    got_ref, right_ref, image_ref, basis_ref, coupling_ref,
-    residual_ref, whole_image_ref, send_hbm, keep_ref, send_ref, sem,
+    sizes_ref, got_ref, right_ref, image_ref, tile_ref, basis_ref, coupling_ref,
+    residual_ref, whole_image_ref, next_image_ref, scalars_ref, send_ref, keep_ref,
 ):
-    scalars = total(got_ref, PLANE, BACK, 18, 3)
+    scalars = total(got_ref, PLANE, ROWS + 2, ROWS, 2)
     curvature, norm = scalars[0:1], scalars[1:2]
     step = norm / curvature
-    coefficients = level_coefficients(got_ref, coupling_ref)
+    coefficients = level_coefficients(got_ref, coupling_ref, ROWS + 2)
     whole = image_ref[...] + expand(coefficients, basis_ref, slice(0, POINTS))
     residual = right_ref[...] - down_rows(step) * whole
     whole_image_ref[...] = whole
     residual_ref[...] = residual
-    keep_ref[...] = jnp.concatenate(
-        [step, curvature, norm, jnp.zeros((5, PROBES), f32)], axis=0
-    )
+    keep_ref[0:1, :] = step
+    keep_ref[1:2, :] = curvature
+    keep_ref[2:3, :] = norm
+    rounded = residual.astype(bf16)
     wide = basis_ref[1:10].reshape(9 * RANK, POINTS)
-    send_levels(dot(wide, residual.astype(bf16), NT), coupling_ref, send_ref)
-    out = pltpu.make_async_copy(send_ref, send_hbm, sem.at[0])
-    out.start()
-    out.wait()
+    send_levels(dot(wide, rounded, NT), coupling_ref, send_ref)
+    leaf = dot(rounded, tile_ref[...], NN)
+    image, own = leaf_level(residual, rounded, leaf, sizes_ref[0, 0], basis_ref, coupling_ref)
+    next_image_ref[...] = image
+    scalars_ref[0:1, :] = own
+    scalars_ref[1:2, :] = rows_of(residual * residual)
+    scalars_ref[2:3, :] = rows_of(residual * whole)
 
 
 def end_kernel(
     got_ref, right_ref, residual_ref, first_image_ref, image_ref, basis_ref, coupling_ref,
     keep_ref, solution_hbm, last_hbm, solution_ref, last_ref, sems,
 ):
-    scalars = total(got_ref, PLANE, BACK, 18, 3)
+    scalars = total(got_ref, PLANE, ROWS + 3, ROWS, 3)
     own, norm, cross = scalars[0:1], scalars[1:2], scalars[2:3]
     step, curvature, norm_before = keep_ref[0:1, :], keep_ref[1:2, :], keep_ref[2:3, :]
     ratio = norm / norm_before
@@ -368,7 +339,7 @@
     solution_ref[...] = down_rows(step) * right + step_down * direction
     copies = [pltpu.make_async_copy(solution_ref, solution_hbm, sems.at[HALVES])]
     copies[0].start()
-    coefficients = level_coefficients(got_ref, coupling_ref)
+    coefficients = level_coefficients(got_ref, coupling_ref, ROWS + 3)
     width = POINTS // HALVES
     for half in range(HALVES):
         span = slice(width * half, width * (half + 1))
@@ -430,17 +401,31 @@
     planes, depths = plane_groups(count), depth_groups(count)
     field = ((PROBES, POINTS), f32)
     message = ((PLANE * ROWS, PROBES), f32)
-    back_message = ((PLANE * BACK, PROBES), f32)
-    z_message = ((DEPTH * Z_ROWS, PROBES), f32)
-    row_block = ((8, PROBES), f32)
     message_scratch = pltpu.VMEM(*message)
 
-    def tree(send, scalars_of):
+    def scalar_rows(rows):
+        return ((rows, PROBES), f32)
+
+    def tree(send, scalars_of, rows):
         got = exchange(send, planes)
         local = scalars_of()
-        (z_send,) = call(plane_kernel, [z_message], [got, local[-1]], 2, 1 << 20, name="plane")
+        (z_send,) = call(
+            functools.partial(plane_kernel, rows),
+            [((DEPTH * (Z_ROWS + rows), PROBES), f32)],
+            [got, local[-1]],
+            2,
+            1 << 20,
+            name="plane",
+        )
         z_got = exchange(z_send, depths)
-        (back,) = call(depth_kernel, [back_message], [got, z_got], 2, 1 << 20, name="depth")
+        (back,) = call(
+            functools.partial(depth_kernel, rows),
+            [((PLANE * (ROWS + rows), PROBES), f32)],
+            [got, z_got],
+            2,
+            1 << 20,
+            name="depth",
+        )
         return local, exchange(back, planes)
 
     (send,) = call(
@@ -464,7 +449,7 @@
         send,
         lambda: call(
             tile_kernel,
-            [((POINTS, POINTS), bf16), field, row_block],
+            [((POINTS, POINTS), bf16), field, scalar_rows(2)],
             [coordinates, tree_order, leaf_sizes, right_side, level_basis, coupling],
             12,
             4 << 30,
@@ -476,33 +461,17 @@
             name="tile",
             far_outs=(0,),
         ),
-    )
-    residual, first_image, send, keep = call(
+        2,
+    )
+    residual, first_image, image, scalars, send, keep = call(
         turn_kernel,
-        [field, field, message, row_block],
-        [got, right_side, image, level_basis, coupling],
+        [field, field, field, scalar_rows(3), message, scalar_rows(3)],
+        [leaf_sizes, got, right_side, image, tile, level_basis, coupling],
         8,
         1 << 28,
-        scratch=[message_scratch, pltpu.SemaphoreType.DMA((1,))],
         name="turn",
-        far_outs=(2,),
-    )
-    (image, _), got = tree(
-        send,
-        lambda: call(
-            leaf_kernel,
-            [field, row_block],
-            [leaf_sizes, residual, first_image, tile, level_basis, coupling],
-            8,
-            1 << 30,
-            scratch=[
-                pltpu.VMEM((POINTS, POINTS), bf16),
-                pltpu.SemaphoreType.DMA((HALVES,)),
-            ],
-            name="leaf",
-            far_ins=(3,),
-        ),
-    )
+    )
+    _, got = tree(send, lambda: (scalars,), 3)
     return tuple(
         call(
             end_kernel,

time: 111 us -> 112 us (level)
  blocking collectives: 70 us -> 82.3 us
  waiting for transfers between devices: 9.84 us -> 3.95 us
  starting transfers between devices: 14.3 us -> 10.4 us
    all_to_all x4 -> x5, blocking collectives: 70 us -> 82.3 us  [exchange(): got = lax.all_to_all(blocks, 'pts', 0, 0, axis_index_groups=groups)]
    all_to_all x2 -> x1, waiting for transfers between devices: 9.84 us -> 3.95 us  [exchange(): got = lax.all_to_all(blocks, 'pts', 0, 0, axis_index_groups=groups)]
    all_to_all x2 -> x1, starting transfers between devices: 14.3 us -> 10.4 us  [exchange(): got = lax.all_to_all(blocks, 'pts', 0, 0, axis_index_groups=groups)]
    pallas_call x9 -> x8, Pallas kernels: 13.5 us -> 12.4 us  [call(): pl.pallas_call(body, out_shape=[(pltpu.HBM if place in far_outs else jax....]
  transfers between devices with their start and end apart: 2 -> 1, of which waited for: 2 -> 1; matrix products, arithmetic and copies ran while one was open for 0% -> 0% of each run, Pallas kernels for 6% -> 5%
where the time goes in v4:
time: 112 us; the launch traced here: 111 us
  blocking collectives  82.3 us (73%)
  Pallas kernels  12.4 us (11%)
  starting transfers between devices  10.4 us (9%)
  waiting for transfers between devices  3.95 us (4%)
  local copies, waits for them, and re-layouts  1.62 us (1%)
    all_to_all x5, blocking collectives, exchange(): got = lax.all_to_all(blocks, 'pts', 0, 0, axis_index_groups=groups)  82.3 us
    pallas_call x8, Pallas kernels, call(): pl.pallas_call(body, out_shape=[(pltpu.HBM if place in far_outs else jax....  12.4 us
    all_to_all x1, starting transfers between devices, exchange(): got = lax.all_to_all(blocks, 'pts', 0, 0, axis_index_groups=groups)  10.4 us
    all_to_all x1, waiting for transfers between devices, exchange(): got = lax.all_to_all(blocks, 'pts', 0, 0, axis_index_groups=groups)  3.95 us
  transfers between devices with their start and end apart: 1, of which 1 were waited for; matrix products, arithmetic and copies ran while one was open for 0% of the time, Pallas kernels for 5%

profile of v4, /device:TPU:1, one launch (start us, length us, event | category | flops | bytes accessed | tf_op | source)
XLA Modules:
  0.0 111.4 jit_solution(14362341206976740676)
XLA Ops:
  0.6 0.0 copy-start.2
  0.6 0.0 copy-start
  0.7 0.0 copy-start.1
  0.7 0.0 copy-start.4
  0.7 0.0 copy-start.6
  0.7 0.0 copy-start.5
  0.7 2.7 %start.1 = f32[576,128]{1,0:T(8,128)} custom-call(f32[128,1024]{1,0:T(8,128)} %right_ref.5, bf16[10,32,1024]{2,1,0:T(8,128)(2,1)} %basis_ref.5, f32[1,10,64,64]{3,2,1,0:T(8,128)} %coupling_ref.5), custom_call_target="tpu_custom_call" | custom-call | flops 67108864 | bytes 2097152 | tf_op jit(solution)/shard_map/start/pallas_call | solution.py:369
  3.4 10.4 %all-to-all-start = ((f32[32,1,2304]{2,1,0:T(1,128)}), f32[32,1,2304]{2,1,0:T(1,128)S(1)}, u32[]{:S(2)}, u32[]{:S(2)}) async-start(f32[32,1,2304]{2,1,0:T(1,128)} %bitcast.25), calls=%async_computation | async-start | bytes 589824 | tf_op jit(solution)/shard_map/all_to_all | solution.py:395
  13.8 0.0 copy-done.2
  13.9 0.0 copy-done
  13.9 0.0 copy-done.1
  13.9 0.0 copy-done.4
  13.9 0.0 copy-done.6
  13.9 0.0 copy-done.5
  13.9 5.3 %tile.1 = (bf16[1024,1024]{1,0:T(8,128)(2,1)}, f32[128,1024]{1,0:T(8,128)S(1)}, f32[2,128]{1,0:T(2,128)S(1)}) custom-call(f32[3,1024]{1,0:T(4,128)S(1)} %copy-done.5, s32[1,1024]{1,0:T(1,128)S(1)} %copy-done.6, s32[1,2]{1,0:T(1,128)S(1)} %copy-done.4, f32[128,1024]{1,0:T(8,128)S(1)} %copy-done.1, bf16[10,32,1024]{2,1,0:T(8,128)(2,1)S(1)} %copy-done, ...), custom_call_target="tpu_custom_call" | custom-call | flops 4294967296 | bytes 2097152 | tf_op jit(solution)/shard_map/tile/pallas_call | solution.py:369
  19.2 3.9 %all-to-all-done = f32[32,1,2304]{2,1,0:T(1,128)S(1)} async-done(((f32[32,1,2304]{2,1,0:T(1,128)}), f32[32,1,2304]{2,1,0:T(1,128)S(1)}, u32[]{:S(2)}, u32[]{:S(2)}) %all-to-all-start) | async-done | bytes 294944 | tf_op jit(solution)/shard_map/all_to_all | solution.py:395
  23.2 24.6 %all_to_all.30 = f32[16,1,1280]{2,1,0:T(1,128)S(1)} all-to-all(f32[16,1,1280]{2,1,0:T(1,128)S(1)} %bitcast.22), channel_id=1, replica_groups={{0,32,64,96,128,160,192,224,256,288,320,352,384,416,448,480},{1,33,65,9..., dimensions={0} | all-to-all | bytes 163840 | tf_op jit(solution)/shard_map/all_to_all | solution.py:395
  47.8 0.1 depth.2
  47.9 14.7 %all_to_all.31 = f32[32,1,2560]{2,1,0:T(1,128)S(1)} all-to-all(f32[32,1,2560]{2,1,0:T(1,128)S(1)} %bitcast.19), channel_id=1, replica_groups={{0,1,2,3,4,5,6,7,8,9,10,11,12,13,14,15,16,17,18,19,20,21,22,23,24,25,26..., dimensions={0} | all-to-all | bytes 655360 | tf_op jit(solution)/shard_map/all_to_all | solution.py:395
  62.6 0.0 copy-start.3
  62.6 1.6 %copy-done.3 = bf16[1024,1024]{1,0:T(8,128)(2,1)S(1)} copy-done((bf16[1024,1024]{1,0:T(8,128)(2,1)S(1)}, bf16[1024,1024]{1,0:T(8,128)(2,1)}, u32[]{:S(2)}) %copy-start.3) | copy-done | bytes 2097176
  64.2 2.6 %turn.1 = (f32[128,1024]{1,0:T(8,128)S(1)}, f32[128,1024]{1,0:T(8,128)S(1)}, f32[128,1024]{1,0:T(8,128)S(1)}, f32[3,128]{1,0:T(4,128)S(1)}, f32[576,128]{1,0:T(8,128)S(1)}, /*index=5*/f32[3,128]{1,0:T(4,128)S(1)}) custom-call(s32[1,2]{1,0:T(1,128)S(1)} %copy-done.4, f32[640,128]{1,0:T(8,128)S(1)} %bitcast.18, f32[128,1024]{1,0:T(8,128)S(1)} %copy-done.1, ...), custom_call_target="tpu_custom_call" | custom-call | flops 268435456 | bytes 2097152 | tf_op jit(solution)/shard_map/turn/pallas_call | solution.py:369
  66.7 12.8 %all_to_all.32 = f32[32,1,2304]{2,1,0:T(1,128)S(1)} all-to-all(f32[32,1,2304]{2,1,0:T(1,128)S(1)} %bitcast.24), channel_id=1, replica_groups={{0,1,2,3,4,5,6,7,8,9,10,11,12,13,14,15,16,17,18,19,20,21,22,23,24,25,26..., dimensions={0} | all-to-all | bytes 589824 | tf_op jit(solution)/shard_map/all_to_all | solution.py:395
  79.5 15.0 %all_to_all.33 = f32[16,1,1408]{2,1,0:T(1,128)S(1)} all-to-all(f32[16,1,1408]{2,1,0:T(1,128)S(1)} %bitcast.21), channel_id=1, replica_groups={{0,32,64,96,128,160,192,224,256,288,320,352,384,416,448,480},{1,33,65,9..., dimensions={0} | all-to-all | bytes 180224 | tf_op jit(solution)/shard_map/all_to_all | solution.py:395
  94.5 0.1 depth.3
  94.6 15.2 %all_to_all.34 = f32[32,1,2688]{2,1,0:T(1,128)S(1)} all-to-all(f32[32,1,2688]{2,1,0:T(1,128)S(1)} %bitcast.17), channel_id=1, replica_groups={{0,1,2,3,4,5,6,7,8,9,10,11,12,13,14,15,16,17,18,19,20,21,22,23,24,25,26..., dimensions={0} | all-to-all | bytes 688128 | tf_op jit(solution)/shard_map/all_to_all | solution.py:395
  109.8 1.6 %end.1 = (f32[128,1024]{1,0:T(8,128)}, f32[128,1024]{1,0:T(8,128)}) custom-call(f32[672,128]{1,0:T(8,128)S(1)} %bitcast.16, f32[128,1024]{1,0:T(8,128)S(1)} %copy-done.1, f32[128,1024]{1,0:T(8,128)S(1)} %get-tuple-element.16.residual_ref, f32[128,1024]{1,0:T(8,128)S(1)} %get-tuple-element.17.first_image_ref, f32[128,1024]{1,0:T(8,128)S(1)} %get-tuple-element.18.image_ref, ...), custom_call_target="tpu_custom_call" | custom-call | flops 268435456 | bytes 2097152 | tf_op jit(solution)/shard_map/end/pallas_call | solution.py:369
  (2 shorter events, 0.1 us)
Async XLA Ops:
  0.6 13.2 %copy-start.2 = (f32[1,10,64,64]{3,2,1,0:T(8,128)S(1)}, f32[1,10,64,64]{3,2,1,0:T(8,128)}, u32[]{:S(2)}) copy-start(f32[1,10,64,64]{3,2,1,0:T(8,128)} %coupling_ref.5) | copy-start | bytes 491524
  0.6 13.2 %copy-start = (bf16[10,32,1024]{2,1,0:T(8,128)(2,1)S(1)}, bf16[10,32,1024]{2,1,0:T(8,128)(2,1)}, u32[]{:S(2)}) copy-start(bf16[10,32,1024]{2,1,0:T(8,128)(2,1)} %basis_ref.5) | copy-start | bytes 1966084
  0.7 13.2 %copy-start.1 = (f32[128,1024]{1,0:T(8,128)S(1)}, f32[128,1024]{1,0:T(8,128)}, u32[]{:S(2)}) copy-start(f32[128,1024]{1,0:T(8,128)} %right_ref.5) | copy-start | bytes 1572868
  0.7 13.2 %copy-start.4 = (s32[1,2]{1,0:T(1,128)S(1)}, s32[1,2]{1,0:T(1,128)}, u32[]{:S(2)}) copy-start(s32[1,2]{1,0:T(1,128)} %sizes_ref.3) | copy-start | bytes 28
  0.7 13.2 %copy-start.6 = (s32[1,1024]{1,0:T(1,128)S(1)}, s32[1,1024]{1,0:T(1,128)}, u32[]{:S(2)}) copy-start(s32[1,1024]{1,0:T(1,128)} %order_ref.1) | copy-start | bytes 12292
  0.7 13.2 %copy-start.5 = (f32[3,1024]{1,0:T(4,128)S(1)}, f32[3,1024]{1,0:T(4,128)}, u32[]{:S(2)}) copy-start(f32[3,1024]{1,0:T(4,128)} %coordinates_ref.1) | copy-start | bytes 36868
  3.4 19.8 %all-to-all-start = ((f32[32,1,2304]{2,1,0:T(1,128)}), f32[32,1,2304]{2,1,0:T(1,128)S(1)}, u32[]{:S(2)}, u32[]{:S(2)}) async-start(f32[32,1,2304]{2,1,0:T(1,128)} %bitcast.25), calls=%async_computation | async-start | bytes 589824 | tf_op jit(solution)/shard_map/all_to_all | solution.py:395
  62.6 1.6 %copy-start.3 = (bf16[1024,1024]{1,0:T(8,128)(2,1)S(1)}, bf16[1024,1024]{1,0:T(8,128)(2,1)}, u32[]{:S(2)}) copy-start(bf16[1024,1024]{1,0:T(8,128)(2,1)} %get-tuple-element.13.tile_ref) | copy-start | bytes 6291460

commit v5 on v4

--- a/solution.py
+++ b/solution.py
@@ -53,6 +53,11 @@
         jnp.concatenate([b_high, b_low, b_high], axis=b_dim),
         dims,
     )
+
+
+def project_split(wide, v):
+    high, low = halves(v)
+    return dot(wide, high, NT) + dot(wide, low, NT)
 
 
 def rows_of(products):
@@ -136,7 +141,8 @@
 
 def tile_kernel(
     coordinates_ref, order_ref, sizes_ref, right_ref, basis_ref, coupling_ref,
-    tile_hbm, image_ref, scalars_ref, tile_ref, down_ref, sems,
+    tile_hbm, image_ref, parts_ref, scalars_ref,
+    tile_ref, down_ref, sems,
 ):
     boundary = sizes_ref[0, 0]
     order = order_ref[...]
@@ -207,8 +213,39 @@
     image_ref[...] = image
     scalars_ref[0:1, :] = curvature
     scalars_ref[1:2, :] = rows_of(v * v)
+    wide = basis_ref[1:10].reshape(9 * RANK, POINTS)
+    parts_ref[:, :PROBES] = project_split(wide, v)
+    parts_ref[:, PROBES : 2 * PROBES] = project_split(wide, image)
+    parts_ref[:, 2 * PROBES :] = dot(wide, wide, NT)
     for copy in copies:
         copy.wait()
+
+
+def leaf_kernel(
+    sizes_ref, residual_ref, first_image_ref, tile_hbm, basis_ref, coupling_ref,
+    image_ref, scalars_ref, tile_ref, sems,
+):
+    width = POINTS // HALVES
+    copies = []
+    for half in range(HALVES):
+        rows = pl.ds(width * half, width)
+        copies.append(pltpu.make_async_copy(tile_hbm.at[rows], tile_ref.at[rows], sems.at[half]))
+        copies[-1].start()
+    v = residual_ref[...]
+    rounded = v.astype(bf16)
+    leaf = None
+    for half in range(HALVES):
+        span = slice(width * half, width * (half + 1))
+        copies[half].wait()
+        part = dot(rounded[:, span], tile_ref[span, :], NN)
+        leaf = part if half == 0 else leaf + part
+    image, curvature = leaf_level(
+        v, rounded, leaf, sizes_ref[0, 0], basis_ref, coupling_ref
+    )
+    image_ref[...] = image
+    scalars_ref[0:1, :] = curvature
+    scalars_ref[1:2, :] = rows_of(v * v)
+    scalars_ref[2:3, :] = rows_of(v * first_image_ref[...])
 
 
 def pair_sums(got_ref):
@@ -299,29 +336,26 @@
 
 
 def turn_kernel(
-    sizes_ref, got_ref, right_ref, image_ref, tile_ref, basis_ref, coupling_ref,
-    residual_ref, whole_image_ref, next_image_ref, scalars_ref, send_ref, keep_ref,
+    got_ref, right_ref, image_ref, parts_ref, basis_ref, coupling_ref,
+    residual_ref, whole_image_ref, send_hbm, keep_ref, send_ref, sem,
 ):
     scalars = total(got_ref, PLANE, ROWS + 2, ROWS, 2)
     curvature, norm = scalars[0:1], scalars[1:2]
     step = norm / curvature
     coefficients = level_coefficients(got_ref, coupling_ref, ROWS + 2)
+    gram_high, gram_low = halves(parts_ref[:, 2 * PROBES :])
+    spread = dot(gram_high, coefficients, NN) + dot(gram_low, coefficients, NN)
+    projected = parts_ref[:, :PROBES] - step * (parts_ref[:, PROBES : 2 * PROBES] + spread)
+    send_levels(projected, coupling_ref, send_ref)
+    out = pltpu.make_async_copy(send_ref, send_hbm, sem.at[0])
+    out.start()
     whole = image_ref[...] + expand(coefficients, basis_ref, slice(0, POINTS))
-    residual = right_ref[...] - down_rows(step) * whole
     whole_image_ref[...] = whole
-    residual_ref[...] = residual
+    residual_ref[...] = right_ref[...] - down_rows(step) * whole
     keep_ref[0:1, :] = step
     keep_ref[1:2, :] = curvature
     keep_ref[2:3, :] = norm
-    rounded = residual.astype(bf16)
-    wide = basis_ref[1:10].reshape(9 * RANK, POINTS)
-    send_levels(dot(wide, rounded, NT), coupling_ref, send_ref)
-    leaf = dot(rounded, tile_ref[...], NN)
-    image, own = leaf_level(residual, rounded, leaf, sizes_ref[0, 0], basis_ref, coupling_ref)
-    next_image_ref[...] = image
-    scalars_ref[0:1, :] = own
-    scalars_ref[1:2, :] = rows_of(residual * residual)
-    scalars_ref[2:3, :] = rows_of(residual * whole)
+    out.wait()
 
 
 def end_kernel(
@@ -402,6 +436,7 @@
     field = ((PROBES, POINTS), f32)
     message = ((PLANE * ROWS, PROBES), f32)
     message_scratch = pltpu.VMEM(*message)
+    parts_block = ((9 * RANK, 2 * PROBES + 9 * RANK), f32)
 
     def scalar_rows(rows):
         return ((rows, PROBES), f32)
@@ -445,11 +480,11 @@
         far_ins=(0, 1, 2),
         far_outs=(0,),
     )
-    (tile, image, _), got = tree(
+    (tile, image, parts, _), got = tree(
         send,
         lambda: call(
             tile_kernel,
-            [((POINTS, POINTS), bf16), field, scalar_rows(2)],
+            [((POINTS, POINTS), bf16), field, parts_block, scalar_rows(2)],
             [coordinates, tree_order, leaf_sizes, right_side, level_basis, coupling],
             12,
             4 << 30,
@@ -463,15 +498,33 @@
         ),
         2,
     )
-    residual, first_image, image, scalars, send, keep = call(
+    residual, first_image, send, keep = call(
         turn_kernel,
-        [field, field, field, scalar_rows(3), message, scalar_rows(3)],
-        [leaf_sizes, got, right_side, image, tile, level_basis, coupling],
+        [field, field, message, scalar_rows(3)],
+        [got, right_side, image, parts, level_basis, coupling],
         8,
         1 << 28,
+        scratch=[message_scratch, pltpu.SemaphoreType.DMA((1,))],
         name="turn",
-    )
-    _, got = tree(send, lambda: (scalars,), 3)
+        far_outs=(2,),
+    )
+    (image, _), got = tree(
+        send,
+        lambda: call(
+            leaf_kernel,
+            [field, scalar_rows(3)],
+            [leaf_sizes, residual, first_image, tile, level_basis, coupling],
+            8,
+            1 << 30,
+            scratch=[
+                pltpu.VMEM((POINTS, POINTS), bf16),
+                pltpu.SemaphoreType.DMA((HALVES,)),
+            ],
+            name="leaf",
+            far_ins=(3,),
+        ),
+        3,
+    )
     return tuple(
         call(
             end_kernel,

time: 112 us -> 111 us (level)
  blocking collectives: 82.3 us -> 71 us
  waiting for transfers between devices: 3.95 us -> 7.99 us
  starting transfers between devices: 10.4 us -> 14.3 us
  Pallas kernels: 12.4 us -> 14.1 us
    all_to_all x5 -> x4, blocking collectives: 82.3 us -> 71 us  [exchange(): got = lax.all_to_all(blocks, 'pts', 0, 0, axis_index_groups=groups)]
    all_to_all x1 -> x2, waiting for transfers between devices: 3.95 us -> 7.99 us  [exchange(): got = lax.all_to_all(blocks, 'pts', 0, 0, axis_index_groups=groups)]
    all_to_all x1 -> x2, starting transfers between devices: 10.4 us -> 14.3 us  [exchange(): got = lax.all_to_all(blocks, 'pts', 0, 0, axis_index_groups=groups)]
    pallas_call x8 -> x9, Pallas kernels: 12.4 us -> 14.1 us  [call(): pl.pallas_call(body, out_shape=[(pltpu.HBM if place in far_outs else jax....]
    unnamed x14 -> x18, local copies, waits for them, and re-layouts: 1.62 us -> 2.48 us
  transfers between devices with their start and end apart: 1 -> 2, of which waited for: 1 -> 2; matrix products, arithmetic and copies ran while one was open for 0% -> 0% of each run, Pallas kernels for 5% -> 7%
where the time goes in v5:
time: 111 us
  blocking collectives  71 us (64%)
  starting transfers between devices  14.3 us (13%)
  Pallas kernels  14.1 us (13%)
  waiting for transfers between devices  7.99 us (7%)
  local copies, waits for them, and re-layouts  2.48 us (2%)
    all_to_all x4, blocking collectives, exchange(): got = lax.all_to_all(blocks, 'pts', 0, 0, axis_index_groups=groups)  71 us
    all_to_all x2, starting transfers between devices, exchange(): got = lax.all_to_all(blocks, 'pts', 0, 0, axis_index_groups=groups)  14.3 us
    pallas_call x9, Pallas kernels, call(): pl.pallas_call(body, out_shape=[(pltpu.HBM if place in far_outs else jax....  14.1 us
    all_to_all x2, waiting for transfers between devices, exchange(): got = lax.all_to_all(blocks, 'pts', 0, 0, axis_index_groups=groups)  7.99 us
    unnamed x18, local copies, waits for them, and re-layouts  2.48 us
  transfers between devices with their start and end apart: 2, of which 2 were waited for; matrix products, arithmetic and copies ran while one was open for 0% of the time, Pallas kernels for 7%

profile of v5, /device:TPU:1, one launch (start us, length us, event | category | flops | bytes accessed | tf_op | source)
XLA Modules:
  0.0 110.7 jit_solution(5223423140009784688)
XLA Ops:
  0.6 0.0 copy-start.1
  0.6 0.0 copy-start
  0.7 0.0 copy-start.2
  0.7 0.0 copy-start.6
  0.7 0.0 copy-start.8
  0.7 0.0 copy-start.7
  0.7 2.7 %start.1 = f32[576,128]{1,0:T(8,128)} custom-call(f32[128,1024]{1,0:T(8,128)} %right_ref.5, bf16[10,32,1024]{2,1,0:T(8,128)(2,1)} %basis_ref.7, f32[1,10,64,64]{3,2,1,0:T(8,128)} %coupling_ref.7), custom_call_target="tpu_custom_call" | custom-call | flops 67108864 | bytes 2097152 | tf_op jit(solution)/shard_map/start/pallas_call | solution.py:403
  3.4 10.4 %all-to-all-start = ((f32[32,1,2304]{2,1,0:T(1,128)}), f32[32,1,2304]{2,1,0:T(1,128)S(1)}, u32[]{:S(2)}, u32[]{:S(2)}) async-start(f32[32,1,2304]{2,1,0:T(1,128)} %bitcast.24), calls=%async_computation | async-start | bytes 589824 | tf_op jit(solution)/shard_map/all_to_all | solution.py:429
  13.8 0.0 copy-done.1
  13.9 0.0 copy-done
  13.9 0.0 copy-done.2
  13.9 0.0 copy-done.6
  13.9 0.0 copy-done.8
  13.9 0.0 copy-done.7
  13.9 6.1 %tile.1 = (bf16[1024,1024]{1,0:T(8,128)(2,1)}, f32[128,1024]{1,0:T(8,128)S(1)}, f32[288,544]{1,0:T(8,128)S(1)}, f32[2,128]{1,0:T(2,128)S(1)}) custom-call(f32[3,1024]{1,0:T(4,128)S(1)} %copy-done.7, s32[1,1024]{1,0:T(1,128)S(1)} %copy-done.8, s32[1,2]{1,0:T(1,128)S(1)} %copy-done.6, f32[128,1024]{1,0:T(8,128)S(1)} %copy-done.2, ...), custom_call_target="tpu_custom_call" | custom-call | flops 4294967296 | bytes 2097152 | tf_op jit(solution)/shard_map/tile/pallas_call | solution.py:403
  20.1 0.0 copy-start.4
  20.1 0.9 copy-done.4
  20.9 2.2 %all-to-all-done = f32[32,1,2304]{2,1,0:T(1,128)S(1)} async-done(((f32[32,1,2304]{2,1,0:T(1,128)}), f32[32,1,2304]{2,1,0:T(1,128)S(1)}, u32[]{:S(2)}, u32[]{:S(2)}) %all-to-all-start) | async-done | bytes 294944 | tf_op jit(solution)/shard_map/all_to_all | solution.py:429
  23.2 0.0 copy-start.5
  23.2 24.8 %all_to_all.30 = f32[16,1,1280]{2,1,0:T(1,128)S(1)} all-to-all(f32[16,1,1280]{2,1,0:T(1,128)S(1)} %bitcast.22), channel_id=1, replica_groups={{0,32,64,96,128,160,192,224,256,288,320,352,384,416,448,480},{1,33,65,9..., dimensions={0} | all-to-all | bytes 163840 | tf_op jit(solution)/shard_map/all_to_all | solution.py:429
  48.0 0.1 depth.2
  48.0 16.5 %all_to_all.31 = f32[32,1,2560]{2,1,0:T(1,128)S(1)} all-to-all(f32[32,1,2560]{2,1,0:T(1,128)S(1)} %bitcast.19), channel_id=1, replica_groups={{0,1,2,3,4,5,6,7,8,9,10,11,12,13,14,15,16,17,18,19,20,21,22,23,24,25,26..., dimensions={0} | all-to-all | bytes 655360 | tf_op jit(solution)/shard_map/all_to_all | solution.py:429
  64.5 0.0 copy-done.5
  64.5 1.5 %turn.1 = (f32[128,1024]{1,0:T(8,128)S(1)}, f32[128,1024]{1,0:T(8,128)S(1)}, f32[576,128]{1,0:T(8,128)}, f32[3,128]{1,0:T(4,128)S(1)}) custom-call(f32[640,128]{1,0:T(8,128)S(1)} %bitcast.18, f32[128,1024]{1,0:T(8,128)S(1)} %copy-done.2, f32[128,1024]{1,0:T(8,128)S(1)} %get-tuple-element.13.image_ref, f32[288,544]{1,0:T(8,128)S(1)} %copy-done.5, ...), custom_call_target="tpu_custom_call" | custom-call | flops 268435456 | bytes 2097152 | tf_op jit(solution)/shard_map/turn/pallas_call | solution.py:403
  66.0 3.8 %all-to-all-start.3 = ((f32[32,1,2304]{2,1,0:T(1,128)}), f32[32,1,2304]{2,1,0:T(1,128)S(1)}, u32[]{:S(2)}, u32[]{:S(2)}) async-start(f32[32,1,2304]{2,1,0:T(1,128)} %bitcast.25), calls=%async_computation.3 | async-start | bytes 589824 | tf_op jit(solution)/shard_map/all_to_all | solution.py:429
  69.8 0.0 copy-start.3
  69.9 1.6 %copy-done.3 = bf16[1024,1024]{1,0:T(8,128)(2,1)S(1)} copy-done((bf16[1024,1024]{1,0:T(8,128)(2,1)S(1)}, bf16[1024,1024]{1,0:T(8,128)(2,1)}, u32[]{:S(2)}) %copy-start.3) | copy-done | bytes 2097176
  71.4 2.0 %leaf.1 = (f32[128,1024]{1,0:T(8,128)S(1)}, f32[3,128]{1,0:T(4,128)S(1)}) custom-call(s32[1,2]{1,0:T(1,128)S(1)} %copy-done.6, f32[128,1024]{1,0:T(8,128)S(1)} %get-tuple-element.16.residual_ref, f32[128,1024]{1,0:T(8,128)S(1)} %get-tuple-element.17.first_image_ref, bf16[1024,1024]{1,0:T(8,128)(2,1)S(1)} %copy-done.3, bf16[10,32,1024]{2,1,0:T(8,128)(2,1)S(1)} %copy-done, ...), custom_call_target="tpu_custom_call" | custom-call | flops 1073741824 | bytes 2097152 | tf_op jit(solution)/shard_map/leaf/pallas_call | solution.py:403
  73.4 5.7 %all-to-all-done.3 = f32[32,1,2304]{2,1,0:T(1,128)S(1)} async-done(((f32[32,1,2304]{2,1,0:T(1,128)}), f32[32,1,2304]{2,1,0:T(1,128)S(1)}, u32[]{:S(2)}, u32[]{:S(2)}) %all-to-all-start.3) | async-done | bytes 294944 | tf_op jit(solution)/shard_map/all_to_all | solution.py:429
  79.2 14.6 %all_to_all.32 = f32[16,1,1408]{2,1,0:T(1,128)S(1)} all-to-all(f32[16,1,1408]{2,1,0:T(1,128)S(1)} %bitcast.21), channel_id=1, replica_groups={{0,32,64,96,128,160,192,224,256,288,320,352,384,416,448,480},{1,33,65,9..., dimensions={0} | all-to-all | bytes 180224 | tf_op jit(solution)/shard_map/all_to_all | solution.py:429
  93.8 0.1 depth.3
  93.9 15.2 %all_to_all.33 = f32[32,1,2688]{2,1,0:T(1,128)S(1)} all-to-all(f32[32,1,2688]{2,1,0:T(1,128)S(1)} %bitcast.17), channel_id=1, replica_groups={{0,1,2,3,4,5,6,7,8,9,10,11,12,13,14,15,16,17,18,19,20,21,22,23,24,25,26..., dimensions={0} | all-to-all | bytes 688128 | tf_op jit(solution)/shard_map/all_to_all | solution.py:429
  109.1 1.6 %end.1 = (f32[128,1024]{1,0:T(8,128)}, f32[128,1024]{1,0:T(8,128)}) custom-call(f32[672,128]{1,0:T(8,128)S(1)} %bitcast.16, f32[128,1024]{1,0:T(8,128)S(1)} %copy-done.2, f32[128,1024]{1,0:T(8,128)S(1)} %get-tuple-element.16.residual_ref, f32[128,1024]{1,0:T(8,128)S(1)} %get-tuple-element.17.first_image_ref, f32[128,1024]{1,0:T(8,128)S(1)} %get-tuple-element.20.image_ref, ...), custom_call_target="tpu_custom_call" | custom-call | flops 268435456 | bytes 2097152 | tf_op jit(solution)/shard_map/end/pallas_call | solution.py:403
  (2 shorter events, 0.1 us)
Async XLA Ops:
  0.6 13.2 %copy-start.1 = (f32[1,10,64,64]{3,2,1,0:T(8,128)S(1)}, f32[1,10,64,64]{3,2,1,0:T(8,128)}, u32[]{:S(2)}) copy-start(f32[1,10,64,64]{3,2,1,0:T(8,128)} %coupling_ref.7) | copy-start | bytes 491524
  0.6 13.2 %copy-start = (bf16[10,32,1024]{2,1,0:T(8,128)(2,1)S(1)}, bf16[10,32,1024]{2,1,0:T(8,128)(2,1)}, u32[]{:S(2)}) copy-start(bf16[10,32,1024]{2,1,0:T(8,128)(2,1)} %basis_ref.7) | copy-start | bytes 1966084
  0.7 13.2 %copy-start.2 = (f32[128,1024]{1,0:T(8,128)S(1)}, f32[128,1024]{1,0:T(8,128)}, u32[]{:S(2)}) copy-start(f32[128,1024]{1,0:T(8,128)} %right_ref.5) | copy-start | bytes 1572868
  0.7 13.2 %copy-start.6 = (s32[1,2]{1,0:T(1,128)S(1)}, s32[1,2]{1,0:T(1,128)}, u32[]{:S(2)}) copy-start(s32[1,2]{1,0:T(1,128)} %sizes_ref.3) | copy-start | bytes 28
  0.7 13.2 %copy-start.8 = (s32[1,1024]{1,0:T(1,128)S(1)}, s32[1,1024]{1,0:T(1,128)}, u32[]{:S(2)}) copy-start(s32[1,1024]{1,0:T(1,128)} %order_ref.1) | copy-start | bytes 12292
  0.7 13.2 %copy-start.7 = (f32[3,1024]{1,0:T(4,128)S(1)}, f32[3,1024]{1,0:T(4,128)}, u32[]{:S(2)}) copy-start(f32[3,1024]{1,0:T(4,128)} %coordinates_ref.1) | copy-start | bytes 36868
  3.4 19.8 %all-to-all-start = ((f32[32,1,2304]{2,1,0:T(1,128)}), f32[32,1,2304]{2,1,0:T(1,128)S(1)}, u32[]{:S(2)}, u32[]{:S(2)}) async-start(f32[32,1,2304]{2,1,0:T(1,128)} %bitcast.24), calls=%async_computation | async-start | bytes 589824 | tf_op jit(solution)/shard_map/all_to_all | solution.py:429
  20.1 0.9 copy-start.4
  23.2 41.3 %copy-start.5 = (f32[288,544]{1,0:T(8,128)S(1)}, f32[288,544]{1,0:T(8,128)}, u32[]{:S(2)}) copy-start(f32[288,544]{1,0:T(8,128)} %copy-done.4) | copy-start | bytes 1880068
  66.0 13.2 %all-to-all-start.3 = ((f32[32,1,2304]{2,1,0:T(1,128)}), f32[32,1,2304]{2,1,0:T(1,128)S(1)}, u32[]{:S(2)}, u32[]{:S(2)}) async-start(f32[32,1,2304]{2,1,0:T(1,128)} %bitcast.25), calls=%async_computation.3 | async-start | bytes 589824 | tf_op jit(solution)/shard_map/all_to_all | solution.py:429
  69.8 1.6 %copy-start.3 = (bf16[1024,1024]{1,0:T(8,128)(2,1)S(1)}, bf16[1024,1024]{1,0:T(8,128)(2,1)}, u32[]{:S(2)}) copy-start(bf16[1024,1024]{1,0:T(8,128)(2,1)} %get-tuple-element.18.tile_hbm) | copy-start | bytes 6291460

commit v6 on v5

--- a/solution.py
+++ b/solution.py
@@ -142,7 +142,7 @@
 def tile_kernel(
     coordinates_ref, order_ref, sizes_ref, right_ref, basis_ref, coupling_ref,
     tile_hbm, image_ref, parts_ref, scalars_ref,
-    tile_ref, down_ref, sems,
+    tile_ref, sems,
 ):
     boundary = sizes_ref[0, 0]
     order = order_ref[...]
@@ -162,47 +162,44 @@
             piece = jnp.where(chosen == number, jnp.take_along_axis(source, lane, axis=1), piece)
         pieces.append(piece)
     x = jnp.concatenate(pieces, axis=1)
+    x = SQRT_THREE * x
     column = x.T
-    for c in range(3):
-        down_ref[c] = jnp.broadcast_to(column[:, c : c + 1], (POINTS, 128))
     edge = boundary.astype(f32) - 0.5
-
-    def fill(row_start, row_stop, col_start, col_stop):
-        group = 128
-        width = col_stop - col_start
-        across = [x[c : c + 1, col_start:col_stop] for c in range(3)]
-        col_ids = col_start + lax.broadcasted_iota(jnp.int32, (1, width), 1)
-        col_side = col_ids.astype(f32) - edge
-
-        def widen(block):
-            return jnp.concatenate([block] * (width // 128), axis=1)
-
-        @pl.loop(0, (row_stop - row_start) // group)
-        def _(block):
-            start = pl.multiple_of(row_start + block * group, group)
+    block = 128
+    last = POINTS // block
+    tile_ref[:LEAST, MOST:] = jnp.zeros((LEAST, POINTS - MOST), bf16)
+    tile_ref[MOST:, :LEAST] = jnp.zeros((POINTS - MOST, LEAST), bf16)
+    ids = lax.broadcasted_iota(jnp.int32, (block, block), 0)
+    lanes = lax.broadcasted_iota(jnp.int32, (block, block), 1)
+    diagonal = jnp.where(ids == lanes, NOISE_VAR, 0.0)
+    row_side = ids.astype(f32) - edge
+    col_side = lanes.astype(f32) - edge
+    least, most = LEAST // block, MOST // block
+    copies = []
+    for up in range(last):
+        rows = slice(block * up, block * (up + 1))
+        down = [
+            jnp.broadcast_to(column[rows, c : c + 1], (block, block)) for c in range(3)
+        ]
+        for across in range(up, most if up < least else last):
+            columns = slice(block * across, block * (across + 1))
             dist_sq = None
             for c in range(3):
-                offset = widen(down_ref[c, pl.ds(start, group), :]) - across[c]
+                offset = down[c] - x[c : c + 1, columns]
                 dist_sq = offset * offset if c == 0 else dist_sq + offset * offset
-            root = dist_sq * lax.rsqrt(jnp.maximum(dist_sq, 1e-37))
-            scaled = SQRT_THREE * root
+            scaled = dist_sq * lax.rsqrt(jnp.maximum(dist_sq, 1e-37))
             values = (1.0 + scaled) * jnp.exp(-scaled)
-            ids = start + lax.broadcasted_iota(jnp.int32, (group, 128), 0)
-            same = widen(ids.astype(f32) - edge) * col_side > 0.0
-            values = jnp.where(same, values, 0.0)
-            values = values + jnp.where(widen(ids) == col_ids, NOISE_VAR, 0.0)
-            tile_ref[pl.ds(start, group), col_start:col_stop] = values.astype(bf16)
-
-    tile_ref[:LEAST, MOST:] = jnp.zeros((LEAST, POINTS - MOST), bf16)
-    tile_ref[MOST:, :LEAST] = jnp.zeros((POINTS - MOST, LEAST), bf16)
-    copies = []
-    for number, (start, stop, low, high) in enumerate(
-        ((0, LEAST, 0, MOST), (LEAST, MOST, 0, POINTS), (MOST, POINTS, LEAST, POINTS))
-    ):
-        fill(start, stop, low, high)
-        rows = pl.ds(start, stop - start)
+            if across >= least and up < most:
+                same = (row_side + block * up) * (col_side + block * across) > 0.0
+                values = jnp.where(same, values, 0.0)
+            if across == up:
+                values = values + diagonal
+            tile_ref[rows, columns] = values.astype(bf16)
+            if across != up:
+                tile_ref[columns, rows] = values.T.astype(bf16)
+        span = pl.ds(block * up, block)
         copies.append(
-            pltpu.make_async_copy(tile_ref.at[rows], tile_hbm.at[rows], sems.at[number])
+            pltpu.make_async_copy(tile_ref.at[span], tile_hbm.at[span], sems.at[up])
         )
         copies[-1].start()
 
@@ -490,8 +487,7 @@
             4 << 30,
             scratch=[
                 pltpu.VMEM((POINTS, POINTS), bf16),
-                pltpu.VMEM((3, POINTS, 128), f32),
-                pltpu.SemaphoreType.DMA((3,)),
+                pltpu.SemaphoreType.DMA((POINTS // 128,)),
             ],
             name="tile",
             far_outs=(0,),

time: 111 us -> 110 us (level)
  waiting for transfers between devices: 7.99 us -> 9.74 us
  Pallas kernels: 14.1 us -> 12.4 us
  blocking collectives: 71 us -> 69.6 us
    pallas_call x9, Pallas kernels: 14.1 us -> 12.4 us  [call(): pl.pallas_call(body, out_shape=[(pltpu.HBM if place in far_outs else jax....]
    all_to_all x2, waiting for transfers between devices: 7.99 us -> 9.74 us  [exchange(): got = lax.all_to_all(blocks, 'pts', 0, 0, axis_index_groups=groups)]
    all_to_all x4, blocking collectives: 71 us -> 69.6 us  [exchange(): got = lax.all_to_all(blocks, 'pts', 0, 0, axis_index_groups=groups)]
  transfers between devices with their start and end apart: 2 -> 2, of which waited for: 2 -> 2; matrix products, arithmetic and copies ran while one was open for 0% -> 0% of each run, Pallas kernels for 7% -> 6%
where the time goes in v6:
time: 110 us; the launch traced here: 109 us
  blocking collectives  69.6 us (63%)
  starting transfers between devices  14.3 us (13%)
  Pallas kernels  12.4 us (11%)
  waiting for transfers between devices  9.74 us (9%)
  local copies, waits for them, and re-layouts  2.48 us (2%)
    all_to_all x4, blocking collectives, exchange(): got = lax.all_to_all(blocks, 'pts', 0, 0, axis_index_groups=groups)  69.6 us
    all_to_all x2, starting transfers between devices, exchange(): got = lax.all_to_all(blocks, 'pts', 0, 0, axis_index_groups=groups)  14.3 us
    pallas_call x9, Pallas kernels, call(): pl.pallas_call(body, out_shape=[(pltpu.HBM if place in far_outs else jax....  12.4 us
    all_to_all x2, waiting for transfers between devices, exchange(): got = lax.all_to_all(blocks, 'pts', 0, 0, axis_index_groups=groups)  9.74 us
    unnamed x18, local copies, waits for them, and re-layouts  2.48 us
  transfers between devices with their start and end apart: 2, of which 2 were waited for; matrix products, arithmetic and copies ran while one was open for 0% of the time, Pallas kernels for 6%

profile of v6, /device:TPU:1, one launch (start us, length us, event | category | flops | bytes accessed | tf_op | source)
XLA Modules:
  0.0 109.3 jit_solution(31606851258892030)
XLA Ops:
  0.6 0.0 copy-start.1
  0.6 0.0 copy-start
  0.7 0.0 copy-start.2
  0.7 0.0 copy-start.6
  0.7 0.0 copy-start.8
  0.7 0.0 copy-start.7
  0.7 2.7 %start.1 = f32[576,128]{1,0:T(8,128)} custom-call(f32[128,1024]{1,0:T(8,128)} %right_ref.5, bf16[10,32,1024]{2,1,0:T(8,128)(2,1)} %basis_ref.7, f32[1,10,64,64]{3,2,1,0:T(8,128)} %coupling_ref.7), custom_call_target="tpu_custom_call" | custom-call | flops 67108864 | bytes 2097152 | tf_op jit(solution)/shard_map/start/pallas_call | solution.py:400
  3.4 10.4 %all-to-all-start = ((f32[32,1,2304]{2,1,0:T(1,128)}), f32[32,1,2304]{2,1,0:T(1,128)S(1)}, u32[]{:S(2)}, u32[]{:S(2)}) async-start(f32[32,1,2304]{2,1,0:T(1,128)} %bitcast.24), calls=%async_computation | async-start | bytes 589824 | tf_op jit(solution)/shard_map/all_to_all | solution.py:426
  13.8 0.0 copy-done.1
  13.9 0.0 copy-done
  13.9 0.0 copy-done.2
  13.9 0.0 copy-done.6
  13.9 0.0 copy-done.8
  13.9 0.0 copy-done.7
  13.9 4.4 %tile.1 = (bf16[1024,1024]{1,0:T(8,128)(2,1)}, f32[128,1024]{1,0:T(8,128)S(1)}, f32[288,544]{1,0:T(8,128)S(1)}, f32[2,128]{1,0:T(2,128)S(1)}) custom-call(f32[3,1024]{1,0:T(4,128)S(1)} %copy-done.7, s32[1,1024]{1,0:T(1,128)S(1)} %copy-done.8, s32[1,2]{1,0:T(1,128)S(1)} %copy-done.6, f32[128,1024]{1,0:T(8,128)S(1)} %copy-done.2, ...), custom_call_target="tpu_custom_call" | custom-call | flops 4294967296 | bytes 2097152 | tf_op jit(solution)/shard_map/tile/pallas_call | solution.py:400
  18.3 0.0 copy-start.4
  18.3 0.9 copy-done.4
  19.2 4.0 %all-to-all-done = f32[32,1,2304]{2,1,0:T(1,128)S(1)} async-done(((f32[32,1,2304]{2,1,0:T(1,128)}), f32[32,1,2304]{2,1,0:T(1,128)S(1)}, u32[]{:S(2)}, u32[]{:S(2)}) %all-to-all-start) | async-done | bytes 294944 | tf_op jit(solution)/shard_map/all_to_all | solution.py:426
  23.2 0.0 copy-start.5
  23.2 24.8 %all_to_all.30 = f32[16,1,1280]{2,1,0:T(1,128)S(1)} all-to-all(f32[16,1,1280]{2,1,0:T(1,128)S(1)} %bitcast.22), channel_id=1, replica_groups={{0,32,64,96,128,160,192,224,256,288,320,352,384,416,448,480},{1,33,65,9..., dimensions={0} | all-to-all | bytes 163840 | tf_op jit(solution)/shard_map/all_to_all | solution.py:426
  48.0 0.1 depth.2
  48.0 14.7 %all_to_all.31 = f32[32,1,2560]{2,1,0:T(1,128)S(1)} all-to-all(f32[32,1,2560]{2,1,0:T(1,128)S(1)} %bitcast.19), channel_id=1, replica_groups={{0,1,2,3,4,5,6,7,8,9,10,11,12,13,14,15,16,17,18,19,20,21,22,23,24,25,26..., dimensions={0} | all-to-all | bytes 655360 | tf_op jit(solution)/shard_map/all_to_all | solution.py:426
  62.7 0.0 copy-done.5
  62.7 1.5 %turn.1 = (f32[128,1024]{1,0:T(8,128)S(1)}, f32[128,1024]{1,0:T(8,128)S(1)}, f32[576,128]{1,0:T(8,128)}, f32[3,128]{1,0:T(4,128)S(1)}) custom-call(f32[640,128]{1,0:T(8,128)S(1)} %bitcast.18, f32[128,1024]{1,0:T(8,128)S(1)} %copy-done.2, f32[128,1024]{1,0:T(8,128)S(1)} %get-tuple-element.13.image_ref, f32[288,544]{1,0:T(8,128)S(1)} %copy-done.5, ...), custom_call_target="tpu_custom_call" | custom-call | flops 268435456 | bytes 2097152 | tf_op jit(solution)/shard_map/turn/pallas_call | solution.py:400
  64.2 3.8 %all-to-all-start.3 = ((f32[32,1,2304]{2,1,0:T(1,128)}), f32[32,1,2304]{2,1,0:T(1,128)S(1)}, u32[]{:S(2)}, u32[]{:S(2)}) async-start(f32[32,1,2304]{2,1,0:T(1,128)} %bitcast.25), calls=%async_computation.3 | async-start | bytes 589824 | tf_op jit(solution)/shard_map/all_to_all | solution.py:426
  68.0 0.0 copy-start.3
  68.1 1.6 %copy-done.3 = bf16[1024,1024]{1,0:T(8,128)(2,1)S(1)} copy-done((bf16[1024,1024]{1,0:T(8,128)(2,1)S(1)}, bf16[1024,1024]{1,0:T(8,128)(2,1)}, u32[]{:S(2)}) %copy-start.3) | copy-done | bytes 2097176
  69.6 2.0 %leaf.1 = (f32[128,1024]{1,0:T(8,128)S(1)}, f32[3,128]{1,0:T(4,128)S(1)}) custom-call(s32[1,2]{1,0:T(1,128)S(1)} %copy-done.6, f32[128,1024]{1,0:T(8,128)S(1)} %get-tuple-element.16.residual_ref, f32[128,1024]{1,0:T(8,128)S(1)} %get-tuple-element.17.first_image_ref, bf16[1024,1024]{1,0:T(8,128)(2,1)S(1)} %copy-done.3, bf16[10,32,1024]{2,1,0:T(8,128)(2,1)S(1)} %copy-done, ...), custom_call_target="tpu_custom_call" | custom-call | flops 1073741824 | bytes 2097152 | tf_op jit(solution)/shard_map/leaf/pallas_call | solution.py:400
  71.6 5.7 %all-to-all-done.3 = f32[32,1,2304]{2,1,0:T(1,128)S(1)} async-done(((f32[32,1,2304]{2,1,0:T(1,128)}), f32[32,1,2304]{2,1,0:T(1,128)S(1)}, u32[]{:S(2)}, u32[]{:S(2)}) %all-to-all-start.3) | async-done | bytes 294944 | tf_op jit(solution)/shard_map/all_to_all | solution.py:426
  77.4 15.0 %all_to_all.32 = f32[16,1,1408]{2,1,0:T(1,128)S(1)} all-to-all(f32[16,1,1408]{2,1,0:T(1,128)S(1)} %bitcast.21), channel_id=1, replica_groups={{0,32,64,96,128,160,192,224,256,288,320,352,384,416,448,480},{1,33,65,9..., dimensions={0} | all-to-all | bytes 180224 | tf_op jit(solution)/shard_map/all_to_all | solution.py:426
  92.4 0.1 depth.3
  92.5 15.2 %all_to_all.33 = f32[32,1,2688]{2,1,0:T(1,128)S(1)} all-to-all(f32[32,1,2688]{2,1,0:T(1,128)S(1)} %bitcast.17), channel_id=1, replica_groups={{0,1,2,3,4,5,6,7,8,9,10,11,12,13,14,15,16,17,18,19,20,21,22,23,24,25,26..., dimensions={0} | all-to-all | bytes 688128 | tf_op jit(solution)/shard_map/all_to_all | solution.py:426
  107.7 1.6 %end.1 = (f32[128,1024]{1,0:T(8,128)}, f32[128,1024]{1,0:T(8,128)}) custom-call(f32[672,128]{1,0:T(8,128)S(1)} %bitcast.16, f32[128,1024]{1,0:T(8,128)S(1)} %copy-done.2, f32[128,1024]{1,0:T(8,128)S(1)} %get-tuple-element.16.residual_ref, f32[128,1024]{1,0:T(8,128)S(1)} %get-tuple-element.17.first_image_ref, f32[128,1024]{1,0:T(8,128)S(1)} %get-tuple-element.20.image_ref, ...), custom_call_target="tpu_custom_call" | custom-call | flops 268435456 | bytes 2097152 | tf_op jit(solution)/shard_map/end/pallas_call | solution.py:400
  (2 shorter events, 0.1 us)
Async XLA Ops:
  0.6 13.2 %copy-start.1 = (f32[1,10,64,64]{3,2,1,0:T(8,128)S(1)}, f32[1,10,64,64]{3,2,1,0:T(8,128)}, u32[]{:S(2)}) copy-start(f32[1,10,64,64]{3,2,1,0:T(8,128)} %coupling_ref.7) | copy-start | bytes 491524
  0.6 13.2 %copy-start = (bf16[10,32,1024]{2,1,0:T(8,128)(2,1)S(1)}, bf16[10,32,1024]{2,1,0:T(8,128)(2,1)}, u32[]{:S(2)}) copy-start(bf16[10,32,1024]{2,1,0:T(8,128)(2,1)} %basis_ref.7) | copy-start | bytes 1966084
  0.7 13.2 %copy-start.2 = (f32[128,1024]{1,0:T(8,128)S(1)}, f32[128,1024]{1,0:T(8,128)}, u32[]{:S(2)}) copy-start(f32[128,1024]{1,0:T(8,128)} %right_ref.5) | copy-start | bytes 1572868
  0.7 13.2 %copy-start.6 = (s32[1,2]{1,0:T(1,128)S(1)}, s32[1,2]{1,0:T(1,128)}, u32[]{:S(2)}) copy-start(s32[1,2]{1,0:T(1,128)} %sizes_ref.3) | copy-start | bytes 28
  0.7 13.2 %copy-start.8 = (s32[1,1024]{1,0:T(1,128)S(1)}, s32[1,1024]{1,0:T(1,128)}, u32[]{:S(2)}) copy-start(s32[1,1024]{1,0:T(1,128)} %order_ref.1) | copy-start | bytes 12292
  0.7 13.2 %copy-start.7 = (f32[3,1024]{1,0:T(4,128)S(1)}, f32[3,1024]{1,0:T(4,128)}, u32[]{:S(2)}) copy-start(f32[3,1024]{1,0:T(4,128)} %coordinates_ref.1) | copy-start | bytes 36868
  3.4 19.8 %all-to-all-start = ((f32[32,1,2304]{2,1,0:T(1,128)}), f32[32,1,2304]{2,1,0:T(1,128)S(1)}, u32[]{:S(2)}, u32[]{:S(2)}) async-start(f32[32,1,2304]{2,1,0:T(1,128)} %bitcast.24), calls=%async_computation | async-start | bytes 589824 | tf_op jit(solution)/shard_map/all_to_all | solution.py:426
  18.3 0.9 copy-start.4
  23.2 39.5 %copy-start.5 = (f32[288,544]{1,0:T(8,128)S(1)}, f32[288,544]{1,0:T(8,128)}, u32[]{:S(2)}) copy-start(f32[288,544]{1,0:T(8,128)} %copy-done.4) | copy-start | bytes 1880068
  64.2 13.2 %all-to-all-start.3 = ((f32[32,1,2304]{2,1,0:T(1,128)}), f32[32,1,2304]{2,1,0:T(1,128)S(1)}, u32[]{:S(2)}, u32[]{:S(2)}) async-start(f32[32,1,2304]{2,1,0:T(1,128)} %bitcast.25), calls=%async_computation.3 | async-start | bytes 589824 | tf_op jit(solution)/shard_map/all_to_all | solution.py:426
  68.0 1.6 %copy-start.3 = (bf16[1024,1024]{1,0:T(8,128)(2,1)S(1)}, bf16[1024,1024]{1,0:T(8,128)(2,1)}, u32[]{:S(2)}) copy-start(bf16[1024,1024]{1,0:T(8,128)(2,1)} %get-tuple-element.18.tile_hbm) | copy-start | bytes 6291460

commit v7 on v6

--- a/solution.py
+++ b/solution.py
@@ -23,6 +23,7 @@
 LEAST = 384
 MOST = 640
 HALVES = 2
+PARTS = 2 * PROBES + 9 * RANK
 
 NT = (((1,), (1,)), ((), ()))
 TN = (((0,), (0,)), ((), ()))
@@ -125,6 +126,17 @@
     out.wait()
 
 
+def leaf_product(rounded, tile_ref):
+    return jnp.concatenate(
+        [
+            dot(rounded[:, :MOST], tile_ref[:MOST, :LEAST], NN),
+            dot(rounded, tile_ref[:, LEAST:MOST], NN),
+            dot(rounded[:, LEAST:], tile_ref[LEAST:, MOST:], NN),
+        ],
+        axis=1,
+    )
+
+
 def leaf_level(v, rounded, leaf, boundary, basis_ref, coupling_ref):
     wide = basis_ref[0].astype(f32)
     in_first = lax.broadcasted_iota(jnp.int32, (RANK, POINTS), 1) < boundary
@@ -141,8 +153,8 @@
 
 def tile_kernel(
     coordinates_ref, order_ref, sizes_ref, right_ref, basis_ref, coupling_ref,
-    tile_hbm, image_ref, parts_ref, scalars_ref,
-    tile_ref, sems,
+    tile_hbm, image_ref, parts_hbm, scalars_ref,
+    tile_ref, parts_ref, sems,
 ):
     boundary = sizes_ref[0, 0]
     order = order_ref[...]
@@ -203,17 +215,28 @@
         )
         copies[-1].start()
 
+    def send_parts(start, stop):
+        lanes = pl.ds(start, stop - start)
+        copies.append(
+            pltpu.make_async_copy(
+                parts_ref.at[:, lanes], parts_hbm.at[:, lanes], sems.at[len(copies)]
+            )
+        )
+        copies[-1].start()
+
     v = right_ref[...]
+    wide = basis_ref[1:10].reshape(9 * RANK, POINTS)
+    parts_ref[:, PROBES : 2 * PROBES] = project_split(wide, v)
+    parts_ref[:, 2 * PROBES :] = dot(wide, wide, NT)
+    send_parts(PROBES, PARTS)
     rounded = v.astype(bf16)
-    leaf = dot(rounded, tile_ref[...], NN)
+    leaf = leaf_product(rounded, tile_ref)
     image, curvature = leaf_level(v, rounded, leaf, boundary, basis_ref, coupling_ref)
+    parts_ref[:, :PROBES] = project_split(wide, image)
+    send_parts(0, PROBES)
     image_ref[...] = image
     scalars_ref[0:1, :] = curvature
     scalars_ref[1:2, :] = rows_of(v * v)
-    wide = basis_ref[1:10].reshape(9 * RANK, POINTS)
-    parts_ref[:, :PROBES] = project_split(wide, v)
-    parts_ref[:, PROBES : 2 * PROBES] = project_split(wide, image)
-    parts_ref[:, 2 * PROBES :] = dot(wide, wide, NT)
     for copy in copies:
         copy.wait()
 
@@ -230,12 +253,9 @@
         copies[-1].start()
     v = residual_ref[...]
     rounded = v.astype(bf16)
-    leaf = None
-    for half in range(HALVES):
-        span = slice(width * half, width * (half + 1))
-        copies[half].wait()
-        part = dot(rounded[:, span], tile_ref[span, :], NN)
-        leaf = part if half == 0 else leaf + part
+    for copy in copies:
+        copy.wait()
+    leaf = leaf_product(rounded, tile_ref)
     image, curvature = leaf_level(
         v, rounded, leaf, sizes_ref[0, 0], basis_ref, coupling_ref
     )
@@ -342,7 +362,7 @@
     coefficients = level_coefficients(got_ref, coupling_ref, ROWS + 2)
     gram_high, gram_low = halves(parts_ref[:, 2 * PROBES :])
     spread = dot(gram_high, coefficients, NN) + dot(gram_low, coefficients, NN)
-    projected = parts_ref[:, :PROBES] - step * (parts_ref[:, PROBES : 2 * PROBES] + spread)
+    projected = parts_ref[:, PROBES : 2 * PROBES] - step * (parts_ref[:, :PROBES] + spread)
     send_levels(projected, coupling_ref, send_ref)
     out = pltpu.make_async_copy(send_ref, send_hbm, sem.at[0])
     out.start()
@@ -433,7 +453,7 @@
     field = ((PROBES, POINTS), f32)
     message = ((PLANE * ROWS, PROBES), f32)
     message_scratch = pltpu.VMEM(*message)
-    parts_block = ((9 * RANK, 2 * PROBES + 9 * RANK), f32)
+    parts_block = ((9 * RANK, PARTS), f32)
 
     def scalar_rows(rows):
         return ((rows, PROBES), f32)
@@ -487,10 +507,11 @@
             4 << 30,
             scratch=[
                 pltpu.VMEM((POINTS, POINTS), bf16),
-                pltpu.SemaphoreType.DMA((POINTS // 128,)),
+                pltpu.VMEM(*parts_block),
+                pltpu.SemaphoreType.DMA((POINTS // 128 + 2,)),
             ],
             name="tile",
-            far_outs=(0,),
+            far_outs=(0, 2),
         ),
         2,
     )

time: 110 us -> 110 us (level)
    unnamed x18 -> x16, local copies, waits for them, and re-layouts: 2.48 us -> 1.61 us
where the time goes in v7:
time: 110 us; the launch traced here: 109 us
  blocking collectives  69.6 us (63%)
  starting transfers between devices  14.3 us (13%)
  Pallas kernels  13 us (12%)
  waiting for transfers between devices  10.1 us (9%)
  local copies, waits for them, and re-layouts  1.61 us (1%)
    all_to_all x4, blocking collectives, exchange(): got = lax.all_to_all(blocks, 'pts', 0, 0, axis_index_groups=groups)  69.6 us
    all_to_all x2, starting transfers between devices, exchange(): got = lax.all_to_all(blocks, 'pts', 0, 0, axis_index_groups=groups)  14.3 us
    pallas_call x9, Pallas kernels, call(): pl.pallas_call(body, out_shape=[(pltpu.HBM if place in far_outs else jax....  13 us
    all_to_all x2, waiting for transfers between devices, exchange(): got = lax.all_to_all(blocks, 'pts', 0, 0, axis_index_groups=groups)  10.1 us
  transfers between devices with their start and end apart: 2, of which 2 were waited for; matrix products, arithmetic and copies ran while one was open for 0% of the time, Pallas kernels for 6%

profile of v7, /device:TPU:1, one launch (start us, length us, event | category | flops | bytes accessed | tf_op | source)
XLA Modules:
  0.0 109.3 jit_solution(9887336754857948186)
XLA Ops:
  0.6 0.0 copy-start.1
  0.6 0.0 copy-start
  0.7 0.0 copy-start.2
  0.7 0.0 copy-start.5
  0.7 0.0 copy-start.7
  0.7 0.0 copy-start.6
  0.7 2.7 %start.1 = f32[576,128]{1,0:T(8,128)} custom-call(f32[128,1024]{1,0:T(8,128)} %right_ref.5, bf16[10,32,1024]{2,1,0:T(8,128)(2,1)} %basis_ref.7, f32[1,10,64,64]{3,2,1,0:T(8,128)} %coupling_ref.7), custom_call_target="tpu_custom_call" | custom-call | flops 67108864 | bytes 2097152 | tf_op jit(solution)/shard_map/start/pallas_call | solution.py:420
  3.4 10.4 %all-to-all-start = ((f32[32,1,2304]{2,1,0:T(1,128)}), f32[32,1,2304]{2,1,0:T(1,128)S(1)}, u32[]{:S(2)}, u32[]{:S(2)}) async-start(f32[32,1,2304]{2,1,0:T(1,128)} %bitcast.24), calls=%async_computation | async-start | bytes 589824 | tf_op jit(solution)/shard_map/all_to_all | solution.py:446
  13.8 0.0 copy-done.1
  13.9 0.0 copy-done
  13.9 0.0 copy-done.2
  13.9 0.0 copy-done.5
  13.9 0.0 copy-done.7
  13.9 0.0 copy-done.6
  13.9 5.1 %tile.1 = (bf16[1024,1024]{1,0:T(8,128)(2,1)}, f32[128,1024]{1,0:T(8,128)S(1)}, f32[288,544]{1,0:T(8,128)}, f32[2,128]{1,0:T(2,128)S(1)}) custom-call(f32[3,1024]{1,0:T(4,128)S(1)} %copy-done.6, s32[1,1024]{1,0:T(1,128)S(1)} %copy-done.7, s32[1,2]{1,0:T(1,128)S(1)} %copy-done.5, f32[128,1024]{1,0:T(8,128)S(1)} %copy-done.2, ...), custom_call_target="tpu_custom_call" | custom-call | flops 4294967296 | bytes 2097152 | tf_op jit(solution)/shard_map/tile/pallas_call | solution.py:420
  19.0 4.2 %all-to-all-done = f32[32,1,2304]{2,1,0:T(1,128)S(1)} async-done(((f32[32,1,2304]{2,1,0:T(1,128)}), f32[32,1,2304]{2,1,0:T(1,128)S(1)}, u32[]{:S(2)}, u32[]{:S(2)}) %all-to-all-start) | async-done | bytes 294944 | tf_op jit(solution)/shard_map/all_to_all | solution.py:446
  23.2 0.0 copy-start.4
  23.2 24.8 %all_to_all.30 = f32[16,1,1280]{2,1,0:T(1,128)S(1)} all-to-all(f32[16,1,1280]{2,1,0:T(1,128)S(1)} %bitcast.22), channel_id=1, replica_groups={{0,32,64,96,128,160,192,224,256,288,320,352,384,416,448,480},{1,33,65,9..., dimensions={0} | all-to-all | bytes 163840 | tf_op jit(solution)/shard_map/all_to_all | solution.py:446
  48.0 0.1 depth.2
  48.0 14.7 %all_to_all.31 = f32[32,1,2560]{2,1,0:T(1,128)S(1)} all-to-all(f32[32,1,2560]{2,1,0:T(1,128)S(1)} %bitcast.19), channel_id=1, replica_groups={{0,1,2,3,4,5,6,7,8,9,10,11,12,13,14,15,16,17,18,19,20,21,22,23,24,25,26..., dimensions={0} | all-to-all | bytes 655360 | tf_op jit(solution)/shard_map/all_to_all | solution.py:446
  62.7 0.0 copy-done.4
  62.7 1.5 %turn.1 = (f32[128,1024]{1,0:T(8,128)S(1)}, f32[128,1024]{1,0:T(8,128)S(1)}, f32[576,128]{1,0:T(8,128)}, f32[3,128]{1,0:T(4,128)S(1)}) custom-call(f32[640,128]{1,0:T(8,128)S(1)} %bitcast.18, f32[128,1024]{1,0:T(8,128)S(1)} %copy-done.2, f32[128,1024]{1,0:T(8,128)S(1)} %get-tuple-element.13.image_ref, f32[288,544]{1,0:T(8,128)S(1)} %copy-done.4, ...), custom_call_target="tpu_custom_call" | custom-call | flops 268435456 | bytes 2097152 | tf_op jit(solution)/shard_map/turn/pallas_call | solution.py:420
  64.2 3.8 %all-to-all-start.3 = ((f32[32,1,2304]{2,1,0:T(1,128)}), f32[32,1,2304]{2,1,0:T(1,128)S(1)}, u32[]{:S(2)}, u32[]{:S(2)}) async-start(f32[32,1,2304]{2,1,0:T(1,128)} %bitcast.25), calls=%async_computation.3 | async-start | bytes 589824 | tf_op jit(solution)/shard_map/all_to_all | solution.py:446
  68.0 0.0 copy-start.3
  68.1 1.6 %copy-done.3 = bf16[1024,1024]{1,0:T(8,128)(2,1)S(1)} copy-done((bf16[1024,1024]{1,0:T(8,128)(2,1)S(1)}, bf16[1024,1024]{1,0:T(8,128)(2,1)}, u32[]{:S(2)}) %copy-start.3) | copy-done | bytes 2097176
  69.6 1.9 %leaf.1 = (f32[128,1024]{1,0:T(8,128)S(1)}, f32[3,128]{1,0:T(4,128)S(1)}) custom-call(s32[1,2]{1,0:T(1,128)S(1)} %copy-done.5, f32[128,1024]{1,0:T(8,128)S(1)} %get-tuple-element.16.residual_ref, f32[128,1024]{1,0:T(8,128)S(1)} %get-tuple-element.17.first_image_ref, bf16[1024,1024]{1,0:T(8,128)(2,1)S(1)} %copy-done.3, bf16[10,32,1024]{2,1,0:T(8,128)(2,1)S(1)} %copy-done, ...), custom_call_target="tpu_custom_call" | custom-call | flops 1073741824 | bytes 2097152 | tf_op jit(solution)/shard_map/leaf/pallas_call | solution.py:420
  71.5 5.8 %all-to-all-done.3 = f32[32,1,2304]{2,1,0:T(1,128)S(1)} async-done(((f32[32,1,2304]{2,1,0:T(1,128)}), f32[32,1,2304]{2,1,0:T(1,128)S(1)}, u32[]{:S(2)}, u32[]{:S(2)}) %all-to-all-start.3) | async-done | bytes 294944 | tf_op jit(solution)/shard_map/all_to_all | solution.py:446
  77.4 15.0 %all_to_all.32 = f32[16,1,1408]{2,1,0:T(1,128)S(1)} all-to-all(f32[16,1,1408]{2,1,0:T(1,128)S(1)} %bitcast.21), channel_id=1, replica_groups={{0,32,64,96,128,160,192,224,256,288,320,352,384,416,448,480},{1,33,65,9..., dimensions={0} | all-to-all | bytes 180224 | tf_op jit(solution)/shard_map/all_to_all | solution.py:446
  92.4 0.1 depth.3
  92.5 15.2 %all_to_all.33 = f32[32,1,2688]{2,1,0:T(1,128)S(1)} all-to-all(f32[32,1,2688]{2,1,0:T(1,128)S(1)} %bitcast.17), channel_id=1, replica_groups={{0,1,2,3,4,5,6,7,8,9,10,11,12,13,14,15,16,17,18,19,20,21,22,23,24,25,26..., dimensions={0} | all-to-all | bytes 688128 | tf_op jit(solution)/shard_map/all_to_all | solution.py:446
  107.7 1.6 %end.1 = (f32[128,1024]{1,0:T(8,128)}, f32[128,1024]{1,0:T(8,128)}) custom-call(f32[672,128]{1,0:T(8,128)S(1)} %bitcast.16, f32[128,1024]{1,0:T(8,128)S(1)} %copy-done.2, f32[128,1024]{1,0:T(8,128)S(1)} %get-tuple-element.16.residual_ref, f32[128,1024]{1,0:T(8,128)S(1)} %get-tuple-element.17.first_image_ref, f32[128,1024]{1,0:T(8,128)S(1)} %get-tuple-element.20.image_ref, ...), custom_call_target="tpu_custom_call" | custom-call | flops 268435456 | bytes 2097152 | tf_op jit(solution)/shard_map/end/pallas_call | solution.py:420
  (2 shorter events, 0.1 us)
Async XLA Ops:
  0.6 13.2 %copy-start.1 = (f32[1,10,64,64]{3,2,1,0:T(8,128)S(1)}, f32[1,10,64,64]{3,2,1,0:T(8,128)}, u32[]{:S(2)}) copy-start(f32[1,10,64,64]{3,2,1,0:T(8,128)} %coupling_ref.7) | copy-start | bytes 491524
  0.6 13.2 %copy-start = (bf16[10,32,1024]{2,1,0:T(8,128)(2,1)S(1)}, bf16[10,32,1024]{2,1,0:T(8,128)(2,1)}, u32[]{:S(2)}) copy-start(bf16[10,32,1024]{2,1,0:T(8,128)(2,1)} %basis_ref.7) | copy-start | bytes 1966084
  0.7 13.2 %copy-start.2 = (f32[128,1024]{1,0:T(8,128)S(1)}, f32[128,1024]{1,0:T(8,128)}, u32[]{:S(2)}) copy-start(f32[128,1024]{1,0:T(8,128)} %right_ref.5) | copy-start | bytes 1572868
  0.7 13.2 %copy-start.5 = (s32[1,2]{1,0:T(1,128)S(1)}, s32[1,2]{1,0:T(1,128)}, u32[]{:S(2)}) copy-start(s32[1,2]{1,0:T(1,128)} %sizes_ref.3) | copy-start | bytes 28
  0.7 13.2 %copy-start.7 = (s32[1,1024]{1,0:T(1,128)S(1)}, s32[1,1024]{1,0:T(1,128)}, u32[]{:S(2)}) copy-start(s32[1,1024]{1,0:T(1,128)} %order_ref.1) | copy-start | bytes 12292
  0.7 13.2 %copy-start.6 = (f32[3,1024]{1,0:T(4,128)S(1)}, f32[3,1024]{1,0:T(4,128)}, u32[]{:S(2)}) copy-start(f32[3,1024]{1,0:T(4,128)} %coordinates_ref.1) | copy-start | bytes 36868
  3.4 19.8 %all-to-all-start = ((f32[32,1,2304]{2,1,0:T(1,128)}), f32[32,1,2304]{2,1,0:T(1,128)S(1)}, u32[]{:S(2)}, u32[]{:S(2)}) async-start(f32[32,1,2304]{2,1,0:T(1,128)} %bitcast.24), calls=%async_computation | async-start | bytes 589824 | tf_op jit(solution)/shard_map/all_to_all | solution.py:446
  23.2 39.5 %copy-start.4 = (f32[288,544]{1,0:T(8,128)S(1)}, f32[288,544]{1,0:T(8,128)}, u32[]{:S(2)}) copy-start(f32[288,544]{1,0:T(8,128)} %get-tuple-element.14.parts_ref) | copy-start | bytes 1880068
  64.2 13.2 %all-to-all-start.3 = ((f32[32,1,2304]{2,1,0:T(1,128)}), f32[32,1,2304]{2,1,0:T(1,128)S(1)}, u32[]{:S(2)}, u32[]{:S(2)}) async-start(f32[32,1,2304]{2,1,0:T(1,128)} %bitcast.25), calls=%async_computation.3 | async-start | bytes 589824 | tf_op jit(solution)/shard_map/all_to_all | solution.py:446
  68.0 1.6 %copy-start.3 = (bf16[1024,1024]{1,0:T(8,128)(2,1)S(1)}, bf16[1024,1024]{1,0:T(8,128)(2,1)}, u32[]{:S(2)}) copy-start(bf16[1024,1024]{1,0:T(8,128)(2,1)} %get-tuple-element.18.tile_hbm) | copy-start | bytes 6291460

commit v8 on v6

--- a/solution.py
+++ b/solution.py
@@ -105,7 +105,10 @@
         right_copy.start()
         basis_copy.start()
         fetches.append((right_copy, basis_copy))
-    factors = pltpu.make_async_copy(coupling_hbm, coupling_ref, sems.at[2 * HALVES])
+    used = (slice(None), pl.ds(1, 9), pl.ds(0, RANK))
+    factors = pltpu.make_async_copy(
+        coupling_hbm.at[used], coupling_ref.at[used], sems.at[2 * HALVES]
+    )
     factors.start()
     projected = None
     for half, (right_copy, basis_copy) in enumerate(fetches):

time: 110 us -> 110 us (level)
  no operation moved by 1% of the time
where the time goes in v8:
time: 110 us; the launch traced here: 109 us
  blocking collectives  69.6 us (63%)
  starting transfers between devices  14.3 us (13%)
  Pallas kernels  12.4 us (11%)
  waiting for transfers between devices  9.74 us (9%)
  local copies, waits for them, and re-layouts  2.48 us (2%)
    all_to_all x4, blocking collectives, exchange(): got = lax.all_to_all(blocks, 'pts', 0, 0, axis_index_groups=groups)  69.6 us
    all_to_all x2, starting transfers between devices, exchange(): got = lax.all_to_all(blocks, 'pts', 0, 0, axis_index_groups=groups)  14.3 us
    pallas_call x9, Pallas kernels, call(): pl.pallas_call(body, out_shape=[(pltpu.HBM if place in far_outs else jax....  12.4 us
    all_to_all x2, waiting for transfers between devices, exchange(): got = lax.all_to_all(blocks, 'pts', 0, 0, axis_index_groups=groups)  9.74 us
    unnamed x18, local copies, waits for them, and re-layouts  2.48 us
  transfers between devices with their start and end apart: 2, of which 2 were waited for; matrix products, arithmetic and copies ran while one was open for 0% of the time, Pallas kernels for 6%

profile of v8, /device:TPU:1, one launch (start us, length us, event | category | flops | bytes accessed | tf_op | source)
XLA Modules:
  0.0 109.3 jit_solution(9336450267037076343)
XLA Ops:
  0.6 0.0 copy-start.1
  0.6 0.0 copy-start
  0.7 0.0 copy-start.2
  0.7 0.0 copy-start.6
  0.7 0.0 copy-start.8
  0.7 0.0 copy-start.7
  0.7 2.7 %start.1 = f32[576,128]{1,0:T(8,128)} custom-call(f32[128,1024]{1,0:T(8,128)} %right_ref.5, bf16[10,32,1024]{2,1,0:T(8,128)(2,1)} %basis_ref.7, f32[1,10,64,64]{3,2,1,0:T(8,128)} %coupling_ref.7), custom_call_target="tpu_custom_call" | custom-call | flops 67108864 | bytes 2097152 | tf_op jit(solution)/shard_map/start/pallas_call | solution.py:403
  3.4 10.4 %all-to-all-start = ((f32[32,1,2304]{2,1,0:T(1,128)}), f32[32,1,2304]{2,1,0:T(1,128)S(1)}, u32[]{:S(2)}, u32[]{:S(2)}) async-start(f32[32,1,2304]{2,1,0:T(1,128)} %bitcast.24), calls=%async_computation | async-start | bytes 589824 | tf_op jit(solution)/shard_map/all_to_all | solution.py:429
  13.8 0.0 copy-done.1
  13.9 0.0 copy-done
  13.9 0.0 copy-done.2
  13.9 0.0 copy-done.6
  13.9 0.0 copy-done.8
  13.9 0.0 copy-done.7
  13.9 4.4 %tile.1 = (bf16[1024,1024]{1,0:T(8,128)(2,1)}, f32[128,1024]{1,0:T(8,128)S(1)}, f32[288,544]{1,0:T(8,128)S(1)}, f32[2,128]{1,0:T(2,128)S(1)}) custom-call(f32[3,1024]{1,0:T(4,128)S(1)} %copy-done.7, s32[1,1024]{1,0:T(1,128)S(1)} %copy-done.8, s32[1,2]{1,0:T(1,128)S(1)} %copy-done.6, f32[128,1024]{1,0:T(8,128)S(1)} %copy-done.2, ...), custom_call_target="tpu_custom_call" | custom-call | flops 4294967296 | bytes 2097152 | tf_op jit(solution)/shard_map/tile/pallas_call | solution.py:403
  18.3 0.0 copy-start.4
  18.3 0.9 copy-done.4
  19.2 4.0 %all-to-all-done = f32[32,1,2304]{2,1,0:T(1,128)S(1)} async-done(((f32[32,1,2304]{2,1,0:T(1,128)}), f32[32,1,2304]{2,1,0:T(1,128)S(1)}, u32[]{:S(2)}, u32[]{:S(2)}) %all-to-all-start) | async-done | bytes 294944 | tf_op jit(solution)/shard_map/all_to_all | solution.py:429
  23.2 0.0 copy-start.5
  23.2 24.8 %all_to_all.30 = f32[16,1,1280]{2,1,0:T(1,128)S(1)} all-to-all(f32[16,1,1280]{2,1,0:T(1,128)S(1)} %bitcast.22), channel_id=1, replica_groups={{0,32,64,96,128,160,192,224,256,288,320,352,384,416,448,480},{1,33,65,9..., dimensions={0} | all-to-all | bytes 163840 | tf_op jit(solution)/shard_map/all_to_all | solution.py:429
  48.0 0.1 depth.2
  48.0 14.7 %all_to_all.31 = f32[32,1,2560]{2,1,0:T(1,128)S(1)} all-to-all(f32[32,1,2560]{2,1,0:T(1,128)S(1)} %bitcast.19), channel_id=1, replica_groups={{0,1,2,3,4,5,6,7,8,9,10,11,12,13,14,15,16,17,18,19,20,21,22,23,24,25,26..., dimensions={0} | all-to-all | bytes 655360 | tf_op jit(solution)/shard_map/all_to_all | solution.py:429
  62.7 0.0 copy-done.5
  62.7 1.5 %turn.1 = (f32[128,1024]{1,0:T(8,128)S(1)}, f32[128,1024]{1,0:T(8,128)S(1)}, f32[576,128]{1,0:T(8,128)}, f32[3,128]{1,0:T(4,128)S(1)}) custom-call(f32[640,128]{1,0:T(8,128)S(1)} %bitcast.18, f32[128,1024]{1,0:T(8,128)S(1)} %copy-done.2, f32[128,1024]{1,0:T(8,128)S(1)} %get-tuple-element.13.image_ref, f32[288,544]{1,0:T(8,128)S(1)} %copy-done.5, ...), custom_call_target="tpu_custom_call" | custom-call | flops 268435456 | bytes 2097152 | tf_op jit(solution)/shard_map/turn/pallas_call | solution.py:403
  64.2 3.8 %all-to-all-start.3 = ((f32[32,1,2304]{2,1,0:T(1,128)}), f32[32,1,2304]{2,1,0:T(1,128)S(1)}, u32[]{:S(2)}, u32[]{:S(2)}) async-start(f32[32,1,2304]{2,1,0:T(1,128)} %bitcast.25), calls=%async_computation.3 | async-start | bytes 589824 | tf_op jit(solution)/shard_map/all_to_all | solution.py:429
  68.0 0.0 copy-start.3
  68.1 1.6 %copy-done.3 = bf16[1024,1024]{1,0:T(8,128)(2,1)S(1)} copy-done((bf16[1024,1024]{1,0:T(8,128)(2,1)S(1)}, bf16[1024,1024]{1,0:T(8,128)(2,1)}, u32[]{:S(2)}) %copy-start.3) | copy-done | bytes 2097176
  69.6 2.0 %leaf.1 = (f32[128,1024]{1,0:T(8,128)S(1)}, f32[3,128]{1,0:T(4,128)S(1)}) custom-call(s32[1,2]{1,0:T(1,128)S(1)} %copy-done.6, f32[128,1024]{1,0:T(8,128)S(1)} %get-tuple-element.16.residual_ref, f32[128,1024]{1,0:T(8,128)S(1)} %get-tuple-element.17.first_image_ref, bf16[1024,1024]{1,0:T(8,128)(2,1)S(1)} %copy-done.3, bf16[10,32,1024]{2,1,0:T(8,128)(2,1)S(1)} %copy-done, ...), custom_call_target="tpu_custom_call" | custom-call | flops 1073741824 | bytes 2097152 | tf_op jit(solution)/shard_map/leaf/pallas_call | solution.py:403
  71.6 5.7 %all-to-all-done.3 = f32[32,1,2304]{2,1,0:T(1,128)S(1)} async-done(((f32[32,1,2304]{2,1,0:T(1,128)}), f32[32,1,2304]{2,1,0:T(1,128)S(1)}, u32[]{:S(2)}, u32[]{:S(2)}) %all-to-all-start.3) | async-done | bytes 294944 | tf_op jit(solution)/shard_map/all_to_all | solution.py:429
  77.4 15.0 %all_to_all.32 = f32[16,1,1408]{2,1,0:T(1,128)S(1)} all-to-all(f32[16,1,1408]{2,1,0:T(1,128)S(1)} %bitcast.21), channel_id=1, replica_groups={{0,32,64,96,128,160,192,224,256,288,320,352,384,416,448,480},{1,33,65,9..., dimensions={0} | all-to-all | bytes 180224 | tf_op jit(solution)/shard_map/all_to_all | solution.py:429
  92.4 0.1 depth.3
  92.5 15.2 %all_to_all.33 = f32[32,1,2688]{2,1,0:T(1,128)S(1)} all-to-all(f32[32,1,2688]{2,1,0:T(1,128)S(1)} %bitcast.17), channel_id=1, replica_groups={{0,1,2,3,4,5,6,7,8,9,10,11,12,13,14,15,16,17,18,19,20,21,22,23,24,25,26..., dimensions={0} | all-to-all | bytes 688128 | tf_op jit(solution)/shard_map/all_to_all | solution.py:429
  107.7 1.6 %end.1 = (f32[128,1024]{1,0:T(8,128)}, f32[128,1024]{1,0:T(8,128)}) custom-call(f32[672,128]{1,0:T(8,128)S(1)} %bitcast.16, f32[128,1024]{1,0:T(8,128)S(1)} %copy-done.2, f32[128,1024]{1,0:T(8,128)S(1)} %get-tuple-element.16.residual_ref, f32[128,1024]{1,0:T(8,128)S(1)} %get-tuple-element.17.first_image_ref, f32[128,1024]{1,0:T(8,128)S(1)} %get-tuple-element.20.image_ref, ...), custom_call_target="tpu_custom_call" | custom-call | flops 268435456 | bytes 2097152 | tf_op jit(solution)/shard_map/end/pallas_call | solution.py:403
  (2 shorter events, 0.1 us)
Async XLA Ops:
  0.6 13.2 %copy-start.1 = (f32[1,10,64,64]{3,2,1,0:T(8,128)S(1)}, f32[1,10,64,64]{3,2,1,0:T(8,128)}, u32[]{:S(2)}) copy-start(f32[1,10,64,64]{3,2,1,0:T(8,128)} %coupling_ref.7) | copy-start | bytes 491524
  0.6 13.2 %copy-start = (bf16[10,32,1024]{2,1,0:T(8,128)(2,1)S(1)}, bf16[10,32,1024]{2,1,0:T(8,128)(2,1)}, u32[]{:S(2)}) copy-start(bf16[10,32,1024]{2,1,0:T(8,128)(2,1)} %basis_ref.7) | copy-start | bytes 1966084
  0.7 13.2 %copy-start.2 = (f32[128,1024]{1,0:T(8,128)S(1)}, f32[128,1024]{1,0:T(8,128)}, u32[]{:S(2)}) copy-start(f32[128,1024]{1,0:T(8,128)} %right_ref.5) | copy-start | bytes 1572868
  0.7 13.2 %copy-start.6 = (s32[1,2]{1,0:T(1,128)S(1)}, s32[1,2]{1,0:T(1,128)}, u32[]{:S(2)}) copy-start(s32[1,2]{1,0:T(1,128)} %sizes_ref.3) | copy-start | bytes 28
  0.7 13.2 %copy-start.8 = (s32[1,1024]{1,0:T(1,128)S(1)}, s32[1,1024]{1,0:T(1,128)}, u32[]{:S(2)}) copy-start(s32[1,1024]{1,0:T(1,128)} %order_ref.1) | copy-start | bytes 12292
  0.7 13.2 %copy-start.7 = (f32[3,1024]{1,0:T(4,128)S(1)}, f32[3,1024]{1,0:T(4,128)}, u32[]{:S(2)}) copy-start(f32[3,1024]{1,0:T(4,128)} %coordinates_ref.1) | copy-start | bytes 36868
  3.4 19.8 %all-to-all-start = ((f32[32,1,2304]{2,1,0:T(1,128)}), f32[32,1,2304]{2,1,0:T(1,128)S(1)}, u32[]{:S(2)}, u32[]{:S(2)}) async-start(f32[32,1,2304]{2,1,0:T(1,128)} %bitcast.24), calls=%async_computation | async-start | bytes 589824 | tf_op jit(solution)/shard_map/all_to_all | solution.py:429
  18.3 0.9 copy-start.4
  23.2 39.5 %copy-start.5 = (f32[288,544]{1,0:T(8,128)S(1)}, f32[288,544]{1,0:T(8,128)}, u32[]{:S(2)}) copy-start(f32[288,544]{1,0:T(8,128)} %copy-done.4) | copy-start | bytes 1880068
  64.2 13.2 %all-to-all-start.3 = ((f32[32,1,2304]{2,1,0:T(1,128)}), f32[32,1,2304]{2,1,0:T(1,128)S(1)}, u32[]{:S(2)}, u32[]{:S(2)}) async-start(f32[32,1,2304]{2,1,0:T(1,128)} %bitcast.25), calls=%async_computation.3 | async-start | bytes 589824 | tf_op jit(solution)/shard_map/all_to_all | solution.py:429
  68.0 1.6 %copy-start.3 = (bf16[1024,1024]{1,0:T(8,128)(2,1)S(1)}, bf16[1024,1024]{1,0:T(8,128)(2,1)}, u32[]{:S(2)}) copy-start(bf16[1024,1024]{1,0:T(8,128)(2,1)} %get-tuple-element.18.tile_hbm) | copy-start | bytes 6291460
